TPU v7x, 256 devices: a whole 4x4x8 slice. The times are simulated.
256 devices in a mesh: chain: 16 (over y, x), heads: 16 (over z, core).
Axes of the slice: x: 4, y: 4, z: 8, core: 2. Of those that a mesh axis runs over, the one named last changes fastest.
Arguments:
- query_input: bfloat16 [8192, 4096], P('chain', 'heads'), may hold values from -8 to 8
- key_input: bfloat16 [8192, 4096], P('chain', 'heads'), may hold values from -8 to 8
- value_input: bfloat16 [8192, 4096], P('chain', 'heads'), may hold values from -6 to 6
- grad_output: bfloat16 [8192, 4096], P('chain', 'heads'), may hold values from -6 to 6
- selection: int32 [16, 32, 3], P(None, 'heads'), may hold values from 0 to 14, as said below
Outputs:
- grad_queries: bfloat16 [8192, 4096], P(('chain', 'heads'))
- grad_keys: bfloat16 [8192, 4096], P(('chain', 'heads'))
- grad_values: bfloat16 [8192, 4096], P(('chain', 'heads'))
Inputs may be any that keep to these rules, and one draw needn't show every extreme that they name: `selection`: for query block b and every head: slot 0 names block b - 1 (b itself when b is 0), the other slots name distinct blocks below b - 1; where no such block is left a slot names b itself and is empty.
All inputs are finite; a program needn't handle non-finite values.
Results may differ from a plain program's by a relative error of at most 0.035.
Values may be sent and summed in bfloat16 or wider, within the bound.
No kernel may reach another device: no remote copies, remote signals or barrier semaphores. Data moves between devices by JAX's collectives and lax.ppermute only.
A program may use at most 128 MiB of HBM per device.

v0:
```python
import jax
import jax.numpy as jnp
from jax import lax
from jax.sharding import PartitionSpec as P

HEAD_DIM = 128
TOPK = 3


MASKED = -1e30


def slot_backward(query_head, key_head, value_head, grad_head, allowed, scaling):
    scores = scaling * jnp.einsum(
        "qd,jkd->qjk", query_head, key_head, preferred_element_type=jnp.float32
    )
    scores = jnp.where(allowed, scores, MASKED)
    row_max = jnp.max(scores, axis=(1, 2), keepdims=True)
    raised = jnp.exp(scores - row_max)
    row_total = jnp.sum(raised, axis=(1, 2), keepdims=True)
    probability = raised / row_total
    probability_low = probability.astype(jnp.bfloat16)
    output = jnp.einsum(
        "qjk,jkd->qd", probability_low, value_head, preferred_element_type=jnp.float32
    )
    delta_row = jnp.sum(grad_head.astype(jnp.float32) * output, axis=1)
    grad_probs = jnp.einsum(
        "qd,jkd->qjk", grad_head, value_head, preferred_element_type=jnp.float32
    )
    grad_scores = (probability * (grad_probs - delta_row[:, None, None])).astype(jnp.bfloat16)
    grad_query = scaling * jnp.einsum(
        "qjk,jkd->qd", grad_scores, key_head, preferred_element_type=jnp.float32
    )
    log_total = row_max[:, 0, 0] + jnp.log(row_total[:, 0, 0])
    return (grad_query, grad_scores, probability_low, log_total, delta_row)


def on_device(query_input, key_input, value_input, grad_output, selection):
    query_rows, key_rows, value_rows, grad_rows = (query_input, key_input, value_input, grad_output)
    block_rows, row_width = query_rows.shape
    head_count = row_width // HEAD_DIM
    blocks = lax.axis_size("chain")
    chain_pos = lax.axis_index("chain")
    scaling = HEAD_DIM ** (-0.5)
    key_all, value_all = (
        lax.all_gather(key_rows, "chain", axis=0, tiled=True),
        lax.all_gather(value_rows, "chain", axis=0, tiled=True),
    )
    head_range = jnp.arange(head_count, dtype=jnp.int32)[:, None]
    key_four = key_all.reshape(blocks, block_rows, head_count, HEAD_DIM)
    value_four = value_all.reshape(blocks, block_rows, head_count, HEAD_DIM)
    chosen = lax.dynamic_index_in_dim(selection, chain_pos, 0, keepdims=False)
    slot_index = jnp.concatenate([chosen, jnp.full((head_count, 1), chain_pos, jnp.int32)], axis=1)
    key_slots = key_four[slot_index, :, head_range, :]
    value_slots = value_four[slot_index, :, head_range, :]
    position = jnp.arange(block_rows)
    causal = position[:, None] >= position[None, :]
    earlier = chosen < chain_pos
    query_three = query_rows.reshape(block_rows, head_count, HEAD_DIM)
    grad_three = grad_rows.reshape(block_rows, head_count, HEAD_DIM)
    query_list, key_terms, value_terms, log_list, delta_list = ([], [], [], [], [])
    for head_index in range(head_count):
        allowed = jnp.concatenate(
            [
                jnp.broadcast_to(
                    earlier[head_index][None, :, None], (block_rows, TOPK, block_rows)
                ),
                causal[:, None, :],
            ],
            axis=1,
        )
        grad_query, grad_scores, probability_low, log_total, delta_row = slot_backward(
            query_three[:, head_index],
            key_slots[head_index],
            value_slots[head_index],
            grad_three[:, head_index],
            allowed,
            scaling,
        )
        query_list.append(grad_query)
        log_list.append(log_total)
        delta_list.append(delta_row)
        key_terms.append(
            scaling
            * jnp.einsum(
                "qjk,qd->jkd",
                grad_scores,
                query_three[:, head_index],
                preferred_element_type=jnp.float32,
            )
        )
        value_terms.append(
            jnp.einsum(
                "qjk,qd->jkd",
                probability_low,
                grad_three[:, head_index],
                preferred_element_type=jnp.float32,
            )
        )
    grad_query_rows = (
        jnp.stack(query_list, axis=1).reshape(block_rows, row_width).astype(jnp.bfloat16)
    )
    key_slot_terms = jnp.stack(key_terms, axis=0)
    value_slot_terms = jnp.stack(value_terms, axis=0)
    row_count = block_rows * lax.axis_size("chain")
    count_blocks = row_count // block_rows
    target = jnp.arange(count_blocks, dtype=jnp.int32)
    member = (slot_index[:, None, :] == target[None, :, None]).astype(jnp.float32)
    key_part = jnp.einsum(
        "hbj,hjkd->bkhd", member, key_slot_terms, precision=lax.Precision.HIGHEST
    ).reshape(row_count, row_width)
    value_part = jnp.einsum(
        "hbj,hjkd->bkhd", member, value_slot_terms, precision=lax.Precision.HIGHEST
    ).reshape(row_count, row_width)
    summed_terms = lax.psum_scatter(
        jnp.concatenate([key_part, value_part], axis=1).astype(jnp.bfloat16),
        "chain",
        scatter_dimension=0,
        tiled=True,
    ).astype(jnp.float32)
    grad_key_rows = summed_terms[:, :row_width].astype(jnp.bfloat16)
    grad_value_rows = summed_terms[:, row_width:].astype(jnp.bfloat16)
    grad_queries, grad_keys, grad_values = (
        lax.all_to_all(grad_query_rows, "heads", split_axis=0, concat_axis=1, tiled=True),
        lax.all_to_all(grad_key_rows, "heads", split_axis=0, concat_axis=1, tiled=True),
        lax.all_to_all(grad_value_rows, "heads", split_axis=0, concat_axis=1, tiled=True),
    )
    return (grad_queries, grad_keys, grad_values)


def solution(mesh):
    in_specs = (
        P("chain", "heads"),
        P("chain", "heads"),
        P("chain", "heads"),
        P("chain", "heads"),
        P(None, "heads", None),
    )
    out_specs = (
        P(("chain", "heads"), None),
        P(("chain", "heads"), None),
        P(("chain", "heads"), None),
    )
    return jax.shard_map(
        on_device, mesh=mesh, in_specs=in_specs, out_specs=out_specs, check_vma=False
    )
```

profile of v0, /device:TPU:1, one launch (start us, length us, event | category | flops | bytes accessed | tf_op | source)
XLA Modules:
  0.0 346.6 jit_solution(12663629632764902300)
XLA Ops:
  7.2 0.0 copy-start
  7.2 0.0 all-gather.3.cloned.1.call-start
  7.2 0.7 all-gather.3.cloned.1.call-update
  7.9 0.0 all-gather.5.cloned.1.call-start
  8.0 0.7 all-gather.5.cloned.1.call-update
  8.7 0.0 reduce-scatter.2.cloned.1.call-start
  8.7 0.1 constant_dynamic-slice_fusion
  8.8 0.1 copy.41
  9.0 0.1 reshape.70
  9.1 1.1 copy.44
  10.2 1.1 copy.48
  11.3 0.1 copy.86
  11.4 0.1 copy.88
  11.5 0.1 iota_compare_fusion
  11.6 59.2 %all-gather.3.cloned.1.call-done = bf16[8192,256]{1,0:T(8,128)(2,1)} async-done(((bf16[512,256]{1,0:T(8,128)(2,1)}), bf16[8192,256]{1,0:T(8,128)(2,1)}) %all-gather.3.cloned.1.call-update) | async-done | bytes 4194320 | tf_op jit(solution)/shard_map/all_gather | solution.py:46
  70.8 6.9 %reshape.104 = bf16[16,512,2,128]{3,2,1,0:T(2,128)(2,1)} reshape(bf16[8192,256]{1,0:T(8,128)(2,1)} %all-gather.3.cloned.1.call-done) | data formatting | bytes 8388608 | tf_op jit(solution)/shard_map/reshape | solution.py:50
  77.8 5.1 %copy.43 = bf16[16,512,2,128]{3,1,2,0:T(8,128)(2,1)} copy(bf16[16,512,2,128]{3,2,1,0:T(2,128)(2,1)} %reshape.104) | data formatting | bytes 8388608 | tf_op jit(solution)/shard_map/reshape | solution.py:50
  82.9 46.7 %all-gather.5.cloned.1.call-done = bf16[8192,256]{1,0:T(8,128)(2,1)} async-done(((bf16[512,256]{1,0:T(8,128)(2,1)}), bf16[8192,256]{1,0:T(8,128)(2,1)}) %all-gather.5.cloned.1.call-update) | async-done | bytes 4194320 | tf_op jit(solution)/shard_map/all_gather | solution.py:47
  129.6 6.9 %reshape.105 = bf16[16,512,2,128]{3,2,1,0:T(2,128)(2,1)} reshape(bf16[8192,256]{1,0:T(8,128)(2,1)} %all-gather.5.cloned.1.call-done) | data formatting | bytes 8388608 | tf_op jit(solution)/shard_map/reshape | solution.py:51
  136.5 5.2 %copy.47 = bf16[16,512,2,128]{3,1,2,0:T(8,128)(2,1)} copy(bf16[16,512,2,128]{3,2,1,0:T(2,128)(2,1)} %reshape.105) | data formatting | bytes 8388608 | tf_op jit(solution)/shard_map/reshape | solution.py:51
  141.7 2.9 gather_fusion.1
  144.6 3.3 gather_fusion
  148.0 0.8 fusion.46
  148.7 0.6 fusion.3
  149.4 0.7 fusion.11
  150.0 0.7 convolution_bitcast_fusion.1
  150.7 0.8 fusion.18
  151.6 1.1 fusion.1
  152.7 0.7 fusion.9
  153.4 0.8 fusion.45
  154.1 0.6 fusion.5
  154.8 0.7 fusion.10
  155.4 0.7 convolution_bitcast_fusion
  156.2 0.8 fusion.19
  157.0 1.0 fusion
  158.1 1.3 copy-done.4
  159.4 0.7 fusion.8
  160.1 0.2 pad_maximum_fusion.2
  160.2 5.7 %convert_bitcast_fusion = bf16[16,512,2,128]{3,0,1,2:T(8,128)(2,1)} fusion(f32[2,4,512,128]{3,2,1,0:T(8,128)S(1)} %pad_maximum_fusion.2, s32[2,4]{1,0:T(2,128)S(1)} %concatenate.18), kind=kOutput, calls=%fused_computation.11 | convolution fusion | flops 102760576 | bytes 6291488 | tf_op jit(solution)/shard_map/hbj,hjkd->bkhd/dot_general | solution.py:112
  165.9 8.6 %copy.65 = bf16[16,512,2,128]{1,0,3,2:T(8,128)(2,1)} copy(bf16[16,512,2,128]{3,0,1,2:T(8,128)(2,1)} %convert_bitcast_fusion) | data formatting | bytes 8388608 | tf_op jit(solution)/shard_map/hbj,hjkd->bkhd/transpose | solution.py:112
  174.5 8.5 %copy.93 = bf16[32,8,16,512]{3,1,2,0:T(8,128)(2,1)} copy(bf16[32,8,16,512]{3,2,1,0:T(8,128)(2,1)} %bitcast.145) | data formatting | bytes 8388608
  183.0 0.1 pad_maximum_fusion.1
  183.1 5.5 %convert_bitcast_fusion.1 = bf16[16,512,2,128]{3,0,1,2:T(8,128)(2,1)} fusion(f32[2,4,512,128]{3,2,1,0:T(8,128)S(1)} %pad_maximum_fusion.1, s32[2,4]{1,0:T(2,128)S(1)} %concatenate.18), kind=kOutput, calls=%fused_computation.12 | convolution fusion | flops 102760576 | bytes 6291488 | tf_op jit(solution)/shard_map/hbj,hjkd->bkhd/dot_general | solution.py:109
  188.7 8.6 %copy.63 = bf16[16,512,2,128]{1,0,3,2:T(8,128)(2,1)} copy(bf16[16,512,2,128]{3,0,1,2:T(8,128)(2,1)} %convert_bitcast_fusion.1) | data formatting | bytes 8388608 | tf_op jit(solution)/shard_map/hbj,hjkd->bkhd/transpose | solution.py:109
  197.3 8.4 %copy.92 = bf16[32,8,16,512]{3,1,2,0:T(8,128)(2,1)} copy(bf16[32,8,16,512]{3,2,1,0:T(8,128)(2,1)} %bitcast.146) | data formatting | bytes 8388608
  205.7 7.7 %pad_maximum_fusion = bf16[8192,512]{0,1:T(8,128)(2,1)} fusion(bf16[8192,256]{0,1:T(8,128)(2,1)} %bitcast.147, bf16[8192,256]{0,1:T(8,128)(2,1)} %bitcast.148), kind=kLoop, calls=%fused_computation.2 | loop fusion | flops 16777216 | bytes 16777216 | tf_op jit(solution)/shard_map/concatenate | solution.py:116
  213.4 0.0 reduce-scatter.2.cloned.1.call-update
  213.4 1.6 copy-done.3
  215.0 0.8 fusion.21
  215.7 2.4 fusion.20
  218.1 0.3 copy.60
  218.4 0.9 convert_element_type.34
  219.3 7.7 %all-to-all-start = ((bf16[16,32,256]{2,1,0:T(8,128)(2,1)}), bf16[16,32,256]{2,1,0:T(8,128)(2,1)S(1)}, u32[]{:S(2)}, u32[]{:S(2)}) async-start(bf16[16,32,256]{2,1,0:T(8,128)(2,1)} %convert_element_type.34), calls=%async_computation | async-start | bytes 524288 | tf_op jit(solution)/shard_map/all_to_all | solution.py:124
  227.0 75.3 %reduce-scatter.2.cloned.1.call-done = bf16[512,512]{0,1:T(8,128)(2,1)} async-done(((bf16[8192,512]{0,1:T(8,128)(2,1)}), bf16[512,512]{0,1:T(8,128)(2,1)}) %reduce-scatter.2.cloned.1.call-update) | async-done | bytes 524304 | tf_op jit(solution)/shard_map/reduce_scatter | solution.py:115
  302.3 1.1 fusion.43
  303.4 0.8 copy.68
  304.2 8.9 %all-to-all-start.2 = ((bf16[16,32,256]{2,1,0:T(8,128)(2,1)}), bf16[16,32,256]{2,1,0:T(8,128)(2,1)S(1)}, u32[]{:S(2)}, u32[]{:S(2)}) async-start(bf16[16,32,256]{2,1,0:T(8,128)(2,1)} %bitcast.36), calls=%async_computation.3 | async-start | bytes 524288 | tf_op jit(solution)/shard_map/all_to_all | solution.py:126
  313.1 0.8 copy.66
  314.0 10.9 %all-to-all-done.2 = bf16[16,32,256]{2,1,0:T(8,128)(2,1)S(1)} async-done(((bf16[16,32,256]{2,1,0:T(8,128)(2,1)}), bf16[16,32,256]{2,1,0:T(8,128)(2,1)S(1)}, u32[]{:S(2)}, u32[]{:S(2)}) %all-to-all-start.2) | async-done | bytes 262176 | tf_op jit(solution)/shard_map/all_to_all | solution.py:126
  324.8 3.4 all-to-all-start.1
  328.3 0.7 copy.89
  329.0 0.7 copy.91
  329.7 9.7 %all-to-all-done.1 = bf16[16,32,256]{2,1,0:T(8,128)(2,1)S(1)} async-done(((bf16[16,32,256]{2,1,0:T(8,128)(2,1)}), bf16[16,32,256]{2,1,0:T(8,128)(2,1)S(1)}, u32[]{:S(2)}, u32[]{:S(2)}) %all-to-all-start.1) | async-done | bytes 262176 | tf_op jit(solution)/shard_map/all_to_all | solution.py:125
  339.4 0.7 copy.90
  (20 shorter events, 0.1 us)
Async XLA Ops:
  7.2 1.6 copy-start
  7.2 63.6 %all-gather.3.cloned.1.call-start = ((), (), s32[]{:S(2)}) async-start(), calls=%async_computation.4 | async-start | bytes 4456448 | tf_op jit(solution)/shard_map/all_gather | solution.py:46
  7.9 121.7 %all-gather.5.cloned.1.call-start = ((), (), s32[]{:S(2)}) async-start(), calls=%async_computation.5 | async-start | bytes 4456448 | tf_op jit(solution)/shard_map/all_gather | solution.py:47
  8.7 293.6 %reduce-scatter.2.cloned.1.call-start = ((), (), s32[]{:S(2)}) async-start(), calls=%async_computation.6 | async-start | bytes 8912896 | tf_op jit(solution)/shard_map/reduce_scatter | solution.py:115
  144.6 6.9 %copy-start.5 = (bf16[8,512,128]{2,1,0:T(8,128)(2,1)}, bf16[8,512,128]{2,1,0:T(8,128)(2,1)S(1)}, u32[]{:S(2)}) copy-start(bf16[8,512,128]{2,1,0:T(8,128)(2,1)S(1)} %gather_fusion.1) | copy-start | bytes 3145732
  152.6 1.5 copy-start.2
  154.8 1.4 copy-start.6
  158.0 1.3 copy-start.4
  213.4 1.6 copy-start.3
  215.0 125.1 %copy-start.1 = (s32[16,2,3]{0,1,2:T(2,128)S(1)}, s32[16,2,3]{0,1,2:T(2,128)}, u32[]{:S(2)}) copy-start(s32[16,2,3]{0,1,2:T(2,128)} %param.9) | copy-start | bytes 1156
  219.3 84.9 %all-to-all-start = ((bf16[16,32,256]{2,1,0:T(8,128)(2,1)}), bf16[16,32,256]{2,1,0:T(8,128)(2,1)S(1)}, u32[]{:S(2)}, u32[]{:S(2)}) async-start(bf16[16,32,256]{2,1,0:T(8,128)(2,1)} %convert_element_type.34), calls=%async_computation | async-start | bytes 524288 | tf_op jit(solution)/shard_map/all_to_all | solution.py:124
  304.2 20.6 %all-to-all-start.2 = ((bf16[16,32,256]{2,1,0:T(8,128)(2,1)}), bf16[16,32,256]{2,1,0:T(8,128)(2,1)S(1)}, u32[]{:S(2)}, u32[]{:S(2)}) async-start(bf16[16,32,256]{2,1,0:T(8,128)(2,1)} %bitcast.36), calls=%async_computation.3 | async-start | bytes 524288 | tf_op jit(solution)/shard_map/all_to_all | solution.py:126
  324.8 14.6 %all-to-all-start.1 = ((bf16[16,32,256]{2,1,0:T(8,128)(2,1)}), bf16[16,32,256]{2,1,0:T(8,128)(2,1)S(1)}, u32[]{:S(2)}, u32[]{:S(2)}) async-start(bf16[16,32,256]{2,1,0:T(8,128)(2,1)} %bitcast.34), calls=%async_computation.2 | async-start | bytes 524288 | tf_op jit(solution)/shard_map/all_to_all | solution.py:125
Sparse Core Ops, SparseCore 0:
  10.4 60.3 all-gather.2
  73.3 56.2 all-gather.4
  213.5 88.7 reduce-scatter.1
where the time goes:
time: 348 us; the launch traced here: 347 us
  waiting for transfers between devices  203 us (58%)
  local copies, waits for them, and re-layouts  76.2 us (22%)
  matrix products  22.4 us (6%)
  starting transfers between devices  20.1 us (6%)
  between operations  14 us (4%)
  other arithmetic  10.7 us (3%)
    reduce_scatter x1, waiting for transfers between devices, on_device(): lax.psum_scatter(jnp.concatenate([key_part, value_part], axis=1).astype(j...  75.3 us
    all_gather x1, waiting for transfers between devices, on_device(): lax.all_gather(key_rows, 'chain', axis=0, tiled=True)  59.2 us
    all_gather x1, waiting for transfers between devices, on_device(): lax.all_gather(value_rows, 'chain', axis=0, tiled=True)  46.7 us
    unnamed x20, local copies, waits for them, and re-layouts  22.2 us
    reshape x2, local copies, waits for them, and re-layouts, on_device(): value_four = value_all.reshape(blocks, block_rows, head_count, HEAD_DIM)  12.1 us
    reshape x2, local copies, waits for them, and re-layouts, on_device(): key_four = key_all.reshape(blocks, block_rows, head_count, HEAD_DIM)  12.1 us
    all_to_all x1, waiting for transfers between devices, on_device(): lax.all_to_all(grad_value_rows, 'heads', split_axis=0, concat_axis=1, til...  10.9 us
    all_to_all x1, waiting for transfers between devices, on_device(): lax.all_to_all(grad_key_rows, 'heads', split_axis=0, concat_axis=1, tiled...  9.68 us
  transfers between devices with their start and end apart: 6, of which 5 were waited for; matrix products, arithmetic and copies ran while one was open for 7% of the time, Pallas kernels for 0%

commit v1 on v0

v1 whole, which is shorter than its diff:
```python
import math

import jax
import jax.numpy as jnp
from jax import lax
from jax.experimental import pallas as pl
from jax.experimental.pallas import tpu as pltpu
from jax.sharding import PartitionSpec as P

HEAD_DIM = 128
TOPK = 3
MASKED = -1e30
SCALING = HEAD_DIM ** (-0.5)
TILE = 256
MIB = 1 << 20


def columns(head):
    return slice(head * HEAD_DIM, (head + 1) * HEAD_DIM)


def pick_kernel(selection_ref, held_ref, out_ref):
    blocks, _, _, width = held_ref.shape
    heads = width // HEAD_DIM

    def fill(block, carry):
        for head in range(heads):
            for slot in range(TOPK):
                source = selection_ref[(block * heads + head) * TOPK + slot]
                out_ref[block, :, slot, :, columns(head)] = held_ref[source, :, :, columns(head)]
        return carry

    lax.fori_loop(0, blocks, fill, 0)


def reduce_kernel(selection_ref, terms_ref, out_ref, total_ref):
    blocks, _, _, width = out_ref.shape
    heads = width // HEAD_DIM
    total_ref[...] = jnp.zeros_like(total_ref)

    def add(block, carry):
        for head in range(heads):
            for slot in range(TOPK):
                target = selection_ref[(block * heads + head) * TOPK + slot]
                total_ref[target, :, :, columns(head)] += terms_ref[
                    block, :, slot, :, columns(head)
                ].astype(jnp.float32)
        return carry

    lax.fori_loop(0, blocks, add, 0)
    out_ref[...] = total_ref[...].astype(out_ref.dtype)


def dot(left, right, left_dim, right_dim):
    return lax.dot_general(
        left, right, (((left_dim,), (right_dim,)), ((), ())), preferred_element_type=jnp.float32
    )


def attend_kernel(
    selection_ref,
    position_ref,
    query_ref,
    key_ref,
    value_ref,
    grad_ref,
    listed_ref,
    grad_query_ref,
    terms_ref,
    own_ref,
    prob_ref,
    grad_prob_ref,
    prob_low_ref,
    grad_score_ref,
):
    head, heads = pl.program_id(0), pl.num_programs(0)
    block = position_ref[0]
    rows = query_ref.shape[0]
    chunks, _, _, chunk, _ = listed_ref.shape
    live = [
        selection_ref[(block * heads + head) * TOPK + slot] < block for slot in range(TOPK)
    ]

    def slot_rows(which, slot):
        if slot == TOPK:
            return (key_ref, value_ref)[which][...]
        return listed_ref[:, which, slot].reshape(rows, HEAD_DIM)

    def query_tile(index, carry):
        first = pl.multiple_of(index * TILE, TILE)
        tile = pl.ds(first, TILE)
        query, grad = query_ref[tile, :], grad_ref[tile, :]
        top = None
        for slot in range(TOPK + 1):
            scores = dot(slot_rows(0, slot), query, 1, 1)
            if slot == TOPK:
                key_at = lax.broadcasted_iota(jnp.int32, scores.shape, 0)
                query_at = lax.broadcasted_iota(jnp.int32, scores.shape, 1) + first
                scores = jnp.where(key_at <= query_at, scores, MASKED)
            prob_ref[slot] = scores
            highest = jnp.max(scores, axis=0, keepdims=True)
            if slot < TOPK:
                highest = jnp.where(live[slot], highest, MASKED)
            top = highest if top is None else jnp.maximum(top, highest)
        total = jnp.zeros_like(top)
        for slot in range(TOPK + 1):
            shift = jnp.where(live[slot], top, -MASKED) if slot < TOPK else top
            raised = jnp.exp2((prob_ref[slot] - shift) * (SCALING * math.log2(math.e)))
            prob_ref[slot] = raised
            total += jnp.sum(raised, axis=0, keepdims=True)
        inverse = 1.0 / total
        delta = jnp.zeros_like(top)
        for slot in range(TOPK + 1):
            probability = prob_ref[slot] * inverse
            prob_ref[slot] = probability
            low = probability.astype(jnp.bfloat16)
            prob_low_ref[slot, :, tile] = low
            grad_probs = dot(slot_rows(1, slot), grad, 1, 1)
            grad_prob_ref[slot] = grad_probs
            delta += jnp.sum(low.astype(jnp.float32) * grad_probs, axis=0, keepdims=True)
        for slot in range(TOPK + 1):
            grad_score_ref[slot, :, tile] = (
                prob_ref[slot] * (grad_prob_ref[slot] - delta)
            ).astype(jnp.bfloat16)
        return carry

    lax.fori_loop(0, rows // TILE, query_tile, 0)
    query, grad = query_ref[...], grad_ref[...]
    grad_query = None
    for slot in range(TOPK + 1):
        grad_scores = grad_score_ref[slot]
        grad_value = dot(prob_low_ref[slot], grad, 1, 0).reshape(chunks, chunk, HEAD_DIM)
        grad_key = (dot(grad_scores, query, 1, 0) * SCALING).reshape(chunks, chunk, HEAD_DIM)
        if slot < TOPK:
            terms_ref[:, 0, slot] = grad_key.astype(jnp.bfloat16)
            terms_ref[:, 1, slot] = grad_value.astype(jnp.bfloat16)
        else:
            own_ref[:, 0] = grad_key
            own_ref[:, 1] = grad_value
        part = dot(slot_rows(0, slot).T, grad_scores, 1, 0)
        grad_query = part if grad_query is None else grad_query + part
    grad_query_ref[...] = (grad_query * SCALING).T.astype(jnp.bfloat16)


def on_device(query_input, key_input, value_input, grad_output, selection):
    rows, width = query_input.shape
    heads = width // HEAD_DIM
    chain, spread = lax.axis_size("chain"), lax.axis_size("heads")
    chunk = rows // chain
    listed = selection.reshape(-1)
    position = lax.axis_index("chain").astype(jnp.int32).reshape(1)
    smem = pl.BlockSpec(memory_space=pltpu.SMEM)
    vmem = pl.BlockSpec(memory_space=pltpu.VMEM)

    def swap(array, axis):
        return lax.all_to_all(array, axis, split_axis=0, concat_axis=0, tiled=True)

    pair = jnp.stack(
        [part.reshape(chain, chunk, width) for part in (key_input, value_input)], axis=1
    )
    held = swap(pair, "chain")
    picked = pl.pallas_call(
        pick_kernel,
        out_shape=jax.ShapeDtypeStruct((chain, 2, TOPK, chunk, width), jnp.bfloat16),
        in_specs=[smem, vmem],
        out_specs=vmem,
        compiler_params=pltpu.CompilerParams(vmem_limit_bytes=8 * MIB),
        name="pick",
    )(listed, held)
    slots = swap(picked, "chain")

    def head_block(*lead):
        block = lead + (HEAD_DIM,)
        return pl.BlockSpec(block, lambda head, *_: (0,) * len(lead) + (head,))

    grad_query, terms, own = pl.pallas_call(
        attend_kernel,
        out_shape=(
            jax.ShapeDtypeStruct((rows, width), jnp.bfloat16),
            jax.ShapeDtypeStruct((chain, 2, TOPK, chunk, width), jnp.bfloat16),
            jax.ShapeDtypeStruct((chain, 2, chunk, width), jnp.float32),
        ),
        grid_spec=pltpu.PrefetchScalarGridSpec(
            num_scalar_prefetch=2,
            grid=(heads,),
            in_specs=[head_block(rows)] * 4 + [head_block(chain, 2, TOPK, chunk)],
            out_specs=(
                head_block(rows),
                head_block(chain, 2, TOPK, chunk),
                head_block(chain, 2, chunk),
            ),
            scratch_shapes=[
                pltpu.VMEM((TOPK + 1, rows, TILE), jnp.float32),
                pltpu.VMEM((TOPK + 1, rows, TILE), jnp.float32),
                pltpu.VMEM((TOPK + 1, rows, rows), jnp.bfloat16),
                pltpu.VMEM((TOPK + 1, rows, rows), jnp.bfloat16),
            ],
        ),
        compiler_params=pltpu.CompilerParams(vmem_limit_bytes=32 * MIB),
        name="attend",
    )(listed, position, query_input, key_input, value_input, grad_output, slots)

    returned = swap(terms, "chain")
    summed = pl.pallas_call(
        reduce_kernel,
        out_shape=jax.ShapeDtypeStruct((chain, 2, chunk, width), jnp.bfloat16),
        in_specs=[smem, vmem],
        out_specs=vmem,
        scratch_shapes=[pltpu.VMEM((chain, 2, chunk, width), jnp.float32)],
        compiler_params=pltpu.CompilerParams(vmem_limit_bytes=8 * MIB),
        name="reduce",
    )(listed, returned)
    others = swap(summed, "chain")
    whole = (others.astype(jnp.float32) + own).astype(jnp.bfloat16)

    share = rows // spread
    whole = whole.reshape(spread, chain // spread, 2, chunk, width).swapaxes(1, 2)
    whole = swap(whole.reshape(spread, 2, share, width), "heads")
    grad_query = swap(grad_query.reshape(spread, share, width), "heads")

    def lay(array):
        return array.swapaxes(0, 1).reshape(share, spread * width)

    return (lay(grad_query), lay(whole[:, 0]), lay(whole[:, 1]))


def solution(mesh):
    in_specs = (
        P("chain", "heads"),
        P("chain", "heads"),
        P("chain", "heads"),
        P("chain", "heads"),
        P(None, "heads", None),
    )
    out_specs = (
        P(("chain", "heads"), None),
        P(("chain", "heads"), None),
        P(("chain", "heads"), None),
    )
    return jax.shard_map(
        on_device, mesh=mesh, in_specs=in_specs, out_specs=out_specs, check_vma=False
    )
```

time: 348 us -> 145 us (0.42)
  waiting for transfers between devices: 203 us -> 57.6 us
  local copies, waits for them, and re-layouts: 76.2 us -> 3.37 us
  blocking collectives: 0 us -> 39.7 us
  matrix products: 22.4 us -> 0 us
  Pallas kernels: 0 us -> 14.1 us
  between operations: 14 us -> 0.73 us
  other arithmetic: 10.7 us -> 2.85 us
  starting transfers between devices: 20.1 us -> 26.2 us
    all_gather x2 -> x0, waiting for transfers between devices: 106 us -> none  [the longest x1 59.2 us: on_device(): lax.all_gather(key_rows, 'chain', axis=0, tiled=True)]
    reduce_scatter x1 -> x0, waiting for transfers between devices: 75.3 us -> none  [on_device(): lax.psum_scatter(jnp.concatenate([key_part, value_part], axis=1).astype(j...]
    all_to_all x0 -> x2, blocking collectives: none -> 39.7 us  [swap(): return lax.all_to_all(array, axis, split_axis=0, concat_axis=0, tiled=True)]
    all_to_all x3 -> x4, waiting for transfers between devices: 20.6 us -> 57.6 us  [swap(): return lax.all_to_all(array, axis, split_axis=0, concat_axis=0, tiled=True)]
    dot_general x14 -> x0, matrix products: 22.4 us -> none  [the longest x1 5.7 us: on_device(): jnp.einsum('hbj,hjkd->bkhd', member, value_slot_terms, precision=lax.Prec...]
    reshape x4, local copies, waits for them, and re-layouts: 24.2 us -> 2.27 us  [the longest x3 2.16 us: lay(): return array.swapaxes(0, 1).reshape(share, spread * width)]
    unnamed x20 -> x14, local copies, waits for them, and re-layouts: 22.2 us -> 1.1 us
    transpose x2 -> x0, local copies, waits for them, and re-layouts: 17.2 us -> none  [the longest x1 8.6 us: on_device(): jnp.einsum('hbj,hjkd->bkhd', member, key_slot_terms, precision=lax.Precis...]
  transfers between devices with their start and end apart: 6 -> 4, of which waited for: 5 -> 4; matrix products, arithmetic and copies ran while one was open for 7% -> 1% of each run, Pallas kernels for 0% -> 0%
where the time goes in v1:
time: 145 us
  waiting for transfers between devices  57.6 us (40%)
  blocking collectives  39.7 us (27%)
  starting transfers between devices  26.2 us (18%)
  Pallas kernels  14.1 us (10%)
  local copies, waits for them, and re-layouts  3.37 us (2%)
  other arithmetic  2.85 us (2%)
    all_to_all x4, waiting for transfers between devices, swap(): return lax.all_to_all(array, axis, split_axis=0, concat_axis=0, tiled=True)  57.6 us
    all_to_all x2, blocking collectives, swap(): return lax.all_to_all(array, axis, split_axis=0, concat_axis=0, tiled=True)  39.7 us
    all_to_all x4, starting transfers between devices, swap(): return lax.all_to_all(array, axis, split_axis=0, concat_axis=0, tiled=True)  26.2 us
    pallas_call x1, Pallas kernels, on_device(): pl.pallas_call(attend_kernel, out_shape=(jax.ShapeDtypeStruct((rows, widt...  10.8 us
  transfers between devices with their start and end apart: 4, of which 4 were waited for; matrix products, arithmetic and copies ran while one was open for 1% of the time, Pallas kernels for 0%

profile of v1, /device:TPU:1, one launch (start us, length us, event | category | flops | bytes accessed | tf_op | source)
XLA Modules:
  0.0 144.6 jit_solution(7513262109134853121)
XLA Ops:
  0.6 0.0 copy-start.5
  0.6 1.9 %pad_maximum_fusion = bf16[16,2,32,256]{3,2,1,0:T(8,128)(2,1)} fusion(bf16[16,1,32,256]{3,2,1,0:T(8,128)(2,1)} %bitcast.20, bf16[16,1,32,256]{3,2,1,0:T(8,128)(2,1)} %bitcast.19), kind=kLoop, calls=%fused_computation.1 | loop fusion | flops 262144 | bytes 1048576 | tf_op jit(solution)/shard_map/stack | solution.py:158
  2.5 7.6 %all-to-all-start = ((bf16[16,2,32,256]{3,2,1,0:T(8,128)(2,1)}), bf16[16,2,32,256]{3,2,1,0:T(8,128)(2,1)S(1)}, u32[]{:S(2)}, u32[]{:S(2)}) async-start(bf16[16,2,32,256]{3,2,1,0:T(8,128)(2,1)} %pad_maximum_fusion), calls=%async_computation | async-start | bytes 1048576 | tf_op jit(solution)/shard_map/all_to_all | solution.py:156
  10.1 0.0 copy-done.5
  10.1 0.1 copy.10
  10.2 0.1 reshape.24.selection_ref
  10.3 10.3 %all-to-all-done.held_ref = bf16[16,2,32,256]{3,2,1,0:T(8,128)(2,1)S(1)} async-done(((bf16[16,2,32,256]{3,2,1,0:T(8,128)(2,1)}), bf16[16,2,32,256]{3,2,1,0:T(8,128)(2,1)S(1)}, u32[]{:S(2)}, u32[]{:S(2)}) %all-to-all-start) | async-done | bytes 524320 | tf_op jit(solution)/shard_map/all_to_all | solution.py:156
  20.6 2.1 %pick.1 = bf16[16,2,3,32,256]{4,3,2,1,0:T(8,128)(2,1)} custom-call(s32[96]{0:T(128)S(1)} %reshape.24.selection_ref, bf16[16,2,32,256]{3,2,1,0:T(8,128)(2,1)S(1)} %all-to-all-done.held_ref), custom_call_target="tpu_custom_call" | custom-call | tf_op jit(solution)/shard_map/pick/pallas_call | solution.py:162
  22.7 0.0 copy-start
  22.7 0.0 copy-start.1
  22.7 0.0 copy-start.2
  22.7 3.8 %all-to-all-start.1 = ((bf16[16,2,3,32,256]{4,3,2,1,0:T(8,128)(2,1)}), bf16[16,2,3,32,256]{4,3,2,1,0:T(8,128)(2,1)S(1)}, u32[]{:S(2)}, u32[]{:S(2)}) async-start(bf16[16,2,3,32,256]{4,3,2,1,0:T(8,128)(2,1)} %pick.1), calls=%async_computation.1 | async-start | bytes 3145728 | tf_op jit(solution)/shard_map/all_to_all | solution.py:156
  26.6 20.5 %all-to-all-done.1.listed_ref = bf16[16,2,3,32,256]{4,3,2,1,0:T(8,128)(2,1)S(1)} async-done(((bf16[16,2,3,32,256]{4,3,2,1,0:T(8,128)(2,1)}), bf16[16,2,3,32,256]{4,3,2,1,0:T(8,128)(2,1)S(1)}, u32[]{:S(2)}, u32[]{:S(2)}) %all-to-all-start.1) | async-done | bytes 1572896 | tf_op jit(solution)/shard_map/all_to_all | solution.py:156
  47.1 0.0 copy-done
  47.1 0.0 copy-done.1
  47.1 0.0 copy-done.2
  47.1 0.0 copy-start.3
  47.1 0.9 copy-done.3
  48.1 10.8 %attend.1 = (bf16[512,256]{1,0:T(8,128)(2,1)S(1)}, bf16[16,2,3,32,256]{4,3,2,1,0:T(8,128)(2,1)S(1)}, f32[16,2,32,256]{3,2,1,0:T(8,128)S(1)}) custom-call(s32[96]{0:T(128)S(1)} %reshape.24.selection_ref, s32[1]{0:T(128)} %bitcast.position_ref, bf16[512,256]{1,0:T(8,128)(2,1)S(1)} %copy-done.2, bf16[512,256]{1,0:T(8,128)(2,1)S(1)} %copy-done, ...), custom_call_target="tpu_custom_call" | custom-call | tf_op jit(solution)/shard_map/attend/pallas_call | solution.py:176
  58.9 0.0 copy-start.4
  58.9 27.1 %all_to_all.30.terms_ref = bf16[16,2,3,32,256]{4,3,2,1,0:T(8,128)(2,1)S(1)} all-to-all(bf16[16,2,3,32,256]{4,3,2,1,0:T(8,128)(2,1)S(1)} %get-tuple-element.7), channel_id=1, replica_groups=mesh['chain'=16,'heads'=16] {'chain'}, dimensions={0} | all-to-all | bytes 3145728 | tf_op jit(solution)/shard_map/all_to_all | solution.py:156
  86.0 0.0 copy-done.4
  86.0 1.1 reduce.1
  87.1 12.7 %all_to_all.31 = bf16[16,2,32,256]{3,2,1,0:T(8,128)(2,1)S(1)} all-to-all(bf16[16,2,32,256]{3,2,1,0:T(8,128)(2,1)S(1)} %reduce.1), channel_id=1, replica_groups=mesh['chain'=16,'heads'=16] {'chain'}, dimensions={0} | all-to-all | bytes 1048576 | tf_op jit(solution)/shard_map/all_to_all | solution.py:156
  99.8 11.3 %all-to-all-start.2 = ((bf16[16,32,256]{2,1,0:T(8,128)(2,1)}), bf16[16,32,256]{2,1,0:T(8,128)(2,1)S(1)}, u32[]{:S(2)}, u32[]{:S(2)}) async-start(bf16[16,32,256]{2,1,0:T(8,128)(2,1)} %bitcast.21), calls=%async_computation.2 | async-start | bytes 524288 | tf_op jit(solution)/shard_map/all_to_all | solution.py:156
  111.1 1.0 add_convert_fusion
  112.1 10.7 %all-to-all-done.2 = bf16[16,32,256]{2,1,0:T(8,128)(2,1)S(1)} async-done(((bf16[16,32,256]{2,1,0:T(8,128)(2,1)}), bf16[16,32,256]{2,1,0:T(8,128)(2,1)S(1)}, u32[]{:S(2)}, u32[]{:S(2)}) %all-to-all-start.2) | async-done | bytes 262176 | tf_op jit(solution)/shard_map/all_to_all | solution.py:156
  122.8 3.5 %all-to-all-start.5 = ((bf16[16,2,32,256]{3,2,1,0:T(8,128)(2,1)}), bf16[16,2,32,256]{3,2,1,0:T(8,128)(2,1)S(1)}, u32[]{:S(2)}, u32[]{:S(2)}) async-start(bf16[16,2,32,256]{3,2,1,0:T(8,128)(2,1)} %add_convert_fusion), calls=%async_computation.5 | async-start | bytes 1048576 | tf_op jit(solution)/shard_map/all_to_all | solution.py:156
  126.3 0.7 copy.14
  127.0 16.0 %all-to-all-done.5 = bf16[16,2,32,256]{3,2,1,0:T(8,128)(2,1)S(1)} async-done(((bf16[16,2,32,256]{3,2,1,0:T(8,128)(2,1)}), bf16[16,2,32,256]{3,2,1,0:T(8,128)(2,1)S(1)}, u32[]{:S(2)}, u32[]{:S(2)}) %all-to-all-start.5) | async-done | bytes 524320 | tf_op jit(solution)/shard_map/all_to_all | solution.py:156
  143.1 0.7 copy.16
  143.8 0.7 copy.15
  (1 shorter events, 0.0 us)
Async XLA Ops:
  0.6 9.5 %copy-start.5 = (s32[16,2,3]{0,1,2:T(2,128)S(1)}, s32[16,2,3]{0,1,2:T(2,128)}, u32[]{:S(2)}) copy-start(s32[16,2,3]{0,1,2:T(2,128)} %param.9) | copy-start | bytes 1156
  2.5 18.1 %all-to-all-start = ((bf16[16,2,32,256]{3,2,1,0:T(8,128)(2,1)}), bf16[16,2,32,256]{3,2,1,0:T(8,128)(2,1)S(1)}, u32[]{:S(2)}, u32[]{:S(2)}) async-start(bf16[16,2,32,256]{3,2,1,0:T(8,128)(2,1)} %pad_maximum_fusion), calls=%async_computation | async-start | bytes 1048576 | tf_op jit(solution)/shard_map/all_to_all | solution.py:156
  22.7 24.4 %copy-start = (bf16[512,256]{1,0:T(8,128)(2,1)S(1)}, bf16[512,256]{1,0:T(8,128)(2,1)}, u32[]{:S(2)}) copy-start(bf16[512,256]{1,0:T(8,128)(2,1)} %key_ref.1) | copy-start | bytes 786436
  22.7 24.4 %copy-start.1 = (bf16[512,256]{1,0:T(8,128)(2,1)S(1)}, bf16[512,256]{1,0:T(8,128)(2,1)}, u32[]{:S(2)}) copy-start(bf16[512,256]{1,0:T(8,128)(2,1)} %value_ref.1) | copy-start | bytes 786436
  22.7 24.4 %copy-start.2 = (bf16[512,256]{1,0:T(8,128)(2,1)S(1)}, bf16[512,256]{1,0:T(8,128)(2,1)}, u32[]{:S(2)}) copy-start(bf16[512,256]{1,0:T(8,128)(2,1)} %query_ref.1) | copy-start | bytes 786436
  22.7 24.4 %all-to-all-start.1 = ((bf16[16,2,3,32,256]{4,3,2,1,0:T(8,128)(2,1)}), bf16[16,2,3,32,256]{4,3,2,1,0:T(8,128)(2,1)S(1)}, u32[]{:S(2)}, u32[]{:S(2)}) async-start(bf16[16,2,3,32,256]{4,3,2,1,0:T(8,128)(2,1)} %pick.1), calls=%async_computation.1 | async-start | bytes 3145728 | tf_op jit(solution)/shard_map/all_to_all | solution.py:156
  47.1 1.0 copy-start.3
  58.9 27.1 %copy-start.4 = (bf16[512,256]{1,0:T(8,128)(2,1)}, bf16[512,256]{1,0:T(8,128)(2,1)S(1)}, u32[]{:S(2)}) copy-start(bf16[512,256]{1,0:T(8,128)(2,1)S(1)} %get-tuple-element.6) | copy-start | bytes 786436
  99.8 23.1 %all-to-all-start.2 = ((bf16[16,32,256]{2,1,0:T(8,128)(2,1)}), bf16[16,32,256]{2,1,0:T(8,128)(2,1)S(1)}, u32[]{:S(2)}, u32[]{:S(2)}) async-start(bf16[16,32,256]{2,1,0:T(8,128)(2,1)} %bitcast.21), calls=%async_computation.2 | async-start | bytes 524288 | tf_op jit(solution)/shard_map/all_to_all | solution.py:156
  122.8 20.2 %all-to-all-start.5 = ((bf16[16,2,32,256]{3,2,1,0:T(8,128)(2,1)}), bf16[16,2,32,256]{3,2,1,0:T(8,128)(2,1)S(1)}, u32[]{:S(2)}, u32[]{:S(2)}) async-start(bf16[16,2,32,256]{3,2,1,0:T(8,128)(2,1)} %add_convert_fusion), calls=%async_computation.5 | async-start | bytes 1048576 | tf_op jit(solution)/shard_map/all_to_all | solution.py:156

commit v2 on v1

v2 whole, which is shorter than its diff:
```python
import math

import jax
import jax.numpy as jnp
from jax import lax
from jax.experimental import pallas as pl
from jax.experimental.pallas import tpu as pltpu
from jax.sharding import PartitionSpec as P

HEAD_DIM = 128
TOPK = 3
MASKED = -1e30
SCALING = HEAD_DIM ** (-0.5)
EXPONENT = SCALING * math.log2(math.e)
TILE = 256
STATS = 8
MIB = 1 << 20


def head_columns(head, offset=0):
    start = head * HEAD_DIM + offset
    if isinstance(head, int):
        return pl.ds(start, HEAD_DIM)
    return pl.ds(pl.multiple_of(start, HEAD_DIM), HEAD_DIM)


def dot(left, right, left_dim, right_dim):
    return lax.dot_general(
        left, right, (((left_dim,), (right_dim,)), ((), ())), preferred_element_type=jnp.float32
    )


def stack_kernel(key_ref, value_ref, out_ref, held_ref, in_sem, out_sem):
    pieces = in_sem.shape[1]
    length = key_ref.shape[0] // pieces
    arrive, leave = [], []
    for index, part in enumerate((key_ref, value_ref)):
        for piece in range(pieces):
            span = pl.ds(piece * length, length)
            held = held_ref.at[index, span]
            arrive.append(pltpu.make_async_copy(part.at[span], held, in_sem.at[index, piece]))
            leave.append(
                pltpu.make_async_copy(held, out_ref.at[span, index], out_sem.at[index, piece])
            )
    for copy in arrive:
        copy.start()
    for first, second in zip(arrive, leave):
        first.wait()
        second.start()
    for copy in leave:
        copy.wait()


def pick_kernel(selection_ref, held_ref, out_ref, filled_ref, sem):
    blocks, _, _, width = held_ref.shape
    heads = width // HEAD_DIM
    copies = []
    for block in range(blocks):
        for head in range(heads):
            for slot in range(TOPK):
                source = selection_ref[(block * heads + head) * TOPK + slot]
                filled_ref[block, :, slot, :, head_columns(head)] = held_ref[
                    source, :, :, head_columns(head)
                ]
        copies.append(
            pltpu.make_async_copy(filled_ref.at[block], out_ref.at[block], sem.at[block])
        )
        copies[-1].start()
    for copy in copies:
        copy.wait()


def reduce_kernel(selection_ref, terms_ref, out_ref, total_ref, low_ref, sem):
    blocks, _, _, width = out_ref.shape
    heads = width // HEAD_DIM
    total_ref[...] = jnp.zeros_like(total_ref)

    def add(block, carry):
        for head in range(heads):
            for slot in range(TOPK):
                target = selection_ref[(block * heads + head) * TOPK + slot]
                total_ref[target, :, :, head_columns(head)] += terms_ref[
                    block, :, slot, :, head_columns(head)
                ].astype(jnp.float32)
        return carry

    lax.fori_loop(0, blocks, add, 0)
    pieces = sem.shape[0]
    copies = []
    for piece in range(pieces):
        span = pl.ds(piece * (blocks // pieces), blocks // pieces)
        low_ref[span] = total_ref[span].astype(low_ref.dtype)
        copies.append(pltpu.make_async_copy(low_ref.at[span], out_ref.at[span], sem.at[piece]))
        copies[-1].start()
    for copy in copies:
        copy.wait()


def causal(scores, first):
    key_at = lax.broadcasted_iota(jnp.int32, scores.shape, 0)
    query_at = lax.broadcasted_iota(jnp.int32, scores.shape, 1) + first
    return jnp.where(key_at <= query_at, scores, MASKED)


def own_forward_kernel(query_ref, key_ref, value_ref, grad_ref, rows_ref, stats_ref):
    heads, _, rows = stats_ref.shape
    width = heads * HEAD_DIM
    rows_ref[:, :width] = query_ref[...]
    rows_ref[:, width:] = grad_ref[...]

    def one_head(head, carry):
        columns = head_columns(head)
        key, value = key_ref[:, columns], value_ref[:, columns]
        for first in range(0, rows, TILE):
            tile = pl.ds(first, TILE)
            scores = causal(dot(key, query_ref[tile, columns], 1, 1), first)
            top = jnp.max(scores, axis=0, keepdims=True)
            raised = jnp.exp2((scores - top) * EXPONENT)
            product = raised * dot(value, grad_ref[tile, columns], 1, 1)
            stats_ref[head, 0:1, tile] = top
            stats_ref[head, 1:2, tile] = jnp.sum(raised, axis=0, keepdims=True)
            stats_ref[head, 2:3, tile] = jnp.sum(product, axis=0, keepdims=True)
        return carry

    lax.fori_loop(0, heads, one_head, 0)


def far_kernel(
    selection_ref,
    position_ref,
    rows_ref,
    listed_ref,
    own_stats_ref,
    terms_ref,
    grad_scores_ref,
    stats_ref,
    score_ref,
    grad_prob_ref,
    prob_ref,
    grad_score_ref,
    term_ref,
    terms_sem,
    grad_scores_sem,
):
    heads, _, rows = own_stats_ref.shape
    chunks, _, _, chunk, width = listed_ref.shape
    block = position_ref[0]
    copies = []

    def send(source, target, sem):
        copies.append(pltpu.make_async_copy(source, target, sem))
        copies[-1].start()

    for head in range(heads):
        columns, grad_columns = head_columns(head), head_columns(head, width)
        live = [
            selection_ref[(block * heads + head) * TOPK + slot] < block for slot in range(TOPK)
        ]
        keys = [listed_ref[:, 0, slot, :, columns].reshape(rows, HEAD_DIM) for slot in range(TOPK)]
        values = [
            listed_ref[:, 1, slot, :, columns].reshape(rows, HEAD_DIM) for slot in range(TOPK)
        ]
        for first in range(0, rows, TILE):
            tile = pl.ds(first, TILE)
            query, grad = rows_ref[tile, columns], rows_ref[tile, grad_columns]
            top = jnp.full((1, TILE), MASKED, jnp.float32)
            for slot in range(TOPK):
                scores = dot(keys[slot], query, 1, 1)
                score_ref[head, slot, :, tile] = scores
                highest = jnp.max(scores, axis=0, keepdims=True)
                top = jnp.maximum(top, jnp.where(live[slot], highest, MASKED))
            total = jnp.zeros_like(top)
            product = jnp.zeros_like(top)
            for slot in range(TOPK):
                shift = jnp.where(live[slot], top, -MASKED)
                raised = jnp.exp2((score_ref[head, slot, :, tile] - shift) * EXPONENT)
                score_ref[head, slot, :, tile] = raised
                grad_probs = dot(values[slot], grad, 1, 1)
                grad_prob_ref[head, slot, :, tile] = grad_probs
                total += jnp.sum(raised, axis=0, keepdims=True)
                product += jnp.sum(raised * grad_probs, axis=0, keepdims=True)
            own_top = own_stats_ref[head, 0:1, tile]
            highest = jnp.maximum(own_top, top)
            own_factor = jnp.exp2((own_top - highest) * EXPONENT)
            factor = jnp.exp2((top - highest) * EXPONENT)
            inverse = 1.0 / (own_factor * own_stats_ref[head, 1:2, tile] + factor * total)
            own_weight, weight = own_factor * inverse, factor * inverse
            delta = own_weight * own_stats_ref[head, 2:3, tile] + weight * product
            stats_ref[head, 0:1, tile] = own_weight
            stats_ref[head, 1:2, tile] = delta
            for slot in range(TOPK):
                probability = score_ref[head, slot, :, tile] * weight
                prob_ref[head, slot, :, tile] = probability.astype(jnp.bfloat16)
                grad_score_ref[head, slot, :, tile] = (
                    probability * (grad_prob_ref[head, slot, :, tile] - delta)
                ).astype(jnp.bfloat16)
        query, grad = rows_ref[:, columns], rows_ref[:, grad_columns]
        shape = (chunks, chunk, HEAD_DIM)
        for slot in range(TOPK):
            grad_scores = grad_score_ref[head, slot]
            send(
                grad_score_ref.at[head, slot],
                grad_scores_ref.at[head, slot],
                grad_scores_sem.at[head, slot],
            )
            grad_key = dot(grad_scores, query, 1, 0) * SCALING
            grad_value = dot(prob_ref[head, slot], grad, 1, 0)
            for which, term in enumerate((grad_key, grad_value)):
                term_ref[:, which, slot, :, columns] = term.astype(jnp.bfloat16).reshape(shape)
                send(
                    term_ref.at[:, which, slot, :, columns],
                    terms_ref.at[:, which, slot, :, columns],
                    terms_sem.at[head, slot, which],
                )
    for copy in copies:
        copy.wait()


def own_backward_kernel(
    query_ref,
    key_ref,
    value_ref,
    grad_ref,
    listed_ref,
    grad_scores_ref,
    own_stats_ref,
    stats_ref,
    own_ref,
):
    heads, _, rows = stats_ref.shape
    chunks, _, chunk, _ = own_ref.shape

    def one_head(head, carry):
        columns = head_columns(head)
        query, key = query_ref[:, columns], key_ref[:, columns]
        value, grad = value_ref[:, columns], grad_ref[:, columns]
        shape = (chunks, chunk, HEAD_DIM)
        scores = causal(dot(key, query, 1, 1), 0)
        raised = jnp.exp2((scores - own_stats_ref[head, 0:1, :]) * EXPONENT)
        probability = raised * stats_ref[head, 0:1, :]
        grad_probs = dot(value, grad, 1, 1)
        grad_scores = (probability * (grad_probs - stats_ref[head, 1:2, :])).astype(jnp.bfloat16)
        grad_key = dot(grad_scores, query, 1, 0) * SCALING
        own_ref[:, 1, :, columns] = grad_key.reshape(shape)
        grad_value = dot(probability.astype(jnp.bfloat16), grad, 1, 0)
        own_ref[:, 2, :, columns] = grad_value.reshape(shape)
        part = dot(key.T, grad_scores, 1, 0)
        for slot in range(TOPK):
            listed = listed_ref[:, 0, slot, :, columns].reshape(rows, HEAD_DIM)
            part += dot(listed.T, grad_scores_ref[head, slot], 1, 0)
        own_ref[:, 0, :, columns] = (part * SCALING).T.reshape(shape)
        return carry

    lax.fori_loop(0, heads, one_head, 0)


def finish_kernel(own_ref, others_ref, out_ref):
    out_ref[:, 0] = own_ref[:, 0].astype(jnp.bfloat16)
    out_ref[:, 1:] = (others_ref[...].astype(jnp.float32) + own_ref[:, 1:]).astype(jnp.bfloat16)


def lay_kernel(parts_ref, *refs):
    outs, sem = refs[:-1], refs[-1]
    senders, _, _, width = parts_ref.shape
    copies = [
        pltpu.make_async_copy(
            parts_ref.at[sender, index],
            out.at[:, pl.ds(sender * width, width)],
            sem.at[index, sender],
        )
        for index, out in enumerate(outs)
        for sender in range(senders)
    ]
    for copy in copies:
        copy.start()
    for copy in copies:
        copy.wait()


def on_device(query_input, key_input, value_input, grad_output, selection):
    rows, width = query_input.shape
    heads = width // HEAD_DIM
    chain, spread = lax.axis_size("chain"), lax.axis_size("heads")
    chunk = rows // chain
    share = rows // spread
    listed = selection.reshape(-1)
    position = lax.axis_index("chain").astype(jnp.int32).reshape(1)
    smem = pl.BlockSpec(memory_space=pltpu.SMEM)
    vmem = pl.BlockSpec(memory_space=pltpu.VMEM)
    anywhere = pl.BlockSpec(memory_space=pl.ANY)
    low, full = jnp.bfloat16, jnp.float32

    def swap(array, axis):
        return lax.all_to_all(array, axis, split_axis=0, concat_axis=0, tiled=True)

    def call(kernel, name, in_specs, out_specs, out_shape, scratch=(), limit=4, slots=0):
        flops = 2 * heads * slots * rows * rows * HEAD_DIM
        return pl.pallas_call(
            kernel,
            out_shape=out_shape,
            in_specs=in_specs,
            out_specs=out_specs,
            scratch_shapes=list(scratch),
            cost_estimate=pl.CostEstimate(
                flops=flops, bytes_accessed=4 * MIB, transcendentals=heads * rows * rows
            ),
            compiler_params=pltpu.CompilerParams(vmem_limit_bytes=limit * MIB),
            name=name,
        )

    pair = call(
        stack_kernel,
        "stack",
        [anywhere] * 2,
        anywhere,
        jax.ShapeDtypeStruct((chain, 2, chunk, width), low),
        [
            pltpu.VMEM((2, chain, chunk, width), low),
            pltpu.SemaphoreType.DMA((2, 2)),
            pltpu.SemaphoreType.DMA((2, 2)),
        ],
        limit=59,
    )(key_input.reshape(chain, chunk, width), value_input.reshape(chain, chunk, width))
    held = swap(pair, "chain")
    picked = call(
        pick_kernel,
        "pick",
        [smem, vmem],
        anywhere,
        jax.ShapeDtypeStruct((chain, 2, TOPK, chunk, width), low),
        [
            pltpu.VMEM((chain, 2, TOPK, chunk, width), low),
            pltpu.SemaphoreType.DMA((chain,)),
        ],
    )(listed, held)
    slots = swap(picked, "chain")
    own_rows, own_stats = call(
        own_forward_kernel,
        "own_forward",
        [vmem] * 4,
        (vmem, vmem),
        (
            jax.ShapeDtypeStruct((rows, 2 * width), low),
            jax.ShapeDtypeStruct((heads, STATS, rows), full),
        ),
        limit=12,
        slots=2,
    )(query_input, key_input, value_input, grad_output)
    terms, grad_scores, stats = call(
        far_kernel,
        "far",
        [smem, smem] + [vmem] * 3,
        (anywhere, anywhere, vmem),
        (
            jax.ShapeDtypeStruct((chain, 2, TOPK, chunk, width), low),
            jax.ShapeDtypeStruct((heads, TOPK, rows, rows), low),
            jax.ShapeDtypeStruct((heads, STATS, rows), full),
        ),
        [
            pltpu.VMEM((heads, TOPK, rows, rows), full),
            pltpu.VMEM((heads, TOPK, rows, rows), full),
            pltpu.VMEM((heads, TOPK, rows, rows), low),
            pltpu.VMEM((heads, TOPK, rows, rows), low),
            pltpu.VMEM((chain, 2, TOPK, chunk, width), low),
            pltpu.SemaphoreType.DMA((heads, TOPK, 2)),
            pltpu.SemaphoreType.DMA((heads, TOPK)),
        ],
        limit=32,
        slots=4 * TOPK,
    )(listed, position, own_rows, slots, own_stats)
    returned = swap(terms, "chain")
    own = call(
        own_backward_kernel,
        "own_backward",
        [vmem] * 8,
        vmem,
        jax.ShapeDtypeStruct((chain, 3, chunk, width), full),
        limit=12,
        slots=5 + TOPK,
    )(
        query_input, key_input, value_input, grad_output, slots, grad_scores, own_stats, stats
    )
    summed = call(
        reduce_kernel,
        "reduce",
        [smem, vmem],
        anywhere,
        jax.ShapeDtypeStruct((chain, 2, chunk, width), low),
        [
            pltpu.VMEM((chain, 2, chunk, width), full),
            pltpu.VMEM((chain, 2, chunk, width), low),
            pltpu.SemaphoreType.DMA((4,)),
        ],
    )(listed, returned)
    others = swap(summed, "chain")

    def by_share(array):
        lead = array.shape[1:-2]
        array = array.reshape((spread, chain // spread) + lead + (chunk, width))
        return jnp.moveaxis(array, 1, -3).reshape((spread,) + lead + (share, width))

    whole = call(
        finish_kernel,
        "finish",
        [vmem] * 2,
        vmem,
        jax.ShapeDtypeStruct((spread, 3, share, width), low),
    )(by_share(own), by_share(others))
    whole = swap(whole, "heads")
    return call(
        lay_kernel,
        "lay",
        [vmem],
        (anywhere,) * 3,
        (jax.ShapeDtypeStruct((share, spread * width), low),) * 3,
        [pltpu.SemaphoreType.DMA((3, spread))],
    )(whole)


def solution(mesh):
    in_specs = (
        P("chain", "heads"),
        P("chain", "heads"),
        P("chain", "heads"),
        P("chain", "heads"),
        P(None, "heads", None),
    )
    out_specs = (
        P(("chain", "heads"), None),
        P(("chain", "heads"), None),
        P(("chain", "heads"), None),
    )
    return jax.shard_map(
        on_device, mesh=mesh, in_specs=in_specs, out_specs=out_specs, check_vma=False
    )
```

time: 145 us -> 138 us (0.952)
  waiting for transfers between devices: 57.6 us -> 31.5 us
  blocking collectives: 39.7 us -> 61.2 us
  starting transfers between devices: 26.2 us -> 15.7 us
  Pallas kernels: 14.1 us -> 21 us
  local copies, waits for them, and re-layouts: 3.37 us -> 6.84 us
  other arithmetic: 2.85 us -> 0 us
    all_to_all x4 -> x3, waiting for transfers between devices: 57.6 us -> 31.5 us  [swap(): return lax.all_to_all(array, axis, split_axis=0, concat_axis=0, tiled=True)]
    all_to_all x2, blocking collectives: 39.7 us -> 61.2 us  [swap(): return lax.all_to_all(array, axis, split_axis=0, concat_axis=0, tiled=True)]
    all_to_all x4 -> x3, starting transfers between devices: 26.2 us -> 15.7 us  [swap(): return lax.all_to_all(array, axis, split_axis=0, concat_axis=0, tiled=True)]
    pallas_call x3 -> x8, Pallas kernels: 14.1 us -> 21 us  [the longest x1 9.51 us: on_device(): call(far_kernel, 'far', [smem, smem] + [vmem] * 3, (anywhere, anywhere, v...]
    unnamed x14 -> x25, local copies, waits for them, and re-layouts: 1.1 us -> 6.72 us
    reshape x3 -> x0, local copies, waits for them, and re-layouts: 2.16 us -> none  [lay(): return array.swapaxes(0, 1).reshape(share, spread * width)]
    another operation x1 -> x0, other arithmetic: 1.87 us -> none  [on_device(): jnp.stack([part.reshape(chain, chunk, width) for part in (key_input, valu...]
  transfers between devices with their start and end apart: 4 -> 3, of which waited for: 4 -> 3; matrix products, arithmetic and copies ran while one was open for 1% -> 0% of each run, Pallas kernels for 0% -> 2%
where the time goes in v2:
time: 138 us; the launch traced here: 137 us
  blocking collectives  61.2 us (44%)
  waiting for transfers between devices  31.5 us (23%)
  Pallas kernels  21 us (15%)
  starting transfers between devices  15.7 us (11%)
  local copies, waits for them, and re-layouts  6.84 us (5%)
    all_to_all x2, blocking collectives, swap(): return lax.all_to_all(array, axis, split_axis=0, concat_axis=0, tiled=True)  61.2 us
    all_to_all x3, waiting for transfers between devices, swap(): return lax.all_to_all(array, axis, split_axis=0, concat_axis=0, tiled=True)  31.5 us
    all_to_all x3, starting transfers between devices, swap(): return lax.all_to_all(array, axis, split_axis=0, concat_axis=0, tiled=True)  15.7 us
    pallas_call x1, Pallas kernels, on_device(): call(far_kernel, 'far', [smem, smem] + [vmem] * 3, (anywhere, anywhere, v...  9.51 us
    unnamed x25, local copies, waits for them, and re-layouts  6.72 us
  transfers between devices with their start and end apart: 3, of which 3 were waited for; matrix products, arithmetic and copies ran while one was open for 0% of the time, Pallas kernels for 2%

profile of v2, /device:TPU:1, one launch (start us, length us, event | category | flops | bytes accessed | tf_op | source)
XLA Modules:
  0.0 137.0 jit_solution(16473592570564965534)
XLA Ops:
  0.6 0.0 copy-start.11
  0.6 1.8 %stack.1 = bf16[16,2,32,256]{3,2,1,0:T(8,128)(2,1)} custom-call(bf16[16,32,256]{2,1,0:T(8,128)(2,1)} %bitcast.3, bf16[16,32,256]{2,1,0:T(8,128)(2,1)} %bitcast.4), custom_call_target="tpu_custom_call" | custom-call | bytes 4194304 | tf_op jit(solution)/shard_map/stack/pallas_call | solution.py:311
  2.5 7.6 %all-to-all-start = ((bf16[16,2,32,256]{3,2,1,0:T(8,128)(2,1)}), bf16[16,2,32,256]{3,2,1,0:T(8,128)(2,1)S(1)}, u32[]{:S(2)}, u32[]{:S(2)}) async-start(bf16[16,2,32,256]{3,2,1,0:T(8,128)(2,1)} %stack.1), calls=%async_computation | async-start | bytes 1048576 | tf_op jit(solution)/shard_map/all_to_all | solution.py:294
  10.1 0.0 copy-done.11
  10.1 0.1 copy.9
  10.2 0.1 reshape.18.selection_ref
  10.3 10.3 %all-to-all-done.held_ref = bf16[16,2,32,256]{3,2,1,0:T(8,128)(2,1)S(1)} async-done(((bf16[16,2,32,256]{3,2,1,0:T(8,128)(2,1)}), bf16[16,2,32,256]{3,2,1,0:T(8,128)(2,1)S(1)}, u32[]{:S(2)}, u32[]{:S(2)}) %all-to-all-start) | async-done | bytes 524320 | tf_op jit(solution)/shard_map/all_to_all | solution.py:294
  20.6 1.9 %pick.1 = bf16[16,2,3,32,256]{4,3,2,1,0:T(8,128)(2,1)} custom-call(s32[96]{0:T(128)S(1)} %reshape.18.selection_ref, bf16[16,2,32,256]{3,2,1,0:T(8,128)(2,1)S(1)} %all-to-all-done.held_ref), custom_call_target="tpu_custom_call" | custom-call | bytes 4194304 | tf_op jit(solution)/shard_map/pick/pallas_call | solution.py:325
  22.5 0.0 copy-start.2
  22.5 0.0 copy-start.3
  22.5 0.0 copy-start.5
  22.5 0.0 copy-start.7
  22.5 3.9 %all-to-all-start.1 = ((bf16[16,2,3,32,256]{4,3,2,1,0:T(8,128)(2,1)}), bf16[16,2,3,32,256]{4,3,2,1,0:T(8,128)(2,1)S(1)}, u32[]{:S(2)}, u32[]{:S(2)}) async-start(bf16[16,2,3,32,256]{4,3,2,1,0:T(8,128)(2,1)} %pick.1), calls=%async_computation.1 | async-start | bytes 3145728 | tf_op jit(solution)/shard_map/all_to_all | solution.py:294
  26.4 0.0 copy-done.2
  26.4 0.0 copy-done.3
  26.4 0.0 copy-done.5
  26.4 0.0 copy-done.7
  26.4 1.2 own_forward.1
  27.6 0.0 copy-start.9
  27.6 0.8 copy-done.9
  28.5 18.5 %all-to-all-done.1.listed_ref = bf16[16,2,3,32,256]{4,3,2,1,0:T(8,128)(2,1)S(1)} async-done(((bf16[16,2,3,32,256]{4,3,2,1,0:T(8,128)(2,1)}), bf16[16,2,3,32,256]{4,3,2,1,0:T(8,128)(2,1)S(1)}, u32[]{:S(2)}, u32[]{:S(2)}) %all-to-all-start.1) | async-done | bytes 1572896 | tf_op jit(solution)/shard_map/all_to_all | solution.py:294
  46.9 0.0 copy-start.10
  46.9 1.0 copy-done.10
  48.0 9.5 %far.1 = (bf16[16,2,3,32,256]{4,3,2,1,0:T(8,128)(2,1)S(1)}, bf16[2,3,512,512]{3,2,1,0:T(8,128)(2,1)S(1)}, f32[2,8,512]{2,1,0:T(8,128)S(1)}) custom-call(s32[96]{0:T(128)S(1)} %reshape.18.selection_ref, s32[1]{0:T(128)} %bitcast.2.position_ref, bf16[512,512]{1,0:T(8,128)(2,1)S(1)} %copy-done.10, bf16[16,2,3,32,256]{4,3,2,1,0:T(8,128)(2,1)S(1)} %all-to-all-done.1.listed_ref, ...), custom_call_target="tpu_custom_call" | custom-call | flops 1610612736 | bytes 4194304 | tf_op jit(solution)/shard_map/far/pallas_call | solution.py:349
  57.5 0.0 copy-start
  57.5 27.1 %all_to_all.25.terms_ref = bf16[16,2,3,32,256]{4,3,2,1,0:T(8,128)(2,1)S(1)} all-to-all(bf16[16,2,3,32,256]{4,3,2,1,0:T(8,128)(2,1)S(1)} %get-tuple-element.12), channel_id=1, replica_groups=mesh['chain'=16,'heads'=16] {'chain'}, dimensions={0} | all-to-all | bytes 3145728 | tf_op jit(solution)/shard_map/all_to_all | solution.py:294
  84.6 0.0 copy-done
  84.6 1.9 %reduce.1 = bf16[16,2,32,256]{3,2,1,0:T(8,128)(2,1)} custom-call(s32[96]{0:T(128)S(1)} %reshape.18.selection_ref, bf16[16,2,3,32,256]{4,3,2,1,0:T(8,128)(2,1)S(1)} %all_to_all.25.terms_ref), custom_call_target="tpu_custom_call" | custom-call | bytes 4194304 | tf_op jit(solution)/shard_map/reduce/pallas_call | solution.py:383
  86.5 4.2 %all-to-all-start.3 = ((bf16[16,2,32,256]{3,2,1,0:T(8,128)(2,1)}), bf16[16,2,32,256]{3,2,1,0:T(8,128)(2,1)}, u32[]{:S(2)}, u32[]{:S(2)}) async-start(bf16[16,2,32,256]{3,2,1,0:T(8,128)(2,1)} %reduce.1), calls=%async_computation.3 | async-start | bytes 1048576 | tf_op jit(solution)/shard_map/all_to_all | solution.py:294
  90.8 0.0 copy-start.1
  90.8 1.9 %copy-done.1 = bf16[2,3,512,512]{3,2,1,0:T(8,128)(2,1)S(1)} copy-done((bf16[2,3,512,512]{3,2,1,0:T(8,128)(2,1)S(1)}, bf16[2,3,512,512]{3,2,1,0:T(8,128)(2,1)}, u32[]{:S(2)}) %copy-start.1) | copy-done | bytes 3145752
  92.7 0.0 copy-start.4
  92.7 0.9 copy-done.4
  93.6 0.0 copy-start.6
  93.6 0.9 copy-done.6
  94.6 0.0 copy-start.8
  94.6 0.9 copy-done.8
  95.5 2.2 %own_backward.1.own_ref = f32[16,3,32,256]{3,2,1,0:T(8,128)S(1)} custom-call(bf16[512,256]{1,0:T(8,128)(2,1)S(1)} %copy-done.6, bf16[512,256]{1,0:T(8,128)(2,1)S(1)} %copy-done.2, bf16[512,256]{1,0:T(8,128)(2,1)S(1)} %copy-done.4, bf16[512,256]{1,0:T(8,128)(2,1)S(1)} %copy-done.8, bf16[16,2,3,32,256]{4,3,2,1,0:T(8,128)(2,1)S(1)} %all-to-all-done.1.listed_ref, ...), custom_call_target="tpu_custom_call" | custom-call | flops 1073741824 | bytes 4194304 | tf_op jit(solution)/shard_map/own_backward/pallas_call | solution.py:372
  97.7 2.7 %all-to-all-done.3.others_ref = bf16[16,2,32,256]{3,2,1,0:T(8,128)(2,1)} async-done(((bf16[16,2,32,256]{3,2,1,0:T(8,128)(2,1)}), bf16[16,2,32,256]{3,2,1,0:T(8,128)(2,1)}, u32[]{:S(2)}, u32[]{:S(2)}) %all-to-all-start.3) | async-done | bytes 524320 | tf_op jit(solution)/shard_map/all_to_all | solution.py:294
  100.4 1.2 finish.1
  101.6 34.1 %all_to_all.26.parts_ref = bf16[16,3,32,256]{3,2,1,0:T(8,128)(2,1)S(1)} all-to-all(bf16[16,3,32,256]{3,2,1,0:T(8,128)(2,1)S(1)} %finish.1), channel_id=1, replica_groups=mesh['chain'=16,'heads'=16] {'heads'}, dimensions={0} | all-to-all | bytes 1572864 | tf_op jit(solution)/shard_map/all_to_all | solution.py:294
  135.7 1.3 lay.1
Async XLA Ops:
  0.6 9.4 %copy-start.11 = (s32[16,2,3]{0,1,2:T(2,128)S(1)}, s32[16,2,3]{0,1,2:T(2,128)}, u32[]{:S(2)}) copy-start(s32[16,2,3]{0,1,2:T(2,128)} %param.9) | copy-start | bytes 1156
  2.5 18.1 %all-to-all-start = ((bf16[16,2,32,256]{3,2,1,0:T(8,128)(2,1)}), bf16[16,2,32,256]{3,2,1,0:T(8,128)(2,1)S(1)}, u32[]{:S(2)}, u32[]{:S(2)}) async-start(bf16[16,2,32,256]{3,2,1,0:T(8,128)(2,1)} %stack.1), calls=%async_computation | async-start | bytes 1048576 | tf_op jit(solution)/shard_map/all_to_all | solution.py:294
  22.5 3.9 %copy-start.2 = (bf16[512,256]{1,0:T(8,128)(2,1)S(1)}, bf16[512,256]{1,0:T(8,128)(2,1)}, u32[]{:S(2)}) copy-start(bf16[512,256]{1,0:T(8,128)(2,1)} %key_ref.3) | copy-start | bytes 786436
  22.5 3.9 %copy-start.3 = (bf16[512,256]{1,0:T(8,128)(2,1)S(1)}, bf16[512,256]{1,0:T(8,128)(2,1)}, u32[]{:S(2)}) copy-start(bf16[512,256]{1,0:T(8,128)(2,1)} %value_ref.3) | copy-start | bytes 786436
  22.5 3.9 %copy-start.5 = (bf16[512,256]{1,0:T(8,128)(2,1)S(1)}, bf16[512,256]{1,0:T(8,128)(2,1)}, u32[]{:S(2)}) copy-start(bf16[512,256]{1,0:T(8,128)(2,1)} %query_ref.3) | copy-start | bytes 786436
  22.5 3.9 %copy-start.7 = (bf16[512,256]{1,0:T(8,128)(2,1)S(1)}, bf16[512,256]{1,0:T(8,128)(2,1)}, u32[]{:S(2)}) copy-start(bf16[512,256]{1,0:T(8,128)(2,1)} %grad_ref.3) | copy-start | bytes 786436
  22.5 24.4 %all-to-all-start.1 = ((bf16[16,2,3,32,256]{4,3,2,1,0:T(8,128)(2,1)}), bf16[16,2,3,32,256]{4,3,2,1,0:T(8,128)(2,1)S(1)}, u32[]{:S(2)}, u32[]{:S(2)}) async-start(bf16[16,2,3,32,256]{4,3,2,1,0:T(8,128)(2,1)} %pick.1), calls=%async_computation.1 | async-start | bytes 3145728 | tf_op jit(solution)/shard_map/all_to_all | solution.py:294
  27.6 0.8 copy-start.9
  46.9 1.0 copy-start.10
  57.5 27.1 %copy-start = (bf16[2,3,512,512]{3,2,1,0:T(8,128)(2,1)}, bf16[2,3,512,512]{3,2,1,0:T(8,128)(2,1)S(1)}, u32[]{:S(2)}) copy-start(bf16[2,3,512,512]{3,2,1,0:T(8,128)(2,1)S(1)} %get-tuple-element.10.grad_scores_ref) | copy-start | bytes 9437188
  86.5 13.9 %all-to-all-start.3 = ((bf16[16,2,32,256]{3,2,1,0:T(8,128)(2,1)}), bf16[16,2,32,256]{3,2,1,0:T(8,128)(2,1)}, u32[]{:S(2)}, u32[]{:S(2)}) async-start(bf16[16,2,32,256]{3,2,1,0:T(8,128)(2,1)} %reduce.1), calls=%async_computation.3 | async-start | bytes 1048576 | tf_op jit(solution)/shard_map/all_to_all | solution.py:294
  90.8 1.9 %copy-start.1 = (bf16[2,3,512,512]{3,2,1,0:T(8,128)(2,1)S(1)}, bf16[2,3,512,512]{3,2,1,0:T(8,128)(2,1)}, u32[]{:S(2)}) copy-start(bf16[2,3,512,512]{3,2,1,0:T(8,128)(2,1)} %copy-done) | copy-start | bytes 9437188
  92.7 0.9 copy-start.4
  93.6 0.9 copy-start.6
  94.6 0.9 copy-start.8

commit v3 on v2

v3 whole, which is shorter than its diff:
```python
import math

import jax
import jax.numpy as jnp
from jax import lax
from jax.experimental import pallas as pl
from jax.experimental.pallas import tpu as pltpu
from jax.sharding import PartitionSpec as P

HEAD_DIM = 128
TOPK = 3
MASKED = -1e30
SCALING = HEAD_DIM ** (-0.5)
EXPONENT = SCALING * math.log2(math.e)
TILE = 256
STATS = 8
MIB = 1 << 20


def head_columns(head, offset=0):
    start = head * HEAD_DIM + offset
    if isinstance(head, int):
        return pl.ds(start, HEAD_DIM)
    return pl.ds(pl.multiple_of(start, HEAD_DIM), HEAD_DIM)


def dot(left, right, left_dim, right_dim):
    return lax.dot_general(
        left, right, (((left_dim,), (right_dim,)), ((), ())), preferred_element_type=jnp.float32
    )


def stack_kernel(key_ref, value_ref, out_ref, held_ref, in_sem, out_sem):
    pieces = in_sem.shape[1]
    length = key_ref.shape[0] // pieces
    arrive, leave = [], []
    for index, part in enumerate((key_ref, value_ref)):
        for piece in range(pieces):
            span = pl.ds(piece * length, length)
            held = held_ref.at[index, span]
            arrive.append(pltpu.make_async_copy(part.at[span], held, in_sem.at[index, piece]))
            leave.append(
                pltpu.make_async_copy(held, out_ref.at[span, index], out_sem.at[index, piece])
            )
    for copy in arrive:
        copy.start()
    for first, second in zip(arrive, leave):
        first.wait()
        second.start()
    for copy in leave:
        copy.wait()


def pick_kernel(selection_ref, held_ref, after_ref, out_ref):
    blocks, _, _, width = held_ref.shape
    heads = width // HEAD_DIM
    for block in range(blocks):
        for head in range(heads):
            for slot in range(TOPK):
                source = selection_ref[(block * heads + head) * TOPK + slot]
                out_ref[block, :, slot, :, head_columns(head)] = held_ref[
                    source, :, :, head_columns(head)
                ]


def reduce_kernel(selection_ref, terms_ref, out_ref, *total_refs):
    blocks, _, _, width = out_ref.shape
    heads = width // HEAD_DIM
    for total_ref in total_refs:
        total_ref[...] = jnp.zeros_like(total_ref)

    def add(block, carry):
        for slot in range(TOPK):
            for head, total_ref in enumerate(total_refs):
                target = selection_ref[(block * heads + head) * TOPK + slot]
                total_ref[target] += terms_ref[block, :, slot, :, head_columns(head)].astype(
                    jnp.float32
                )
        return carry

    lax.fori_loop(0, blocks, add, 0, unroll=4)
    for head, total_ref in enumerate(total_refs):
        out_ref[:, :, :, head_columns(head)] = total_ref[...].astype(out_ref.dtype)


def causal(scores, first):
    key_at = lax.broadcasted_iota(jnp.int32, scores.shape, 0)
    query_at = lax.broadcasted_iota(jnp.int32, scores.shape, 1) + first
    return jnp.where(key_at <= query_at, scores, MASKED)


def own_forward_kernel(
    query_ref, key_ref, value_ref, grad_ref, rows_ref, stats_ref, held_ref, sem
):
    heads, _, rows = stats_ref.shape
    targets = (rows_ref, held_ref.at[0], held_ref.at[1], held_ref.at[2])
    copies = [
        pltpu.make_async_copy(source, target, sem.at[index])
        for index, (source, target) in enumerate(
            zip((query_ref, key_ref, value_ref, grad_ref), targets)
        )
    ]
    for copy in copies:
        copy.start()
    for copy in copies:
        copy.wait()

    def one_head(head, carry):
        columns = head_columns(head)
        key, value = held_ref[0, :, columns], held_ref[1, :, columns]
        for first in range(0, rows, TILE):
            tile = pl.ds(first, TILE)
            scores = causal(dot(key, rows_ref[tile, columns], 1, 1), first)
            top = jnp.max(scores, axis=0, keepdims=True)
            raised = jnp.exp2((scores - top) * EXPONENT)
            product = raised * dot(value, held_ref[2, tile, columns], 1, 1)
            stats_ref[head, 0:1, tile] = top
            stats_ref[head, 1:2, tile] = jnp.sum(raised, axis=0, keepdims=True)
            stats_ref[head, 2:3, tile] = jnp.sum(product, axis=0, keepdims=True)
        return carry

    lax.fori_loop(0, heads, one_head, 0)


def far_kernel(
    selection_ref,
    position_ref,
    rows_ref,
    grad_ref,
    listed_ref,
    own_stats_ref,
    terms_ref,
    part_ref,
    stats_ref,
    grad_rows_ref,
    sem,
    *scratch,
):
    heads, _, rows = own_stats_ref.shape
    chunks, _, _, chunk, _ = listed_ref.shape
    block = position_ref[0]
    fetch = pltpu.make_async_copy(grad_ref, grad_rows_ref, sem)
    fetch.start()

    def listed(which, slot, head):
        return listed_ref[:, which, slot, :, head_columns(head)].reshape(rows, HEAD_DIM)

    def softmax(head):
        score_ref, grad_prob_ref, prob_ref, grad_score_ref = scratch[4 * head : 4 * head + 4]
        columns = head_columns(head)
        live = [
            selection_ref[(block * heads + head) * TOPK + slot] < block for slot in range(TOPK)
        ]
        for first in range(0, rows, TILE):
            tile = pl.ds(first, TILE)
            top = jnp.full((1, TILE), MASKED, jnp.float32)
            for slot in range(TOPK):
                scores = dot(listed(0, slot, head), rows_ref[tile, columns], 1, 1)
                score_ref[slot, :, tile] = scores
                highest = jnp.max(scores, axis=0, keepdims=True)
                top = jnp.maximum(top, jnp.where(live[slot], highest, MASKED))
            if head == 0 and first == 0:
                fetch.wait()
            total = jnp.zeros_like(top)
            product = jnp.zeros_like(top)
            for slot in range(TOPK):
                shift = jnp.where(live[slot], top, -MASKED)
                raised = jnp.exp2((score_ref[slot, :, tile] - shift) * EXPONENT)
                score_ref[slot, :, tile] = raised
                grad_probs = dot(listed(1, slot, head), grad_rows_ref[tile, columns], 1, 1)
                grad_prob_ref[slot, :, tile] = grad_probs
                total += jnp.sum(raised, axis=0, keepdims=True)
                product += jnp.sum(raised * grad_probs, axis=0, keepdims=True)
            own_top = own_stats_ref[head, 0:1, tile]
            highest = jnp.maximum(own_top, top)
            own_factor = jnp.exp2((own_top - highest) * EXPONENT)
            factor = jnp.exp2((top - highest) * EXPONENT)
            inverse = 1.0 / (own_factor * own_stats_ref[head, 1:2, tile] + factor * total)
            own_weight, weight = own_factor * inverse, factor * inverse
            delta = own_weight * own_stats_ref[head, 2:3, tile] + weight * product
            stats_ref[head, 0:1, tile] = own_weight
            stats_ref[head, 1:2, tile] = delta
            for slot in range(TOPK):
                probability = score_ref[slot, :, tile] * weight
                prob_ref[slot, :, tile] = probability.astype(jnp.bfloat16)
                grad_score_ref[slot, :, tile] = (
                    probability * (grad_prob_ref[slot, :, tile] - delta)
                ).astype(jnp.bfloat16)

    def gradients(head):
        _, _, prob_ref, grad_score_ref = scratch[4 * head : 4 * head + 4]
        columns = head_columns(head)
        query, grad = rows_ref[:, columns], grad_rows_ref[:, columns]
        shape = (chunks, chunk, HEAD_DIM)
        part = None
        for slot in range(TOPK):
            grad_scores = grad_score_ref[slot]
            grad_key = dot(grad_scores, query, 1, 0) * SCALING
            terms_ref[:, 0, slot, :, columns] = grad_key.astype(jnp.bfloat16).reshape(shape)
            grad_value = dot(prob_ref[slot], grad, 1, 0)
            terms_ref[:, 1, slot, :, columns] = grad_value.astype(jnp.bfloat16).reshape(shape)
            product = dot(listed(0, slot, head).T, grad_scores, 1, 0)
            part = product if part is None else part + product
        part_ref[head] = part

    for head in range(heads):
        softmax(head)
        gradients(head)


def own_backward_kernel(
    query_ref,
    key_ref,
    value_ref,
    grad_ref,
    part_ref,
    own_stats_ref,
    stats_ref,
    own_ref,
):
    heads, _, rows = stats_ref.shape
    chunks, _, chunk, _ = own_ref.shape

    def one_head(head, carry):
        columns = head_columns(head)
        query, key = query_ref[:, columns], key_ref[:, columns]
        value, grad = value_ref[:, columns], grad_ref[:, columns]
        scores = causal(dot(key, query, 1, 1), 0)
        raised = jnp.exp2((scores - own_stats_ref[head, 0:1, :]) * EXPONENT)
        probability = raised * stats_ref[head, 0:1, :]
        grad_probs = dot(value, grad, 1, 1)
        grad_scores = (probability * (grad_probs - stats_ref[head, 1:2, :])).astype(jnp.bfloat16)
        results = (
            ((part_ref[head] + dot(key.T, grad_scores, 1, 0)) * SCALING).T,
            dot(grad_scores, query, 1, 0) * SCALING,
            dot(probability.astype(jnp.bfloat16), grad, 1, 0),
        )
        for index, result in enumerate(results):
            own_ref[:, index, :, columns] = result.astype(jnp.bfloat16).reshape(
                chunks, chunk, HEAD_DIM
            )
        return carry

    lax.fori_loop(0, heads, one_head, 0)


def finish_kernel(own_ref, others_ref, out_ref):
    out_ref[:, 0] = own_ref[:, 0]
    out_ref[:, 1:] = (
        others_ref[...].astype(jnp.float32) + own_ref[:, 1:].astype(jnp.float32)
    ).astype(jnp.bfloat16)


def lay_kernel(parts_ref, *refs):
    outs, sem = refs[:-1], refs[-1]
    senders, _, _, width = parts_ref.shape
    copies = [
        pltpu.make_async_copy(
            parts_ref.at[sender, index],
            out.at[:, pl.ds(sender * width, width)],
            sem.at[index, sender],
        )
        for index, out in enumerate(outs)
        for sender in range(senders)
    ]
    for copy in copies:
        copy.start()
    for copy in copies:
        copy.wait()


def on_device(query_input, key_input, value_input, grad_output, selection):
    rows, width = query_input.shape
    heads = width // HEAD_DIM
    chain, spread = lax.axis_size("chain"), lax.axis_size("heads")
    chunk = rows // chain
    share = rows // spread
    listed = selection.reshape(-1)
    position = lax.axis_index("chain").astype(jnp.int32).reshape(1)
    smem = pl.BlockSpec(memory_space=pltpu.SMEM)
    vmem = pl.BlockSpec(memory_space=pltpu.VMEM)
    anywhere = pl.BlockSpec(memory_space=pl.ANY)
    low, full = jnp.bfloat16, jnp.float32

    def swap(array, axis):
        return lax.all_to_all(array, axis, split_axis=0, concat_axis=0, tiled=True)

    def call(kernel, name, in_specs, out_specs, out_shape, scratch=(), limit=4, slots=0):
        flops = 2 * heads * slots * rows * rows * HEAD_DIM
        return pl.pallas_call(
            kernel,
            out_shape=out_shape,
            in_specs=in_specs,
            out_specs=out_specs,
            scratch_shapes=list(scratch),
            cost_estimate=pl.CostEstimate(
                flops=flops, bytes_accessed=4 * MIB, transcendentals=heads * rows * rows
            ),
            compiler_params=pltpu.CompilerParams(vmem_limit_bytes=limit * MIB),
            name=name,
        )

    pair = call(
        stack_kernel,
        "stack",
        [anywhere] * 2,
        anywhere,
        jax.ShapeDtypeStruct((chain, 2, chunk, width), low),
        [
            pltpu.VMEM((2, chain, chunk, width), low),
            pltpu.SemaphoreType.DMA((2, 2)),
            pltpu.SemaphoreType.DMA((2, 2)),
        ],
        limit=59,
    )(key_input.reshape(chain, chunk, width), value_input.reshape(chain, chunk, width))
    held = swap(pair, "chain")
    own_rows, own_stats = call(
        own_forward_kernel,
        "own_forward",
        [anywhere] * 4,
        (vmem, vmem),
        (
            jax.ShapeDtypeStruct((rows, width), low),
            jax.ShapeDtypeStruct((heads, STATS, rows), full),
        ),
        [pltpu.VMEM((3, rows, width), low), pltpu.SemaphoreType.DMA((4,))],
        limit=58,
        slots=2,
    )(query_input, key_input, value_input, grad_output)
    picked = call(
        pick_kernel,
        "pick",
        [smem, vmem, anywhere],
        vmem,
        jax.ShapeDtypeStruct((chain, 2, TOPK, chunk, width), low),
    )(listed, held, own_stats)
    slots = swap(picked, "chain")
    terms, part, stats = call(
        far_kernel,
        "far",
        [smem, smem, vmem, anywhere, vmem, vmem],
        (vmem, vmem, vmem),
        (
            jax.ShapeDtypeStruct((chain, 2, TOPK, chunk, width), low),
            jax.ShapeDtypeStruct((heads, HEAD_DIM, rows), full),
            jax.ShapeDtypeStruct((heads, STATS, rows), full),
        ),
        [pltpu.VMEM((rows, width), low), pltpu.SemaphoreType.DMA(())]
        + [
            pltpu.VMEM((TOPK, rows, rows), full),
            pltpu.VMEM((TOPK, rows, rows), full),
            pltpu.VMEM((TOPK, rows, rows), low),
            pltpu.VMEM((TOPK, rows, rows), low),
        ]
        * heads,
        limit=32,
        slots=5 * TOPK,
    )(listed, position, own_rows, grad_output, slots, own_stats)
    returned = swap(terms, "chain")
    own = call(
        own_backward_kernel,
        "own_backward",
        [vmem] * 7,
        vmem,
        jax.ShapeDtypeStruct((chain, 3, chunk, width), low),
        limit=12,
        slots=5,
    )(query_input, key_input, value_input, grad_output, part, own_stats, stats)
    summed = call(
        reduce_kernel,
        "reduce",
        [smem, vmem],
        vmem,
        jax.ShapeDtypeStruct((chain, 2, chunk, width), low),
        [pltpu.VMEM((chain, 2, chunk, HEAD_DIM), full)] * heads,
    )(listed, returned)
    others = swap(summed, "chain")

    def by_share(array):
        lead = array.shape[1:-2]
        array = array.reshape((spread, chain // spread) + lead + (chunk, width))
        return jnp.moveaxis(array, 1, -3).reshape((spread,) + lead + (share, width))

    whole = call(
        finish_kernel,
        "finish",
        [vmem] * 2,
        vmem,
        jax.ShapeDtypeStruct((spread, 3, share, width), low),
    )(by_share(own), by_share(others))
    whole = swap(whole, "heads")
    return call(
        lay_kernel,
        "lay",
        [vmem],
        (anywhere,) * 3,
        (jax.ShapeDtypeStruct((share, spread * width), low),) * 3,
        [pltpu.SemaphoreType.DMA((3, spread))],
    )(whole)


def solution(mesh):
    in_specs = (
        P("chain", "heads"),
        P("chain", "heads"),
        P("chain", "heads"),
        P("chain", "heads"),
        P(None, "heads", None),
    )
    out_specs = (
        P(("chain", "heads"), None),
        P(("chain", "heads"), None),
        P(("chain", "heads"), None),
    )
    return jax.shard_map(
        on_device, mesh=mesh, in_specs=in_specs, out_specs=out_specs, check_vma=False
    )
```

time: 138 us -> 133 us (0.964)
  local copies, waits for them, and re-layouts: 6.84 us -> 0.99 us
  waiting for transfers between devices: 31.5 us -> 35.5 us
  Pallas kernels: 21 us -> 18.7 us
    unnamed x25 -> x17, local copies, waits for them, and re-layouts: 6.72 us -> 0.88 us
    all_to_all x3, waiting for transfers between devices: 31.5 us -> 35.5 us  [swap(): return lax.all_to_all(array, axis, split_axis=0, concat_axis=0, tiled=True)]
  transfers between devices with their start and end apart: 3 -> 3, of which waited for: 3 -> 3; matrix products, arithmetic and copies ran while one was open for 0% -> 0% of each run, Pallas kernels for 2% -> 4%
where the time goes in v3:
time: 133 us; the launch traced here: 132 us
  blocking collectives  61.2 us (46%)
  waiting for transfers between devices  35.5 us (27%)
  Pallas kernels  18.7 us (14%)
  starting transfers between devices  15 us (11%)
    all_to_all x2, blocking collectives, swap(): return lax.all_to_all(array, axis, split_axis=0, concat_axis=0, tiled=True)  61.2 us
    all_to_all x3, waiting for transfers between devices, swap(): return lax.all_to_all(array, axis, split_axis=0, concat_axis=0, tiled=True)  35.5 us
    all_to_all x3, starting transfers between devices, swap(): return lax.all_to_all(array, axis, split_axis=0, concat_axis=0, tiled=True)  15 us
    pallas_call x1, Pallas kernels, on_device(): call(far_kernel, 'far', [smem, smem, vmem, anywhere, vmem, vmem], (vmem,...  6.78 us
    pallas_call x1, Pallas kernels, on_device(): call(own_forward_kernel, 'own_forward', [anywhere] * 4, (vmem, vmem), (ja...  2.98 us
  transfers between devices with their start and end apart: 3, of which 3 were waited for; matrix products, arithmetic and copies ran while one was open for 0% of the time, Pallas kernels for 4%

profile of v3, /device:TPU:1, one launch (start us, length us, event | category | flops | bytes accessed | tf_op | source)
XLA Modules:
  0.0 132.2 jit_solution(7247284730187523810)
XLA Ops:
  0.6 0.0 copy-start.7
  0.6 1.8 %stack.1 = bf16[16,2,32,256]{3,2,1,0:T(8,128)(2,1)} custom-call(bf16[16,32,256]{2,1,0:T(8,128)(2,1)} %bitcast.3, bf16[16,32,256]{2,1,0:T(8,128)(2,1)} %bitcast.4), custom_call_target="tpu_custom_call" | custom-call | bytes 4194304 | tf_op jit(solution)/shard_map/stack/pallas_call | solution.py:303
  2.5 7.6 %all-to-all-start = ((bf16[16,2,32,256]{3,2,1,0:T(8,128)(2,1)}), bf16[16,2,32,256]{3,2,1,0:T(8,128)(2,1)S(1)}, u32[]{:S(2)}, u32[]{:S(2)}) async-start(bf16[16,2,32,256]{3,2,1,0:T(8,128)(2,1)} %stack.1), calls=%async_computation | async-start | bytes 1048576 | tf_op jit(solution)/shard_map/all_to_all | solution.py:286
  10.1 0.0 copy-done.7
  10.1 0.1 copy.9
  10.2 0.1 reshape.18.selection_ref
  10.3 3.0 %own_forward.1 = (bf16[512,256]{1,0:T(8,128)(2,1)}, f32[2,8,512]{2,1,0:T(8,128)}) custom-call(bf16[512,256]{1,0:T(8,128)(2,1)} %query_ref.3, bf16[512,256]{1,0:T(8,128)(2,1)} %key_ref.3, bf16[512,256]{1,0:T(8,128)(2,1)} %value_ref.3, bf16[512,256]{1,0:T(8,128)(2,1)} %grad_ref.5), custom_call_target="tpu_custom_call" | custom-call | flops 268435456 | bytes 4194304 | tf_op jit(solution)/shard_map/own_forward/pallas_call | solution.py:317
  13.3 7.3 %all-to-all-done.held_ref = bf16[16,2,32,256]{3,2,1,0:T(8,128)(2,1)S(1)} async-done(((bf16[16,2,32,256]{3,2,1,0:T(8,128)(2,1)}), bf16[16,2,32,256]{3,2,1,0:T(8,128)(2,1)S(1)}, u32[]{:S(2)}, u32[]{:S(2)}) %all-to-all-start) | async-done | bytes 524320 | tf_op jit(solution)/shard_map/all_to_all | solution.py:286
  20.6 0.0 copy-start.4
  20.6 0.8 copy-done.4
  21.4 2.0 %pick.1 = bf16[16,2,3,32,256]{4,3,2,1,0:T(8,128)(2,1)} custom-call(s32[96]{0:T(128)S(1)} %reshape.18.selection_ref, bf16[16,2,32,256]{3,2,1,0:T(8,128)(2,1)S(1)} %all-to-all-done.held_ref, f32[2,8,512]{2,1,0:T(8,128)S(1)} %copy-done.4), custom_call_target="tpu_custom_call" | custom-call | bytes 4194304 | tf_op jit(solution)/shard_map/pick/pallas_call | solution.py:330
  23.4 0.0 copy-start.3
  23.4 0.0 copy-start.5
  23.4 0.0 copy-start.6
  23.4 3.8 %all-to-all-start.1 = ((bf16[16,2,3,32,256]{4,3,2,1,0:T(8,128)(2,1)}), bf16[16,2,3,32,256]{4,3,2,1,0:T(8,128)(2,1)S(1)}, u32[]{:S(2)}, u32[]{:S(2)}) async-start(bf16[16,2,3,32,256]{4,3,2,1,0:T(8,128)(2,1)} %pick.1), calls=%async_computation.1 | async-start | bytes 3145728 | tf_op jit(solution)/shard_map/all_to_all | solution.py:286
  27.3 20.5 %all-to-all-done.1.listed_ref = bf16[16,2,3,32,256]{4,3,2,1,0:T(8,128)(2,1)S(1)} async-done(((bf16[16,2,3,32,256]{4,3,2,1,0:T(8,128)(2,1)}), bf16[16,2,3,32,256]{4,3,2,1,0:T(8,128)(2,1)S(1)}, u32[]{:S(2)}, u32[]{:S(2)}) %all-to-all-start.1) | async-done | bytes 1572896 | tf_op jit(solution)/shard_map/all_to_all | solution.py:286
  47.8 0.0 copy-done.3
  47.8 0.0 copy-done.5
  47.8 0.0 copy-done.6
  47.8 6.8 %far.1 = (bf16[16,2,3,32,256]{4,3,2,1,0:T(8,128)(2,1)S(1)}, f32[2,128,512]{2,1,0:T(8,128)S(1)}, f32[2,8,512]{2,1,0:T(8,128)S(1)}) custom-call(s32[96]{0:T(128)S(1)} %reshape.18.selection_ref, s32[1]{0:T(128)} %bitcast.position_ref, bf16[512,256]{1,0:T(8,128)(2,1)S(1)} %copy-done.6, bf16[512,256]{1,0:T(8,128)(2,1)S(1)} %copy-done.3, ...), custom_call_target="tpu_custom_call" | custom-call | flops 2013265920 | bytes 4194304 | tf_op jit(solution)/shard_map/far/pallas_call | solution.py:338
  54.6 27.1 %all_to_all.25.terms_ref = bf16[16,2,3,32,256]{4,3,2,1,0:T(8,128)(2,1)S(1)} all-to-all(bf16[16,2,3,32,256]{4,3,2,1,0:T(8,128)(2,1)S(1)} %get-tuple-element.12), channel_id=1, replica_groups=mesh['chain'=16,'heads'=16] {'chain'}, dimensions={0} | all-to-all | bytes 3145728 | tf_op jit(solution)/shard_map/all_to_all | solution.py:286
  81.7 0.0 copy-start
  81.7 0.0 copy-start.1
  81.7 0.0 copy-start.2
  81.7 1.8 %reduce.1 = bf16[16,2,32,256]{3,2,1,0:T(8,128)(2,1)} custom-call(s32[96]{0:T(128)S(1)} %reshape.18.selection_ref, bf16[16,2,3,32,256]{4,3,2,1,0:T(8,128)(2,1)S(1)} %all_to_all.25.terms_ref), custom_call_target="tpu_custom_call" | custom-call | bytes 4194304 | tf_op jit(solution)/shard_map/reduce/pallas_call | solution.py:369
  83.5 3.6 %all-to-all-start.3 = ((bf16[16,2,32,256]{3,2,1,0:T(8,128)(2,1)}), bf16[16,2,32,256]{3,2,1,0:T(8,128)(2,1)S(1)}, u32[]{:S(2)}, u32[]{:S(2)}) async-start(bf16[16,2,32,256]{3,2,1,0:T(8,128)(2,1)} %reduce.1), calls=%async_computation.3 | async-start | bytes 1048576 | tf_op jit(solution)/shard_map/all_to_all | solution.py:286
  87.1 0.0 copy-done
  87.1 0.0 copy-done.1
  87.1 0.0 copy-done.2
  87.1 1.9 %own_backward.1.own_ref = bf16[16,3,32,256]{3,2,1,0:T(8,128)(2,1)S(1)} custom-call(bf16[512,256]{1,0:T(8,128)(2,1)S(1)} %copy-done.2, bf16[512,256]{1,0:T(8,128)(2,1)S(1)} %copy-done, bf16[512,256]{1,0:T(8,128)(2,1)S(1)} %copy-done.1, bf16[512,256]{1,0:T(8,128)(2,1)S(1)} %copy-done.3, f32[2,128,512]{2,1,0:T(8,128)S(1)} %get-tuple-element.10.part_ref, ...), custom_call_target="tpu_custom_call" | custom-call | flops 671088640 | bytes 4194304 | tf_op jit(solution)/shard_map/own_backward/pallas_call | solution.py:360
  89.0 7.7 %all-to-all-done.3.others_ref = bf16[16,2,32,256]{3,2,1,0:T(8,128)(2,1)S(1)} async-done(((bf16[16,2,32,256]{3,2,1,0:T(8,128)(2,1)}), bf16[16,2,32,256]{3,2,1,0:T(8,128)(2,1)S(1)}, u32[]{:S(2)}, u32[]{:S(2)}) %all-to-all-start.3) | async-done | bytes 524320 | tf_op jit(solution)/shard_map/all_to_all | solution.py:286
  96.6 0.1 finish.1
  96.8 34.2 %all_to_all.26.parts_ref = bf16[16,3,32,256]{3,2,1,0:T(8,128)(2,1)S(1)} all-to-all(bf16[16,3,32,256]{3,2,1,0:T(8,128)(2,1)S(1)} %finish.1), channel_id=1, replica_groups=mesh['chain'=16,'heads'=16] {'heads'}, dimensions={0} | all-to-all | bytes 1572864 | tf_op jit(solution)/shard_map/all_to_all | solution.py:286
  130.9 1.3 lay.1
Async XLA Ops:
  0.6 9.5 %copy-start.7 = (s32[16,2,3]{0,1,2:T(2,128)S(1)}, s32[16,2,3]{0,1,2:T(2,128)}, u32[]{:S(2)}) copy-start(s32[16,2,3]{0,1,2:T(2,128)} %param.9) | copy-start | bytes 1156
  2.5 18.1 %all-to-all-start = ((bf16[16,2,32,256]{3,2,1,0:T(8,128)(2,1)}), bf16[16,2,32,256]{3,2,1,0:T(8,128)(2,1)S(1)}, u32[]{:S(2)}, u32[]{:S(2)}) async-start(bf16[16,2,32,256]{3,2,1,0:T(8,128)(2,1)} %stack.1), calls=%async_computation | async-start | bytes 1048576 | tf_op jit(solution)/shard_map/all_to_all | solution.py:286
  20.6 0.8 copy-start.4
  23.4 24.4 %copy-start.3 = (bf16[512,256]{1,0:T(8,128)(2,1)S(1)}, bf16[512,256]{1,0:T(8,128)(2,1)}, u32[]{:S(2)}) copy-start(bf16[512,256]{1,0:T(8,128)(2,1)} %grad_ref.5) | copy-start | bytes 786436
  23.4 24.4 %copy-start.5 = (f32[2,8,512]{2,1,0:T(8,128)S(1)}, f32[2,8,512]{2,1,0:T(8,128)}, u32[]{:S(2)}) copy-start(f32[2,8,512]{2,1,0:T(8,128)} %get-tuple-element.9.after_ref.own_stats_ref) | copy-start | bytes 98308
  23.4 24.4 %copy-start.6 = (bf16[512,256]{1,0:T(8,128)(2,1)S(1)}, bf16[512,256]{1,0:T(8,128)(2,1)}, u32[]{:S(2)}) copy-start(bf16[512,256]{1,0:T(8,128)(2,1)} %get-tuple-element.8.rows_ref) | copy-start | bytes 786436
  23.4 24.4 %all-to-all-start.1 = ((bf16[16,2,3,32,256]{4,3,2,1,0:T(8,128)(2,1)}), bf16[16,2,3,32,256]{4,3,2,1,0:T(8,128)(2,1)S(1)}, u32[]{:S(2)}, u32[]{:S(2)}) async-start(bf16[16,2,3,32,256]{4,3,2,1,0:T(8,128)(2,1)} %pick.1), calls=%async_computation.1 | async-start | bytes 3145728 | tf_op jit(solution)/shard_map/all_to_all | solution.py:286
  81.7 5.4 %copy-start = (bf16[512,256]{1,0:T(8,128)(2,1)S(1)}, bf16[512,256]{1,0:T(8,128)(2,1)}, u32[]{:S(2)}) copy-start(bf16[512,256]{1,0:T(8,128)(2,1)} %key_ref.3) | copy-start | bytes 786436
  81.7 5.4 %copy-start.1 = (bf16[512,256]{1,0:T(8,128)(2,1)S(1)}, bf16[512,256]{1,0:T(8,128)(2,1)}, u32[]{:S(2)}) copy-start(bf16[512,256]{1,0:T(8,128)(2,1)} %value_ref.3) | copy-start | bytes 786436
  81.7 5.4 %copy-start.2 = (bf16[512,256]{1,0:T(8,128)(2,1)S(1)}, bf16[512,256]{1,0:T(8,128)(2,1)}, u32[]{:S(2)}) copy-start(bf16[512,256]{1,0:T(8,128)(2,1)} %query_ref.3) | copy-start | bytes 786436
  83.5 13.1 %all-to-all-start.3 = ((bf16[16,2,32,256]{3,2,1,0:T(8,128)(2,1)}), bf16[16,2,32,256]{3,2,1,0:T(8,128)(2,1)S(1)}, u32[]{:S(2)}, u32[]{:S(2)}) async-start(bf16[16,2,32,256]{3,2,1,0:T(8,128)(2,1)} %reduce.1), calls=%async_computation.3 | async-start | bytes 1048576 | tf_op jit(solution)/shard_map/all_to_all | solution.py:286

commit v4 on v3

--- a/solution.py
+++ b/solution.py
@@ -51,34 +51,38 @@
         copy.wait()
 
 
-def pick_kernel(selection_ref, held_ref, after_ref, out_ref):
+def pick_kernel(selection_ref, held_ref, out_ref, filled_ref, sem):
     blocks, _, _, width = held_ref.shape
     heads = width // HEAD_DIM
+    copies = []
     for block in range(blocks):
+        filled_ref[block, :, 0] = held_ref[max(block - 1, 0)]
         for head in range(heads):
-            for slot in range(TOPK):
+            columns = head_columns(head)
+            for slot in range(1, TOPK):
                 source = selection_ref[(block * heads + head) * TOPK + slot]
-                out_ref[block, :, slot, :, head_columns(head)] = held_ref[
-                    source, :, :, head_columns(head)
-                ]
+                filled_ref[block, :, slot, :, columns] = held_ref[source, :, :, columns]
+        copies.append(
+            pltpu.make_async_copy(filled_ref.at[block], out_ref.at[block], sem.at[block])
+        )
+        copies[-1].start()
+    for copy in copies:
+        copy.wait()
 
 
 def reduce_kernel(selection_ref, terms_ref, out_ref, *total_refs):
     blocks, _, _, width = out_ref.shape
     heads = width // HEAD_DIM
-    for total_ref in total_refs:
-        total_ref[...] = jnp.zeros_like(total_ref)
-
-    def add(block, carry):
-        for slot in range(TOPK):
+    for head, total_ref in enumerate(total_refs):
+        total_ref[: blocks - 1] = terms_ref[1:, :, 0, :, head_columns(head)].astype(jnp.float32)
+        total_ref[blocks - 1] = jnp.zeros_like(total_ref[blocks - 1])
+    for block in range(blocks):
+        for slot in range(1, TOPK):
             for head, total_ref in enumerate(total_refs):
                 target = selection_ref[(block * heads + head) * TOPK + slot]
                 total_ref[target] += terms_ref[block, :, slot, :, head_columns(head)].astype(
                     jnp.float32
                 )
-        return carry
-
-    lax.fori_loop(0, blocks, add, 0, unroll=4)
     for head, total_ref in enumerate(total_refs):
         out_ref[:, :, :, head_columns(head)] = total_ref[...].astype(out_ref.dtype)
 
@@ -134,7 +138,10 @@
     stats_ref,
     grad_rows_ref,
     sem,
-    *scratch,
+    score_ref,
+    grad_prob_ref,
+    prob_ref,
+    grad_score_ref,
 ):
     heads, _, rows = own_stats_ref.shape
     chunks, _, _, chunk, _ = listed_ref.shape
@@ -142,32 +149,35 @@
     fetch = pltpu.make_async_copy(grad_ref, grad_rows_ref, sem)
     fetch.start()
 
-    def listed(which, slot, head):
-        return listed_ref[:, which, slot, :, head_columns(head)].reshape(rows, HEAD_DIM)
-
-    def softmax(head):
-        score_ref, grad_prob_ref, prob_ref, grad_score_ref = scratch[4 * head : 4 * head + 4]
+    def one_head(head, carry):
         columns = head_columns(head)
         live = [
             selection_ref[(block * heads + head) * TOPK + slot] < block for slot in range(TOPK)
         ]
-        for first in range(0, rows, TILE):
-            tile = pl.ds(first, TILE)
+
+        def listed(which, slot):
+            return listed_ref[:, which, slot, :, columns].reshape(rows, HEAD_DIM)
+
+        def scores_of(tile):
             top = jnp.full((1, TILE), MASKED, jnp.float32)
             for slot in range(TOPK):
-                scores = dot(listed(0, slot, head), rows_ref[tile, columns], 1, 1)
+                scores = dot(listed(0, slot), rows_ref[tile, columns], 1, 1)
                 score_ref[slot, :, tile] = scores
                 highest = jnp.max(scores, axis=0, keepdims=True)
                 top = jnp.maximum(top, jnp.where(live[slot], highest, MASKED))
-            if head == 0 and first == 0:
-                fetch.wait()
+            return top
+
+        tiles = [pl.ds(first, TILE) for first in range(0, rows, TILE)]
+        tops = [scores_of(tile) for tile in tiles]
+        pl.when(head == 0)(fetch.wait)
+        for tile, top in zip(tiles, tops):
             total = jnp.zeros_like(top)
             product = jnp.zeros_like(top)
             for slot in range(TOPK):
                 shift = jnp.where(live[slot], top, -MASKED)
                 raised = jnp.exp2((score_ref[slot, :, tile] - shift) * EXPONENT)
                 score_ref[slot, :, tile] = raised
-                grad_probs = dot(listed(1, slot, head), grad_rows_ref[tile, columns], 1, 1)
+                grad_probs = dot(listed(1, slot), grad_rows_ref[tile, columns], 1, 1)
                 grad_prob_ref[slot, :, tile] = grad_probs
                 total += jnp.sum(raised, axis=0, keepdims=True)
                 product += jnp.sum(raised * grad_probs, axis=0, keepdims=True)
@@ -186,10 +196,6 @@
                 grad_score_ref[slot, :, tile] = (
                     probability * (grad_prob_ref[slot, :, tile] - delta)
                 ).astype(jnp.bfloat16)
-
-    def gradients(head):
-        _, _, prob_ref, grad_score_ref = scratch[4 * head : 4 * head + 4]
-        columns = head_columns(head)
         query, grad = rows_ref[:, columns], grad_rows_ref[:, columns]
         shape = (chunks, chunk, HEAD_DIM)
         part = None
@@ -199,13 +205,12 @@
             terms_ref[:, 0, slot, :, columns] = grad_key.astype(jnp.bfloat16).reshape(shape)
             grad_value = dot(prob_ref[slot], grad, 1, 0)
             terms_ref[:, 1, slot, :, columns] = grad_value.astype(jnp.bfloat16).reshape(shape)
-            product = dot(listed(0, slot, head).T, grad_scores, 1, 0)
+            product = dot(listed(0, slot).T, grad_scores, 1, 0)
             part = product if part is None else part + product
         part_ref[head] = part
-
-    for head in range(heads):
-        softmax(head)
-        gradients(head)
+        return carry
+
+    lax.fori_loop(0, heads, one_head, 0)
 
 
 def own_backward_kernel(
@@ -330,10 +335,14 @@
     picked = call(
         pick_kernel,
         "pick",
-        [smem, vmem, anywhere],
-        vmem,
+        [smem, vmem],
+        anywhere,
         jax.ShapeDtypeStruct((chain, 2, TOPK, chunk, width), low),
-    )(listed, held, own_stats)
+        [
+            pltpu.VMEM((chain, 2, TOPK, chunk, width), low),
+            pltpu.SemaphoreType.DMA((chain,)),
+        ],
+    )(listed, held)
     slots = swap(picked, "chain")
     terms, part, stats = call(
         far_kernel,
@@ -345,15 +354,15 @@
             jax.ShapeDtypeStruct((heads, HEAD_DIM, rows), full),
             jax.ShapeDtypeStruct((heads, STATS, rows), full),
         ),
-        [pltpu.VMEM((rows, width), low), pltpu.SemaphoreType.DMA(())]
-        + [
+        [
+            pltpu.VMEM((rows, width), low),
+            pltpu.SemaphoreType.DMA(()),
             pltpu.VMEM((TOPK, rows, rows), full),
             pltpu.VMEM((TOPK, rows, rows), full),
             pltpu.VMEM((TOPK, rows, rows), low),
             pltpu.VMEM((TOPK, rows, rows), low),
-        ]
-        * heads,
-        limit=32,
+        ],
+        limit=24,
         slots=5 * TOPK,
     )(listed, position, own_rows, grad_output, slots, own_stats)
     returned = swap(terms, "chain")

time: 133 us -> 134 us (level)
  no operation moved by 1% of the time
where the time goes in v4:
time: 134 us; the launch traced here: 133 us
  blocking collectives  61.2 us (46%)
  waiting for transfers between devices  35.5 us (26%)
  Pallas kernels  18.8 us (14%)
  starting transfers between devices  15 us (11%)
  local copies, waits for them, and re-layouts  1.94 us (1%)
    all_to_all x2, blocking collectives, swap(): return lax.all_to_all(array, axis, split_axis=0, concat_axis=0, tiled=True)  61.2 us
    all_to_all x3, waiting for transfers between devices, swap(): return lax.all_to_all(array, axis, split_axis=0, concat_axis=0, tiled=True)  35.5 us
    all_to_all x3, starting transfers between devices, swap(): return lax.all_to_all(array, axis, split_axis=0, concat_axis=0, tiled=True)  15 us
    pallas_call x1, Pallas kernels, on_device(): call(far_kernel, 'far', [smem, smem, vmem, anywhere, vmem, vmem], (vmem,...  7.14 us
    pallas_call x1, Pallas kernels, on_device(): call(own_forward_kernel, 'own_forward', [anywhere] * 4, (vmem, vmem), (ja...  2.98 us
  transfers between devices with their start and end apart: 3, of which 3 were waited for; matrix products, arithmetic and copies ran while one was open for 0% of the time, Pallas kernels for 4%

profile of v4, /device:TPU:1, one launch (start us, length us, event | category | flops | bytes accessed | tf_op | source)
XLA Modules:
  0.0 133.2 jit_solution(10384101795748066632)
XLA Ops:
  0.6 0.0 copy-start.7
  0.6 1.8 %stack.1 = bf16[16,2,32,256]{3,2,1,0:T(8,128)(2,1)} custom-call(bf16[16,32,256]{2,1,0:T(8,128)(2,1)} %bitcast.3, bf16[16,32,256]{2,1,0:T(8,128)(2,1)} %bitcast.4), custom_call_target="tpu_custom_call" | custom-call | bytes 4194304 | tf_op jit(solution)/shard_map/stack/pallas_call | solution.py:308
  2.5 7.6 %all-to-all-start = ((bf16[16,2,32,256]{3,2,1,0:T(8,128)(2,1)}), bf16[16,2,32,256]{3,2,1,0:T(8,128)(2,1)S(1)}, u32[]{:S(2)}, u32[]{:S(2)}) async-start(bf16[16,2,32,256]{3,2,1,0:T(8,128)(2,1)} %stack.1), calls=%async_computation | async-start | bytes 1048576 | tf_op jit(solution)/shard_map/all_to_all | solution.py:291
  10.1 0.0 copy-done.7
  10.1 0.1 copy.9
  10.2 0.1 reshape.18.selection_ref
  10.3 10.3 %all-to-all-done.held_ref = bf16[16,2,32,256]{3,2,1,0:T(8,128)(2,1)S(1)} async-done(((bf16[16,2,32,256]{3,2,1,0:T(8,128)(2,1)}), bf16[16,2,32,256]{3,2,1,0:T(8,128)(2,1)S(1)}, u32[]{:S(2)}, u32[]{:S(2)}) %all-to-all-start) | async-done | bytes 524320 | tf_op jit(solution)/shard_map/all_to_all | solution.py:291
  20.6 1.9 %pick.1 = bf16[16,2,3,32,256]{4,3,2,1,0:T(8,128)(2,1)} custom-call(s32[96]{0:T(128)S(1)} %reshape.18.selection_ref, bf16[16,2,32,256]{3,2,1,0:T(8,128)(2,1)S(1)} %all-to-all-done.held_ref), custom_call_target="tpu_custom_call" | custom-call | bytes 4194304 | tf_op jit(solution)/shard_map/pick/pallas_call | solution.py:335
  22.5 0.0 copy-start.3
  22.5 3.9 %all-to-all-start.1 = ((bf16[16,2,3,32,256]{4,3,2,1,0:T(8,128)(2,1)}), bf16[16,2,3,32,256]{4,3,2,1,0:T(8,128)(2,1)S(1)}, u32[]{:S(2)}, u32[]{:S(2)}) async-start(bf16[16,2,3,32,256]{4,3,2,1,0:T(8,128)(2,1)} %pick.1), calls=%async_computation.1 | async-start | bytes 3145728 | tf_op jit(solution)/shard_map/all_to_all | solution.py:291
  26.3 3.0 %own_forward.1 = (bf16[512,256]{1,0:T(8,128)(2,1)}, f32[2,8,512]{2,1,0:T(8,128)}) custom-call(bf16[512,256]{1,0:T(8,128)(2,1)} %query_ref.3, bf16[512,256]{1,0:T(8,128)(2,1)} %key_ref.3, bf16[512,256]{1,0:T(8,128)(2,1)} %value_ref.3, bf16[512,256]{1,0:T(8,128)(2,1)} %grad_ref.5), custom_call_target="tpu_custom_call" | custom-call | flops 268435456 | bytes 4194304 | tf_op jit(solution)/shard_map/own_forward/pallas_call | solution.py:322
  29.3 17.5 %all-to-all-done.1.listed_ref = bf16[16,2,3,32,256]{4,3,2,1,0:T(8,128)(2,1)S(1)} async-done(((bf16[16,2,3,32,256]{4,3,2,1,0:T(8,128)(2,1)}), bf16[16,2,3,32,256]{4,3,2,1,0:T(8,128)(2,1)S(1)}, u32[]{:S(2)}, u32[]{:S(2)}) %all-to-all-start.1) | async-done | bytes 1572896 | tf_op jit(solution)/shard_map/all_to_all | solution.py:291
  46.9 0.0 copy-done.3
  46.9 0.0 copy-start.4
  46.9 0.9 copy-done.4
  47.8 0.0 copy-start.5
  47.8 0.8 copy-done.5
  48.6 7.1 %far.1 = (bf16[16,2,3,32,256]{4,3,2,1,0:T(8,128)(2,1)S(1)}, f32[2,128,512]{2,1,0:T(8,128)S(1)}, f32[2,8,512]{2,1,0:T(8,128)S(1)}) custom-call(s32[96]{0:T(128)S(1)} %reshape.18.selection_ref, s32[1]{0:T(128)} %bitcast.position_ref, bf16[512,256]{1,0:T(8,128)(2,1)S(1)} %copy-done.4, bf16[512,256]{1,0:T(8,128)(2,1)S(1)} %copy-done.3, ...), custom_call_target="tpu_custom_call" | custom-call | flops 2013265920 | bytes 4194304 | tf_op jit(solution)/shard_map/far/pallas_call | solution.py:347
  55.7 27.1 %all_to_all.25.terms_ref = bf16[16,2,3,32,256]{4,3,2,1,0:T(8,128)(2,1)S(1)} all-to-all(bf16[16,2,3,32,256]{4,3,2,1,0:T(8,128)(2,1)S(1)} %get-tuple-element.12), channel_id=1, replica_groups=mesh['chain'=16,'heads'=16] {'chain'}, dimensions={0} | all-to-all | bytes 3145728 | tf_op jit(solution)/shard_map/all_to_all | solution.py:291
  82.8 0.0 copy-start
  82.8 0.0 copy-start.1
  82.8 0.0 copy-start.2
  82.8 0.0 copy-start.6
  82.8 1.7 %reduce.1 = bf16[16,2,32,256]{3,2,1,0:T(8,128)(2,1)} custom-call(s32[96]{0:T(128)S(1)} %reshape.18.selection_ref, bf16[16,2,3,32,256]{4,3,2,1,0:T(8,128)(2,1)S(1)} %all_to_all.25.terms_ref), custom_call_target="tpu_custom_call" | custom-call | bytes 4194304 | tf_op jit(solution)/shard_map/reduce/pallas_call | solution.py:378
  84.5 3.6 %all-to-all-start.3 = ((bf16[16,2,32,256]{3,2,1,0:T(8,128)(2,1)}), bf16[16,2,32,256]{3,2,1,0:T(8,128)(2,1)S(1)}, u32[]{:S(2)}, u32[]{:S(2)}) async-start(bf16[16,2,32,256]{3,2,1,0:T(8,128)(2,1)} %reduce.1), calls=%async_computation.3 | async-start | bytes 1048576 | tf_op jit(solution)/shard_map/all_to_all | solution.py:291
  88.1 0.0 copy-done
  88.1 0.0 copy-done.1
  88.1 0.0 copy-done.2
  88.1 0.0 copy-done.6
  88.1 1.9 %own_backward.1.own_ref = bf16[16,3,32,256]{3,2,1,0:T(8,128)(2,1)S(1)} custom-call(bf16[512,256]{1,0:T(8,128)(2,1)S(1)} %copy-done.2, bf16[512,256]{1,0:T(8,128)(2,1)S(1)} %copy-done, bf16[512,256]{1,0:T(8,128)(2,1)S(1)} %copy-done.1, bf16[512,256]{1,0:T(8,128)(2,1)S(1)} %copy-done.3, f32[2,128,512]{2,1,0:T(8,128)S(1)} %get-tuple-element.10.part_ref, ...), custom_call_target="tpu_custom_call" | custom-call | flops 671088640 | bytes 4194304 | tf_op jit(solution)/shard_map/own_backward/pallas_call | solution.py:369
  90.0 7.7 %all-to-all-done.3.others_ref = bf16[16,2,32,256]{3,2,1,0:T(8,128)(2,1)S(1)} async-done(((bf16[16,2,32,256]{3,2,1,0:T(8,128)(2,1)}), bf16[16,2,32,256]{3,2,1,0:T(8,128)(2,1)S(1)}, u32[]{:S(2)}, u32[]{:S(2)}) %all-to-all-start.3) | async-done | bytes 524320 | tf_op jit(solution)/shard_map/all_to_all | solution.py:291
  97.7 0.1 finish.1
  97.8 34.2 %all_to_all.26.parts_ref = bf16[16,3,32,256]{3,2,1,0:T(8,128)(2,1)S(1)} all-to-all(bf16[16,3,32,256]{3,2,1,0:T(8,128)(2,1)S(1)} %finish.1), channel_id=1, replica_groups=mesh['chain'=16,'heads'=16] {'heads'}, dimensions={0} | all-to-all | bytes 1572864 | tf_op jit(solution)/shard_map/all_to_all | solution.py:291
  132.0 1.3 lay.1
Async XLA Ops:
  0.6 9.5 %copy-start.7 = (s32[16,2,3]{0,1,2:T(2,128)S(1)}, s32[16,2,3]{0,1,2:T(2,128)}, u32[]{:S(2)}) copy-start(s32[16,2,3]{0,1,2:T(2,128)} %param.9) | copy-start | bytes 1156
  2.5 18.1 %all-to-all-start = ((bf16[16,2,32,256]{3,2,1,0:T(8,128)(2,1)}), bf16[16,2,32,256]{3,2,1,0:T(8,128)(2,1)S(1)}, u32[]{:S(2)}, u32[]{:S(2)}) async-start(bf16[16,2,32,256]{3,2,1,0:T(8,128)(2,1)} %stack.1), calls=%async_computation | async-start | bytes 1048576 | tf_op jit(solution)/shard_map/all_to_all | solution.py:291
  22.5 24.4 %copy-start.3 = (bf16[512,256]{1,0:T(8,128)(2,1)S(1)}, bf16[512,256]{1,0:T(8,128)(2,1)}, u32[]{:S(2)}) copy-start(bf16[512,256]{1,0:T(8,128)(2,1)} %grad_ref.5) | copy-start | bytes 786436
  22.5 24.4 %all-to-all-start.1 = ((bf16[16,2,3,32,256]{4,3,2,1,0:T(8,128)(2,1)}), bf16[16,2,3,32,256]{4,3,2,1,0:T(8,128)(2,1)S(1)}, u32[]{:S(2)}, u32[]{:S(2)}) async-start(bf16[16,2,3,32,256]{4,3,2,1,0:T(8,128)(2,1)} %pick.1), calls=%async_computation.1 | async-start | bytes 3145728 | tf_op jit(solution)/shard_map/all_to_all | solution.py:291
  46.9 1.0 copy-start.4
  47.8 0.8 copy-start.5
  82.8 5.3 %copy-start = (bf16[512,256]{1,0:T(8,128)(2,1)S(1)}, bf16[512,256]{1,0:T(8,128)(2,1)}, u32[]{:S(2)}) copy-start(bf16[512,256]{1,0:T(8,128)(2,1)} %key_ref.3) | copy-start | bytes 786436
  82.8 5.3 %copy-start.1 = (bf16[512,256]{1,0:T(8,128)(2,1)S(1)}, bf16[512,256]{1,0:T(8,128)(2,1)}, u32[]{:S(2)}) copy-start(bf16[512,256]{1,0:T(8,128)(2,1)} %value_ref.3) | copy-start | bytes 786436
  82.8 5.3 %copy-start.2 = (bf16[512,256]{1,0:T(8,128)(2,1)S(1)}, bf16[512,256]{1,0:T(8,128)(2,1)}, u32[]{:S(2)}) copy-start(bf16[512,256]{1,0:T(8,128)(2,1)} %query_ref.3) | copy-start | bytes 786436
  82.8 5.3 %copy-start.6 = (f32[2,8,512]{2,1,0:T(8,128)S(1)}, f32[2,8,512]{2,1,0:T(8,128)}, u32[]{:S(2)}) copy-start(f32[2,8,512]{2,1,0:T(8,128)} %get-tuple-element.9.own_stats_ref) | copy-start | bytes 98308
  84.5 13.1 %all-to-all-start.3 = ((bf16[16,2,32,256]{3,2,1,0:T(8,128)(2,1)}), bf16[16,2,32,256]{3,2,1,0:T(8,128)(2,1)S(1)}, u32[]{:S(2)}, u32[]{:S(2)}) async-start(bf16[16,2,32,256]{3,2,1,0:T(8,128)(2,1)} %reduce.1), calls=%async_computation.3 | async-start | bytes 1048576 | tf_op jit(solution)/shard_map/all_to_all | solution.py:291

commit v5 on v4

--- a/solution.py
+++ b/solution.py
@@ -94,30 +94,44 @@
 
 
 def own_forward_kernel(
-    query_ref, key_ref, value_ref, grad_ref, rows_ref, stats_ref, held_ref, sem
+    selection_ref,
+    query_ref,
+    key_ref,
+    value_ref,
+    grad_ref,
+    listed_ref,
+    turned_ref,
+    stats_ref,
+    held_ref,
+    sem,
 ):
     heads, _, rows = stats_ref.shape
-    targets = (rows_ref, held_ref.at[0], held_ref.at[1], held_ref.at[2])
     copies = [
-        pltpu.make_async_copy(source, target, sem.at[index])
-        for index, (source, target) in enumerate(
-            zip((query_ref, key_ref, value_ref, grad_ref), targets)
-        )
+        pltpu.make_async_copy(source, held_ref.at[index], sem.at[index])
+        for index, source in enumerate((query_ref, grad_ref, key_ref, value_ref))
     ]
     for copy in copies:
         copy.start()
+
+    def hand_on(index, carry):
+        listed_ref[index] = selection_ref[index]
+        return carry
+
+    lax.fori_loop(0, selection_ref.shape[0], hand_on, 0)
     for copy in copies:
         copy.wait()
 
     def one_head(head, carry):
         columns = head_columns(head)
-        key, value = held_ref[0, :, columns], held_ref[1, :, columns]
+        key, value = held_ref[2, :, columns], held_ref[3, :, columns]
+        for index in range(2):
+            turned_ref[index, head] = held_ref[index, :, columns].T
         for first in range(0, rows, TILE):
             tile = pl.ds(first, TILE)
-            scores = causal(dot(key, rows_ref[tile, columns], 1, 1), first)
+            scores = causal(dot(key, turned_ref[0, head, :, tile], 1, 0), first)
             top = jnp.max(scores, axis=0, keepdims=True)
             raised = jnp.exp2((scores - top) * EXPONENT)
-            product = raised * dot(value, held_ref[2, tile, columns], 1, 1)
+            product = raised * dot(value, turned_ref[1, head, :, tile], 1, 0)
             stats_ref[head, 0:1, tile] = top
             stats_ref[head, 1:2, tile] = jnp.sum(raised, axis=0, keepdims=True)
             stats_ref[head, 2:3, tile] = jnp.sum(product, axis=0, keepdims=True)
@@ -129,55 +143,51 @@
 def far_kernel(
     selection_ref,
     position_ref,
-    rows_ref,
+    turned_ref,
+    query_ref,
     grad_ref,
     listed_ref,
     own_stats_ref,
     terms_ref,
     part_ref,
     stats_ref,
-    grad_rows_ref,
+    rows_ref,
     sem,
-    score_ref,
-    grad_prob_ref,
-    prob_ref,
-    grad_score_ref,
+    *scratch,
 ):
     heads, _, rows = own_stats_ref.shape
     chunks, _, _, chunk, _ = listed_ref.shape
     block = position_ref[0]
-    fetch = pltpu.make_async_copy(grad_ref, grad_rows_ref, sem)
-    fetch.start()
-
-    def one_head(head, carry):
-        columns = head_columns(head)
+    copies = [
+        pltpu.make_async_copy(source, rows_ref.at[index], sem.at[index])
+        for index, source in enumerate((query_ref, grad_ref))
+    ]
+    for copy in copies:
+        copy.start()
+
+    def listed(which, slot, head):
+        return listed_ref[:, which, slot, :, head_columns(head)].reshape(rows, HEAD_DIM)
+
+    def softmax(head):
+        score_ref, grad_prob_ref, prob_ref, grad_score_ref = scratch[4 * head : 4 * head + 4]
         live = [
             selection_ref[(block * heads + head) * TOPK + slot] < block for slot in range(TOPK)
         ]
-
-        def listed(which, slot):
-            return listed_ref[:, which, slot, :, columns].reshape(rows, HEAD_DIM)
-
-        def scores_of(tile):
+        for first in range(0, rows, TILE):
+            tile = pl.ds(first, TILE)
             top = jnp.full((1, TILE), MASKED, jnp.float32)
             for slot in range(TOPK):
-                scores = dot(listed(0, slot), rows_ref[tile, columns], 1, 1)
+                scores = dot(listed(0, slot, head), turned_ref[0, head, :, tile], 1, 0)
                 score_ref[slot, :, tile] = scores
                 highest = jnp.max(scores, axis=0, keepdims=True)
                 top = jnp.maximum(top, jnp.where(live[slot], highest, MASKED))
-            return top
-
-        tiles = [pl.ds(first, TILE) for first in range(0, rows, TILE)]
-        tops = [scores_of(tile) for tile in tiles]
-        pl.when(head == 0)(fetch.wait)
-        for tile, top in zip(tiles, tops):
             total = jnp.zeros_like(top)
             product = jnp.zeros_like(top)
             for slot in range(TOPK):
                 shift = jnp.where(live[slot], top, -MASKED)
                 raised = jnp.exp2((score_ref[slot, :, tile] - shift) * EXPONENT)
                 score_ref[slot, :, tile] = raised
-                grad_probs = dot(listed(1, slot), grad_rows_ref[tile, columns], 1, 1)
+                grad_probs = dot(listed(1, slot, head), turned_ref[1, head, :, tile], 1, 0)
                 grad_prob_ref[slot, :, tile] = grad_probs
                 total += jnp.sum(raised, axis=0, keepdims=True)
                 product += jnp.sum(raised * grad_probs, axis=0, keepdims=True)
@@ -196,7 +206,11 @@
                 grad_score_ref[slot, :, tile] = (
                     probability * (grad_prob_ref[slot, :, tile] - delta)
                 ).astype(jnp.bfloat16)
-        query, grad = rows_ref[:, columns], grad_rows_ref[:, columns]
+
+    def gradients(head):
+        _, _, prob_ref, grad_score_ref = scratch[4 * head : 4 * head + 4]
+        columns = head_columns(head)
+        query, grad = rows_ref[0, :, columns], rows_ref[1, :, columns]
         shape = (chunks, chunk, HEAD_DIM)
         part = None
         for slot in range(TOPK):
@@ -205,12 +219,16 @@
             terms_ref[:, 0, slot, :, columns] = grad_key.astype(jnp.bfloat16).reshape(shape)
             grad_value = dot(prob_ref[slot], grad, 1, 0)
             terms_ref[:, 1, slot, :, columns] = grad_value.astype(jnp.bfloat16).reshape(shape)
-            product = dot(listed(0, slot).T, grad_scores, 1, 0)
+            product = dot(listed(0, slot, head).T, grad_scores, 1, 0)
             part = product if part is None else part + product
         part_ref[head] = part
-        return carry
-
-    lax.fori_loop(0, heads, one_head, 0)
+
+    for head in range(heads):
+        softmax(head)
+        if head == 0:
+            for copy in copies:
+                copy.wait()
+        gradients(head)
 
 
 def own_backward_kernel(
@@ -319,19 +337,20 @@
         limit=59,
     )(key_input.reshape(chain, chunk, width), value_input.reshape(chain, chunk, width))
     held = swap(pair, "chain")
-    own_rows, own_stats = call(
+    listed, turned, own_stats = call(
         own_forward_kernel,
         "own_forward",
-        [anywhere] * 4,
-        (vmem, vmem),
+        [smem] + [anywhere] * 4,
+        (smem, vmem, vmem),
         (
-            jax.ShapeDtypeStruct((rows, width), low),
+            jax.ShapeDtypeStruct(listed.shape, jnp.int32),
+            jax.ShapeDtypeStruct((2, heads, HEAD_DIM, rows), low),
             jax.ShapeDtypeStruct((heads, STATS, rows), full),
         ),
-        [pltpu.VMEM((3, rows, width), low), pltpu.SemaphoreType.DMA((4,))],
+        [pltpu.VMEM((4, rows, width), low), pltpu.SemaphoreType.DMA((4,))],
         limit=58,
         slots=2,
-    )(query_input, key_input, value_input, grad_output)
+    )(listed, query_input, key_input, value_input, grad_output)
     picked = call(
         pick_kernel,
         "pick",
@@ -347,24 +366,24 @@
     terms, part, stats = call(
         far_kernel,
         "far",
-        [smem, smem, vmem, anywhere, vmem, vmem],
+        [smem, smem, vmem, anywhere, anywhere, vmem, vmem],
         (vmem, vmem, vmem),
         (
             jax.ShapeDtypeStruct((chain, 2, TOPK, chunk, width), low),
             jax.ShapeDtypeStruct((heads, HEAD_DIM, rows), full),
             jax.ShapeDtypeStruct((heads, STATS, rows), full),
         ),
-        [
-            pltpu.VMEM((rows, width), low),
-            pltpu.SemaphoreType.DMA(()),
+        [pltpu.VMEM((2, rows, width), low), pltpu.SemaphoreType.DMA((2,))]
+        + [
             pltpu.VMEM((TOPK, rows, rows), full),
             pltpu.VMEM((TOPK, rows, rows), full),
             pltpu.VMEM((TOPK, rows, rows), low),
             pltpu.VMEM((TOPK, rows, rows), low),
-        ],
-        limit=24,
+        ]
+        * heads,
+        limit=32,
         slots=5 * TOPK,
-    )(listed, position, own_rows, grad_output, slots, own_stats)
+    )(listed, position, turned, query_input, grad_output, slots, own_stats)
     returned = swap(terms, "chain")
     own = call(
         own_backward_kernel,

time: 134 us -> 132 us (0.985)
  transfers between devices with their start and end apart: 3 -> 3, of which waited for: 3 -> 3; matrix products, arithmetic and copies ran while one was open for 0% -> 1% of each run, Pallas kernels for 4% -> 4%
where the time goes in v5:
time: 132 us
  blocking collectives  61.2 us (46%)
  waiting for transfers between devices  34.3 us (26%)
  Pallas kernels  19.2 us (15%)
  starting transfers between devices  15 us (11%)
  local copies, waits for them, and re-layouts  1.42 us (1%)
    all_to_all x2, blocking collectives, swap(): return lax.all_to_all(array, axis, split_axis=0, concat_axis=0, tiled=True)  61.2 us
    all_to_all x3, waiting for transfers between devices, swap(): return lax.all_to_all(array, axis, split_axis=0, concat_axis=0, tiled=True)  34.3 us
    all_to_all x3, starting transfers between devices, swap(): return lax.all_to_all(array, axis, split_axis=0, concat_axis=0, tiled=True)  15 us
    pallas_call x1, Pallas kernels, on_device(): call(far_kernel, 'far', [smem, smem, vmem, anywhere, anywhere, vmem, vmem...  6.8 us
    pallas_call x1, Pallas kernels, on_device(): call(own_forward_kernel, 'own_forward', [smem] + [anywhere] * 4, (smem, v...  3.71 us
  transfers between devices with their start and end apart: 3, of which 3 were waited for; matrix products, arithmetic and copies ran while one was open for 1% of the time, Pallas kernels for 4%

profile of v5, /device:TPU:1, one launch (start us, length us, event | category | flops | bytes accessed | tf_op | source)
XLA Modules:
  0.0 131.9 jit_solution(2881554764387348077)
XLA Ops:
  0.6 0.0 copy-start.8
  0.6 1.8 %stack.1 = bf16[16,2,32,256]{3,2,1,0:T(8,128)(2,1)} custom-call(bf16[16,32,256]{2,1,0:T(8,128)(2,1)} %bitcast.3, bf16[16,32,256]{2,1,0:T(8,128)(2,1)} %bitcast.4), custom_call_target="tpu_custom_call" | custom-call | bytes 4194304 | tf_op jit(solution)/shard_map/stack/pallas_call | solution.py:326
  2.5 7.6 %all-to-all-start = ((bf16[16,2,32,256]{3,2,1,0:T(8,128)(2,1)}), bf16[16,2,32,256]{3,2,1,0:T(8,128)(2,1)S(1)}, u32[]{:S(2)}, u32[]{:S(2)}) async-start(bf16[16,2,32,256]{3,2,1,0:T(8,128)(2,1)} %stack.1), calls=%async_computation | async-start | bytes 1048576 | tf_op jit(solution)/shard_map/all_to_all | solution.py:309
  10.1 0.0 copy-done.8
  10.1 0.1 copy.9
  10.2 0.6 reshape.18.selection_ref
  10.8 3.7 %own_forward.1 = (s32[96]{0:T(128)}, bf16[2,2,128,512]{3,2,1,0:T(8,128)(2,1)}, f32[2,8,512]{2,1,0:T(8,128)}) custom-call(s32[96]{0:T(128)} %reshape.18.selection_ref, bf16[512,256]{1,0:T(8,128)(2,1)} %query_ref.5, bf16[512,256]{1,0:T(8,128)(2,1)} %key_ref.3, bf16[512,256]{1,0:T(8,128)(2,1)} %value_ref.3, bf16[512,256]{1,0:T(8,128)(2,1)} %grad_ref.5), custom_call_target="tpu_custom_call" | custom-call | flops 268435456 | bytes 4194304 | tf_op jit(solution)/shard_map/own_forward/pallas_call | solution.py:340
  14.5 6.1 %all-to-all-done.held_ref = bf16[16,2,32,256]{3,2,1,0:T(8,128)(2,1)S(1)} async-done(((bf16[16,2,32,256]{3,2,1,0:T(8,128)(2,1)}), bf16[16,2,32,256]{3,2,1,0:T(8,128)(2,1)S(1)}, u32[]{:S(2)}, u32[]{:S(2)}) %all-to-all-start) | async-done | bytes 524320 | tf_op jit(solution)/shard_map/all_to_all | solution.py:309
  20.6 0.0 copy-start.4
  20.6 0.7 copy-done.4
  21.2 1.9 %pick.1 = bf16[16,2,3,32,256]{4,3,2,1,0:T(8,128)(2,1)} custom-call(s32[96]{0:T(128)S(1)} %copy-done.4, bf16[16,2,32,256]{3,2,1,0:T(8,128)(2,1)S(1)} %all-to-all-done.held_ref), custom_call_target="tpu_custom_call" | custom-call | bytes 4194304 | tf_op jit(solution)/shard_map/pick/pallas_call | solution.py:354
  23.1 0.0 copy-start.2
  23.1 0.0 copy-start.3
  23.2 0.0 copy-start.5
  23.2 0.0 copy-start.6
  23.2 0.0 copy-start.7
  23.2 3.9 %all-to-all-start.1 = ((bf16[16,2,3,32,256]{4,3,2,1,0:T(8,128)(2,1)}), bf16[16,2,3,32,256]{4,3,2,1,0:T(8,128)(2,1)S(1)}, u32[]{:S(2)}, u32[]{:S(2)}) async-start(bf16[16,2,3,32,256]{4,3,2,1,0:T(8,128)(2,1)} %pick.1), calls=%async_computation.1 | async-start | bytes 3145728 | tf_op jit(solution)/shard_map/all_to_all | solution.py:309
  27.1 20.5 %all-to-all-done.1.listed_ref = bf16[16,2,3,32,256]{4,3,2,1,0:T(8,128)(2,1)S(1)} async-done(((bf16[16,2,3,32,256]{4,3,2,1,0:T(8,128)(2,1)}), bf16[16,2,3,32,256]{4,3,2,1,0:T(8,128)(2,1)S(1)}, u32[]{:S(2)}, u32[]{:S(2)}) %all-to-all-start.1) | async-done | bytes 1572896 | tf_op jit(solution)/shard_map/all_to_all | solution.py:309
  47.6 0.0 copy-done.2
  47.6 0.0 copy-done.3
  47.6 0.0 copy-done.5
  47.6 0.0 copy-done.6
  47.6 0.0 copy-done.7
  47.6 6.8 %far.1 = (bf16[16,2,3,32,256]{4,3,2,1,0:T(8,128)(2,1)S(1)}, f32[2,128,512]{2,1,0:T(8,128)S(1)}, f32[2,8,512]{2,1,0:T(8,128)S(1)}) custom-call(s32[96]{0:T(128)S(1)} %copy-done.5, s32[1]{0:T(128)} %bitcast.position_ref, bf16[2,2,128,512]{3,2,1,0:T(8,128)(2,1)S(1)} %copy-done.6, bf16[512,256]{1,0:T(8,128)(2,1)S(1)} %copy-done.2, ...), custom_call_target="tpu_custom_call" | custom-call | flops 2013265920 | bytes 4194304 | tf_op jit(solution)/shard_map/far/pallas_call | solution.py:366
  54.4 27.1 %all_to_all.25.terms_ref = bf16[16,2,3,32,256]{4,3,2,1,0:T(8,128)(2,1)S(1)} all-to-all(bf16[16,2,3,32,256]{4,3,2,1,0:T(8,128)(2,1)S(1)} %get-tuple-element.14), channel_id=1, replica_groups=mesh['chain'=16,'heads'=16] {'chain'}, dimensions={0} | all-to-all | bytes 3145728 | tf_op jit(solution)/shard_map/all_to_all | solution.py:309
  81.5 0.0 copy-start
  81.5 0.0 copy-start.1
  81.5 1.7 %reduce.1 = bf16[16,2,32,256]{3,2,1,0:T(8,128)(2,1)} custom-call(s32[96]{0:T(128)S(1)} %copy-done.5, bf16[16,2,3,32,256]{4,3,2,1,0:T(8,128)(2,1)S(1)} %all_to_all.25.terms_ref), custom_call_target="tpu_custom_call" | custom-call | bytes 4194304 | tf_op jit(solution)/shard_map/reduce/pallas_call | solution.py:397
  83.2 3.6 %all-to-all-start.3 = ((bf16[16,2,32,256]{3,2,1,0:T(8,128)(2,1)}), bf16[16,2,32,256]{3,2,1,0:T(8,128)(2,1)S(1)}, u32[]{:S(2)}, u32[]{:S(2)}) async-start(bf16[16,2,32,256]{3,2,1,0:T(8,128)(2,1)} %reduce.1), calls=%async_computation.3 | async-start | bytes 1048576 | tf_op jit(solution)/shard_map/all_to_all | solution.py:309
  86.8 0.0 copy-done
  86.8 0.0 copy-done.1
  86.8 1.9 %own_backward.1.own_ref = bf16[16,3,32,256]{3,2,1,0:T(8,128)(2,1)S(1)} custom-call(bf16[512,256]{1,0:T(8,128)(2,1)S(1)} %copy-done.2, bf16[512,256]{1,0:T(8,128)(2,1)S(1)} %copy-done, bf16[512,256]{1,0:T(8,128)(2,1)S(1)} %copy-done.1, bf16[512,256]{1,0:T(8,128)(2,1)S(1)} %copy-done.3, f32[2,128,512]{2,1,0:T(8,128)S(1)} %get-tuple-element.12.part_ref, ...), custom_call_target="tpu_custom_call" | custom-call | flops 671088640 | bytes 4194304 | tf_op jit(solution)/shard_map/own_backward/pallas_call | solution.py:388
  88.7 7.7 %all-to-all-done.3.others_ref = bf16[16,2,32,256]{3,2,1,0:T(8,128)(2,1)S(1)} async-done(((bf16[16,2,32,256]{3,2,1,0:T(8,128)(2,1)}), bf16[16,2,32,256]{3,2,1,0:T(8,128)(2,1)S(1)}, u32[]{:S(2)}, u32[]{:S(2)}) %all-to-all-start.3) | async-done | bytes 524320 | tf_op jit(solution)/shard_map/all_to_all | solution.py:309
  96.3 0.1 finish.1
  96.5 34.1 %all_to_all.26.parts_ref = bf16[16,3,32,256]{3,2,1,0:T(8,128)(2,1)S(1)} all-to-all(bf16[16,3,32,256]{3,2,1,0:T(8,128)(2,1)S(1)} %finish.1), channel_id=1, replica_groups=mesh['chain'=16,'heads'=16] {'heads'}, dimensions={0} | all-to-all | bytes 1572864 | tf_op jit(solution)/shard_map/all_to_all | solution.py:309
  130.6 1.3 lay.1
Async XLA Ops:
  0.6 9.5 %copy-start.8 = (s32[16,2,3]{0,1,2:T(2,128)S(1)}, s32[16,2,3]{0,1,2:T(2,128)}, u32[]{:S(2)}) copy-start(s32[16,2,3]{0,1,2:T(2,128)} %param.9) | copy-start | bytes 1156
  2.5 18.1 %all-to-all-start = ((bf16[16,2,32,256]{3,2,1,0:T(8,128)(2,1)}), bf16[16,2,32,256]{3,2,1,0:T(8,128)(2,1)S(1)}, u32[]{:S(2)}, u32[]{:S(2)}) async-start(bf16[16,2,32,256]{3,2,1,0:T(8,128)(2,1)} %stack.1), calls=%async_computation | async-start | bytes 1048576 | tf_op jit(solution)/shard_map/all_to_all | solution.py:309
  20.6 0.7 copy-start.4
  23.1 24.5 %copy-start.2 = (bf16[512,256]{1,0:T(8,128)(2,1)S(1)}, bf16[512,256]{1,0:T(8,128)(2,1)}, u32[]{:S(2)}) copy-start(bf16[512,256]{1,0:T(8,128)(2,1)} %query_ref.5) | copy-start | bytes 786436
  23.1 24.4 %copy-start.3 = (bf16[512,256]{1,0:T(8,128)(2,1)S(1)}, bf16[512,256]{1,0:T(8,128)(2,1)}, u32[]{:S(2)}) copy-start(bf16[512,256]{1,0:T(8,128)(2,1)} %grad_ref.5) | copy-start | bytes 786436
  23.2 24.4 %copy-start.5 = (s32[96]{0:T(128)S(1)}, s32[96]{0:T(128)}, u32[]{:S(2)}) copy-start(s32[96]{0:T(128)} %get-tuple-element.9.selection_ref) | copy-start | bytes 1156
  23.2 24.4 %copy-start.6 = (bf16[2,2,128,512]{3,2,1,0:T(8,128)(2,1)S(1)}, bf16[2,2,128,512]{3,2,1,0:T(8,128)(2,1)}, u32[]{:S(2)}) copy-start(bf16[2,2,128,512]{3,2,1,0:T(8,128)(2,1)} %get-tuple-element.10.turned_ref) | copy-start | bytes 1572868
  23.2 24.4 %copy-start.7 = (f32[2,8,512]{2,1,0:T(8,128)S(1)}, f32[2,8,512]{2,1,0:T(8,128)}, u32[]{:S(2)}) copy-start(f32[2,8,512]{2,1,0:T(8,128)} %get-tuple-element.11.own_stats_ref) | copy-start | bytes 98308
  23.2 24.4 %all-to-all-start.1 = ((bf16[16,2,3,32,256]{4,3,2,1,0:T(8,128)(2,1)}), bf16[16,2,3,32,256]{4,3,2,1,0:T(8,128)(2,1)S(1)}, u32[]{:S(2)}, u32[]{:S(2)}) async-start(bf16[16,2,3,32,256]{4,3,2,1,0:T(8,128)(2,1)} %pick.1), calls=%async_computation.1 | async-start | bytes 3145728 | tf_op jit(solution)/shard_map/all_to_all | solution.py:309
  81.5 5.3 %copy-start = (bf16[512,256]{1,0:T(8,128)(2,1)S(1)}, bf16[512,256]{1,0:T(8,128)(2,1)}, u32[]{:S(2)}) copy-start(bf16[512,256]{1,0:T(8,128)(2,1)} %key_ref.3) | copy-start | bytes 786436
  81.5 5.3 %copy-start.1 = (bf16[512,256]{1,0:T(8,128)(2,1)S(1)}, bf16[512,256]{1,0:T(8,128)(2,1)}, u32[]{:S(2)}) copy-start(bf16[512,256]{1,0:T(8,128)(2,1)} %value_ref.3) | copy-start | bytes 786436
  83.2 13.1 %all-to-all-start.3 = ((bf16[16,2,32,256]{3,2,1,0:T(8,128)(2,1)}), bf16[16,2,32,256]{3,2,1,0:T(8,128)(2,1)S(1)}, u32[]{:S(2)}, u32[]{:S(2)}) async-start(bf16[16,2,32,256]{3,2,1,0:T(8,128)(2,1)} %reduce.1), calls=%async_computation.3 | async-start | bytes 1048576 | tf_op jit(solution)/shard_map/all_to_all | solution.py:309

commit v6 on v5

--- a/solution.py
+++ b/solution.py
@@ -14,6 +14,7 @@
 EXPONENT = SCALING * math.log2(math.e)
 TILE = 256
 STATS = 8
+SUBLANES = 8
 MIB = 1 << 20
 
 
@@ -85,6 +86,10 @@
                 )
     for head, total_ref in enumerate(total_refs):
         out_ref[:, :, :, head_columns(head)] = total_ref[...].astype(out_ref.dtype)
+
+
+def fold(array):
+    return jnp.sum(array.reshape(-1, SUBLANES, array.shape[1]), axis=0)
 
 
 def causal(scores, first):
@@ -165,32 +170,38 @@
     for copy in copies:
         copy.start()
 
-    def listed(which, slot, head):
-        return listed_ref[:, which, slot, :, head_columns(head)].reshape(rows, HEAD_DIM)
+    def listed(which, head):
+        return listed_ref[:, which, :, :, head_columns(head)].reshape(TOPK * rows, HEAD_DIM)
 
     def softmax(head):
         score_ref, grad_prob_ref, prob_ref, grad_score_ref = scratch[4 * head : 4 * head + 4]
         live = [
             selection_ref[(block * heads + head) * TOPK + slot] < block for slot in range(TOPK)
         ]
+        shape = (chunks, TOPK, chunk, TILE)
         for first in range(0, rows, TILE):
             tile = pl.ds(first, TILE)
+            scores = dot(listed(0, head), turned_ref[0, head, :, tile], 1, 0)
+            score_ref[:, :, :, tile] = scores.reshape(shape)
+            grad_probs = dot(listed(1, head), turned_ref[1, head, :, tile], 1, 0)
+            grad_prob_ref[:, :, :, tile] = grad_probs.reshape(shape)
             top = jnp.full((1, TILE), MASKED, jnp.float32)
             for slot in range(TOPK):
-                scores = dot(listed(0, slot, head), turned_ref[0, head, :, tile], 1, 0)
-                score_ref[slot, :, tile] = scores
-                highest = jnp.max(scores, axis=0, keepdims=True)
+                highest = jnp.max(
+                    score_ref[:, slot, :, tile].reshape(rows, TILE), axis=0, keepdims=True
+                )
                 top = jnp.maximum(top, jnp.where(live[slot], highest, MASKED))
-            total = jnp.zeros_like(top)
-            product = jnp.zeros_like(top)
+            total = jnp.zeros((SUBLANES, TILE), jnp.float32)
+            product = jnp.zeros_like(total)
             for slot in range(TOPK):
                 shift = jnp.where(live[slot], top, -MASKED)
-                raised = jnp.exp2((score_ref[slot, :, tile] - shift) * EXPONENT)
-                score_ref[slot, :, tile] = raised
-                grad_probs = dot(listed(1, slot, head), turned_ref[1, head, :, tile], 1, 0)
-                grad_prob_ref[slot, :, tile] = grad_probs
-                total += jnp.sum(raised, axis=0, keepdims=True)
-                product += jnp.sum(raised * grad_probs, axis=0, keepdims=True)
+                for part in range(chunks):
+                    raised = jnp.exp2((score_ref[part, slot, :, tile] - shift) * EXPONENT)
+                    score_ref[part, slot, :, tile] = raised
+                    total += fold(raised)
+                    product += fold(raised * grad_prob_ref[part, slot, :, tile])
+            total = jnp.sum(total, axis=0, keepdims=True)
+            product = jnp.sum(product, axis=0, keepdims=True)
             own_top = own_stats_ref[head, 0:1, tile]
             highest = jnp.maximum(own_top, top)
             own_factor = jnp.exp2((own_top - highest) * EXPONENT)
@@ -201,27 +212,25 @@
             stats_ref[head, 0:1, tile] = own_weight
             stats_ref[head, 1:2, tile] = delta
             for slot in range(TOPK):
-                probability = score_ref[slot, :, tile] * weight
-                prob_ref[slot, :, tile] = probability.astype(jnp.bfloat16)
-                grad_score_ref[slot, :, tile] = (
-                    probability * (grad_prob_ref[slot, :, tile] - delta)
-                ).astype(jnp.bfloat16)
+                for part in range(chunks):
+                    probability = score_ref[part, slot, :, tile] * weight
+                    prob_ref[part, slot, :, tile] = probability.astype(jnp.bfloat16)
+                    grad_score_ref[part, slot, :, tile] = (
+                        probability * (grad_prob_ref[part, slot, :, tile] - delta)
+                    ).astype(jnp.bfloat16)
 
     def gradients(head):
         _, _, prob_ref, grad_score_ref = scratch[4 * head : 4 * head + 4]
         columns = head_columns(head)
         query, grad = rows_ref[0, :, columns], rows_ref[1, :, columns]
-        shape = (chunks, chunk, HEAD_DIM)
-        part = None
-        for slot in range(TOPK):
-            grad_scores = grad_score_ref[slot]
-            grad_key = dot(grad_scores, query, 1, 0) * SCALING
-            terms_ref[:, 0, slot, :, columns] = grad_key.astype(jnp.bfloat16).reshape(shape)
-            grad_value = dot(prob_ref[slot], grad, 1, 0)
-            terms_ref[:, 1, slot, :, columns] = grad_value.astype(jnp.bfloat16).reshape(shape)
-            product = dot(listed(0, slot, head).T, grad_scores, 1, 0)
-            part = product if part is None else part + product
-        part_ref[head] = part
+        shape = (chunks, TOPK, chunk, HEAD_DIM)
+        prob = prob_ref[...].reshape(TOPK * rows, rows)
+        grad_scores = grad_score_ref[...].reshape(TOPK * rows, rows)
+        grad_key = dot(grad_scores, query, 1, 0) * SCALING
+        terms_ref[:, 0, :, :, columns] = grad_key.astype(jnp.bfloat16).reshape(shape)
+        grad_value = dot(prob, grad, 1, 0)
+        terms_ref[:, 1, :, :, columns] = grad_value.astype(jnp.bfloat16).reshape(shape)
+        part_ref[head] = dot(listed(0, head).T, grad_scores, 1, 0)
 
     for head in range(heads):
         softmax(head)
@@ -348,7 +357,7 @@
             jax.ShapeDtypeStruct((heads, STATS, rows), full),
         ),
         [pltpu.VMEM((4, rows, width), low), pltpu.SemaphoreType.DMA((4,))],
-        limit=58,
+        limit=16,
         slots=2,
     )(listed, query_input, key_input, value_input, grad_output)
     picked = call(
@@ -375,10 +384,10 @@
         ),
         [pltpu.VMEM((2, rows, width), low), pltpu.SemaphoreType.DMA((2,))]
         + [
-            pltpu.VMEM((TOPK, rows, rows), full),
-            pltpu.VMEM((TOPK, rows, rows), full),
-            pltpu.VMEM((TOPK, rows, rows), low),
-            pltpu.VMEM((TOPK, rows, rows), low),
+            pltpu.VMEM((chain, TOPK, chunk, rows), full),
+            pltpu.VMEM((chain, TOPK, chunk, rows), full),
+            pltpu.VMEM((chain, TOPK, chunk, rows), low),
+            pltpu.VMEM((chain, TOPK, chunk, rows), low),
         ]
         * heads,
         limit=32,

time: 132 us -> 132 us (level)
  transfers between devices with their start and end apart: 3 -> 3, of which waited for: 3 -> 3; matrix products, arithmetic and copies ran while one was open for 1% -> 0% of each run, Pallas kernels for 4% -> 3%
where the time goes in v6:
time: 132 us; the launch traced here: 131 us
  blocking collectives  61.2 us (46%)
  waiting for transfers between devices  35 us (27%)
  Pallas kernels  18 us (14%)
  starting transfers between devices  14.9 us (11%)
    all_to_all x2, blocking collectives, swap(): return lax.all_to_all(array, axis, split_axis=0, concat_axis=0, tiled=True)  61.2 us
    all_to_all x3, waiting for transfers between devices, swap(): return lax.all_to_all(array, axis, split_axis=0, concat_axis=0, tiled=True)  35 us
    all_to_all x3, starting transfers between devices, swap(): return lax.all_to_all(array, axis, split_axis=0, concat_axis=0, tiled=True)  14.9 us
    pallas_call x1, Pallas kernels, on_device(): call(far_kernel, 'far', [smem, smem, vmem, anywhere, anywhere, vmem, vmem...  6.87 us
  transfers between devices with their start and end apart: 3, of which 3 were waited for; matrix products, arithmetic and copies ran while one was open for 0% of the time, Pallas kernels for 3%

profile of v6, /device:TPU:1, one launch (start us, length us, event | category | flops | bytes accessed | tf_op | source)
XLA Modules:
  0.0 131.2 jit_solution(4578009555896301566)
XLA Ops:
  0.6 0.0 copy-start
  0.6 0.0 copy-start.1
  0.7 0.0 copy-start.6
  0.7 0.0 copy-start.3
  0.7 0.0 copy-start.2
  0.7 1.9 %stack.1 = bf16[16,2,32,256]{3,2,1,0:T(8,128)(2,1)} custom-call(bf16[16,32,256]{2,1,0:T(8,128)(2,1)} %bitcast.3, bf16[16,32,256]{2,1,0:T(8,128)(2,1)} %bitcast.4), custom_call_target="tpu_custom_call" | custom-call | bytes 4194304 | tf_op jit(solution)/shard_map/stack/pallas_call | solution.py:335
  2.6 7.6 %all-to-all-start = ((bf16[16,2,32,256]{3,2,1,0:T(8,128)(2,1)}), bf16[16,2,32,256]{3,2,1,0:T(8,128)(2,1)S(1)}, u32[]{:S(2)}, u32[]{:S(2)}) async-start(bf16[16,2,32,256]{3,2,1,0:T(8,128)(2,1)} %stack.1), calls=%async_computation | async-start | bytes 1048576 | tf_op jit(solution)/shard_map/all_to_all | solution.py:318
  10.2 0.0 copy-done.6
  10.2 0.1 copy.9
  10.3 0.1 reshape.18.selection_ref
  10.4 0.0 copy-done
  10.4 0.0 copy-done.1
  10.4 0.0 copy-done.3
  10.4 0.0 copy-done.2
  10.4 2.4 %own_forward.1 = (s32[96]{0:T(128)S(1)}, bf16[2,2,128,512]{3,2,1,0:T(8,128)(2,1)S(1)}, f32[2,8,512]{2,1,0:T(8,128)S(1)}) custom-call(s32[96]{0:T(128)S(1)} %reshape.18.selection_ref, bf16[512,256]{1,0:T(8,128)(2,1)S(1)} %copy-done.2, bf16[512,256]{1,0:T(8,128)(2,1)S(1)} %copy-done, bf16[512,256]{1,0:T(8,128)(2,1)S(1)} %copy-done.1, ...), custom_call_target="tpu_custom_call" | custom-call | flops 268435456 | bytes 4194304 | tf_op jit(solution)/shard_map/own_forward/pallas_call | solution.py:349
  12.9 7.8 %all-to-all-done.held_ref = bf16[16,2,32,256]{3,2,1,0:T(8,128)(2,1)S(1)} async-done(((bf16[16,2,32,256]{3,2,1,0:T(8,128)(2,1)}), bf16[16,2,32,256]{3,2,1,0:T(8,128)(2,1)S(1)}, u32[]{:S(2)}, u32[]{:S(2)}) %all-to-all-start) | async-done | bytes 524320 | tf_op jit(solution)/shard_map/all_to_all | solution.py:318
  20.7 1.9 %pick.1 = bf16[16,2,3,32,256]{4,3,2,1,0:T(8,128)(2,1)} custom-call(s32[96]{0:T(128)S(1)} %get-tuple-element.9.selection_ref, bf16[16,2,32,256]{3,2,1,0:T(8,128)(2,1)S(1)} %all-to-all-done.held_ref), custom_call_target="tpu_custom_call" | custom-call | bytes 4194304 | tf_op jit(solution)/shard_map/pick/pallas_call | solution.py:363
  22.6 3.7 %all-to-all-start.1 = ((bf16[16,2,3,32,256]{4,3,2,1,0:T(8,128)(2,1)}), bf16[16,2,3,32,256]{4,3,2,1,0:T(8,128)(2,1)S(1)}, u32[]{:S(2)}, u32[]{:S(2)}) async-start(bf16[16,2,3,32,256]{4,3,2,1,0:T(8,128)(2,1)} %pick.1), calls=%async_computation.1 | async-start | bytes 3145728 | tf_op jit(solution)/shard_map/all_to_all | solution.py:318
  26.3 20.5 %all-to-all-done.1.listed_ref = bf16[16,2,3,32,256]{4,3,2,1,0:T(8,128)(2,1)S(1)} async-done(((bf16[16,2,3,32,256]{4,3,2,1,0:T(8,128)(2,1)}), bf16[16,2,3,32,256]{4,3,2,1,0:T(8,128)(2,1)S(1)}, u32[]{:S(2)}, u32[]{:S(2)}) %all-to-all-start.1) | async-done | bytes 1572896 | tf_op jit(solution)/shard_map/all_to_all | solution.py:318
  46.8 6.9 %far.1 = (bf16[16,2,3,32,256]{4,3,2,1,0:T(8,128)(2,1)S(1)}, f32[2,128,512]{2,1,0:T(8,128)S(1)}, f32[2,8,512]{2,1,0:T(8,128)S(1)}) custom-call(s32[96]{0:T(128)S(1)} %get-tuple-element.9.selection_ref, s32[1]{0:T(128)} %bitcast.position_ref, bf16[2,2,128,512]{3,2,1,0:T(8,128)(2,1)S(1)} %get-tuple-element.10.turned_ref, bf16[512,256]{1,0:T(8,128)(2,1)S(1)} %copy-done.2, ...), custom_call_target="tpu_custom_call" | custom-call | flops 2013265920 | bytes 4194304 | tf_op jit(solution)/shard_map/far/pallas_call | solution.py:375
  53.7 0.0 copy-start.4
  53.7 27.1 %all_to_all.25.terms_ref = bf16[16,2,3,32,256]{4,3,2,1,0:T(8,128)(2,1)S(1)} all-to-all(bf16[16,2,3,32,256]{4,3,2,1,0:T(8,128)(2,1)S(1)} %get-tuple-element.14), channel_id=1, replica_groups=mesh['chain'=16,'heads'=16] {'chain'}, dimensions={0} | all-to-all | bytes 3145728 | tf_op jit(solution)/shard_map/all_to_all | solution.py:318
  80.8 0.0 copy-done.4
  80.8 1.7 %reduce.1 = bf16[16,2,32,256]{3,2,1,0:T(8,128)(2,1)} custom-call(s32[96]{0:T(128)S(1)} %get-tuple-element.9.selection_ref, bf16[16,2,3,32,256]{4,3,2,1,0:T(8,128)(2,1)S(1)} %all_to_all.25.terms_ref), custom_call_target="tpu_custom_call" | custom-call | bytes 4194304 | tf_op jit(solution)/shard_map/reduce/pallas_call | solution.py:406
  82.5 3.6 %all-to-all-start.3 = ((bf16[16,2,32,256]{3,2,1,0:T(8,128)(2,1)}), bf16[16,2,32,256]{3,2,1,0:T(8,128)(2,1)S(1)}, u32[]{:S(2)}, u32[]{:S(2)}) async-start(bf16[16,2,32,256]{3,2,1,0:T(8,128)(2,1)} %reduce.1), calls=%async_computation.3 | async-start | bytes 1048576 | tf_op jit(solution)/shard_map/all_to_all | solution.py:318
  86.1 0.0 copy-start.5
  86.1 1.0 copy-done.5
  87.1 1.8 %own_backward.1.own_ref = bf16[16,3,32,256]{3,2,1,0:T(8,128)(2,1)S(1)} custom-call(bf16[512,256]{1,0:T(8,128)(2,1)S(1)} %copy-done.2, bf16[512,256]{1,0:T(8,128)(2,1)S(1)} %copy-done, bf16[512,256]{1,0:T(8,128)(2,1)S(1)} %copy-done.1, bf16[512,256]{1,0:T(8,128)(2,1)S(1)} %copy-done.3, f32[2,128,512]{2,1,0:T(8,128)S(1)} %copy-done.5, ...), custom_call_target="tpu_custom_call" | custom-call | flops 671088640 | bytes 4194304 | tf_op jit(solution)/shard_map/own_backward/pallas_call | solution.py:397
  89.0 6.7 %all-to-all-done.3.others_ref = bf16[16,2,32,256]{3,2,1,0:T(8,128)(2,1)S(1)} async-done(((bf16[16,2,32,256]{3,2,1,0:T(8,128)(2,1)}), bf16[16,2,32,256]{3,2,1,0:T(8,128)(2,1)S(1)}, u32[]{:S(2)}, u32[]{:S(2)}) %all-to-all-start.3) | async-done | bytes 524320 | tf_op jit(solution)/shard_map/all_to_all | solution.py:318
  95.6 0.1 finish.1
  95.8 34.1 %all_to_all.26.parts_ref = bf16[16,3,32,256]{3,2,1,0:T(8,128)(2,1)S(1)} all-to-all(bf16[16,3,32,256]{3,2,1,0:T(8,128)(2,1)S(1)} %finish.1), channel_id=1, replica_groups=mesh['chain'=16,'heads'=16] {'heads'}, dimensions={0} | all-to-all | bytes 1572864 | tf_op jit(solution)/shard_map/all_to_all | solution.py:318
  129.9 1.3 lay.1
Async XLA Ops:
  0.6 9.8 %copy-start = (bf16[512,256]{1,0:T(8,128)(2,1)S(1)}, bf16[512,256]{1,0:T(8,128)(2,1)}, u32[]{:S(2)}) copy-start(bf16[512,256]{1,0:T(8,128)(2,1)} %key_ref.3) | copy-start | bytes 786436
  0.6 9.8 %copy-start.1 = (bf16[512,256]{1,0:T(8,128)(2,1)S(1)}, bf16[512,256]{1,0:T(8,128)(2,1)}, u32[]{:S(2)}) copy-start(bf16[512,256]{1,0:T(8,128)(2,1)} %value_ref.3) | copy-start | bytes 786436
  0.7 9.5 %copy-start.6 = (s32[16,2,3]{0,1,2:T(2,128)S(1)}, s32[16,2,3]{0,1,2:T(2,128)}, u32[]{:S(2)}) copy-start(s32[16,2,3]{0,1,2:T(2,128)} %param.9) | copy-start | bytes 1156
  0.7 9.8 %copy-start.3 = (bf16[512,256]{1,0:T(8,128)(2,1)S(1)}, bf16[512,256]{1,0:T(8,128)(2,1)}, u32[]{:S(2)}) copy-start(bf16[512,256]{1,0:T(8,128)(2,1)} %grad_ref.5) | copy-start | bytes 786436
  0.7 9.8 %copy-start.2 = (bf16[512,256]{1,0:T(8,128)(2,1)S(1)}, bf16[512,256]{1,0:T(8,128)(2,1)}, u32[]{:S(2)}) copy-start(bf16[512,256]{1,0:T(8,128)(2,1)} %query_ref.5) | copy-start | bytes 786436
  2.6 18.1 %all-to-all-start = ((bf16[16,2,32,256]{3,2,1,0:T(8,128)(2,1)}), bf16[16,2,32,256]{3,2,1,0:T(8,128)(2,1)S(1)}, u32[]{:S(2)}, u32[]{:S(2)}) async-start(bf16[16,2,32,256]{3,2,1,0:T(8,128)(2,1)} %stack.1), calls=%async_computation | async-start | bytes 1048576 | tf_op jit(solution)/shard_map/all_to_all | solution.py:318
  22.6 24.3 %all-to-all-start.1 = ((bf16[16,2,3,32,256]{4,3,2,1,0:T(8,128)(2,1)}), bf16[16,2,3,32,256]{4,3,2,1,0:T(8,128)(2,1)S(1)}, u32[]{:S(2)}, u32[]{:S(2)}) async-start(bf16[16,2,3,32,256]{4,3,2,1,0:T(8,128)(2,1)} %pick.1), calls=%async_computation.1 | async-start | bytes 3145728 | tf_op jit(solution)/shard_map/all_to_all | solution.py:318
  53.7 27.1 %copy-start.4 = (f32[2,128,512]{2,1,0:T(8,128)}, f32[2,128,512]{2,1,0:T(8,128)S(1)}, u32[]{:S(2)}) copy-start(f32[2,128,512]{2,1,0:T(8,128)S(1)} %get-tuple-element.12.part_ref) | copy-start | bytes 1572868
  82.5 13.1 %all-to-all-start.3 = ((bf16[16,2,32,256]{3,2,1,0:T(8,128)(2,1)}), bf16[16,2,32,256]{3,2,1,0:T(8,128)(2,1)S(1)}, u32[]{:S(2)}, u32[]{:S(2)}) async-start(bf16[16,2,32,256]{3,2,1,0:T(8,128)(2,1)} %reduce.1), calls=%async_computation.3 | async-start | bytes 1048576 | tf_op jit(solution)/shard_map/all_to_all | solution.py:318
  86.1 1.0 copy-start.5

commit v7 on v6

--- a/solution.py
+++ b/solution.py
@@ -154,7 +154,6 @@
     listed_ref,
     own_stats_ref,
     terms_ref,
-    part_ref,
     stats_ref,
     rows_ref,
     sem,
@@ -207,10 +206,11 @@
             own_factor = jnp.exp2((own_top - highest) * EXPONENT)
             factor = jnp.exp2((top - highest) * EXPONENT)
             inverse = 1.0 / (own_factor * own_stats_ref[head, 1:2, tile] + factor * total)
-            own_weight, weight = own_factor * inverse, factor * inverse
-            delta = own_weight * own_stats_ref[head, 2:3, tile] + weight * product
-            stats_ref[head, 0:1, tile] = own_weight
-            stats_ref[head, 1:2, tile] = delta
+            weight = factor * inverse
+            delta = own_factor * inverse * own_stats_ref[head, 2:3, tile] + weight * product
+            stats_ref[head, 0:1, tile] = highest
+            stats_ref[head, 1:2, tile] = inverse
+            stats_ref[head, 2:3, tile] = delta
             for slot in range(TOPK):
                 for part in range(chunks):
                     probability = score_ref[part, slot, :, tile] * weight
@@ -230,7 +230,6 @@
         terms_ref[:, 0, :, :, columns] = grad_key.astype(jnp.bfloat16).reshape(shape)
         grad_value = dot(prob, grad, 1, 0)
         terms_ref[:, 1, :, :, columns] = grad_value.astype(jnp.bfloat16).reshape(shape)
-        part_ref[head] = dot(listed(0, head).T, grad_scores, 1, 0)
 
     for head in range(heads):
         softmax(head)
@@ -241,33 +240,48 @@
 
 
 def own_backward_kernel(
+    selection_ref,
+    position_ref,
     query_ref,
     key_ref,
     value_ref,
     grad_ref,
-    part_ref,
-    own_stats_ref,
+    listed_ref,
     stats_ref,
     own_ref,
 ):
     heads, _, rows = stats_ref.shape
     chunks, _, chunk, _ = own_ref.shape
+    block = position_ref[0]
 
     def one_head(head, carry):
         columns = head_columns(head)
-        query, key = query_ref[:, columns], key_ref[:, columns]
-        value, grad = value_ref[:, columns], grad_ref[:, columns]
-        scores = causal(dot(key, query, 1, 1), 0)
-        raised = jnp.exp2((scores - own_stats_ref[head, 0:1, :]) * EXPONENT)
-        probability = raised * stats_ref[head, 0:1, :]
-        grad_probs = dot(value, grad, 1, 1)
-        grad_scores = (probability * (grad_probs - stats_ref[head, 1:2, :])).astype(jnp.bfloat16)
-        results = (
-            ((part_ref[head] + dot(key.T, grad_scores, 1, 0)) * SCALING).T,
-            dot(grad_scores, query, 1, 0) * SCALING,
-            dot(probability.astype(jnp.bfloat16), grad, 1, 0),
+        query, grad = query_ref[:, columns], grad_ref[:, columns]
+        highest, inverse = stats_ref[head, 0:1, :], stats_ref[head, 1:2, :]
+        delta = stats_ref[head, 2:3, :]
+
+        def scores_and_grads(scores, shift, value):
+            probability = jnp.exp2((scores - shift) * EXPONENT) * inverse
+            grad_probs = dot(value, grad, 1, 1)
+            return probability, (probability * (grad_probs - delta)).astype(jnp.bfloat16)
+
+        key = key_ref[:, columns]
+        probability, grad_scores = scores_and_grads(
+            causal(dot(key, query, 1, 1), 0), highest, value_ref[:, columns]
         )
-        for index, result in enumerate(results):
+        total = dot(key.T, grad_scores, 1, 0)
+        grad_key = dot(grad_scores, query, 1, 0) * SCALING
+        grad_value = dot(probability.astype(jnp.bfloat16), grad, 1, 0)
+        for slot in range(TOPK):
+            live = selection_ref[(block * heads + head) * TOPK + slot] < block
+            shift = jnp.where(live, highest, -MASKED)
+            key, value = (
+                listed_ref[:, which, slot, :, columns].reshape(rows, HEAD_DIM)
+                for which in range(2)
+            )
+            _, grad_scores = scores_and_grads(dot(key, query, 1, 1), shift, value)
+            total += dot(key.T, grad_scores, 1, 0)
+        for index, result in enumerate(((total * SCALING).T, grad_key, grad_value)):
             own_ref[:, index, :, columns] = result.astype(jnp.bfloat16).reshape(
                 chunks, chunk, HEAD_DIM
             )
@@ -372,14 +386,13 @@
         ],
     )(listed, held)
     slots = swap(picked, "chain")
-    terms, part, stats = call(
+    terms, stats = call(
         far_kernel,
         "far",
         [smem, smem, vmem, anywhere, anywhere, vmem, vmem],
-        (vmem, vmem, vmem),
+        (vmem, vmem),
         (
             jax.ShapeDtypeStruct((chain, 2, TOPK, chunk, width), low),
-            jax.ShapeDtypeStruct((heads, HEAD_DIM, rows), full),
             jax.ShapeDtypeStruct((heads, STATS, rows), full),
         ),
         [pltpu.VMEM((2, rows, width), low), pltpu.SemaphoreType.DMA((2,))]
@@ -391,18 +404,18 @@
         ]
         * heads,
         limit=32,
-        slots=5 * TOPK,
+        slots=4 * TOPK,
     )(listed, position, turned, query_input, grad_output, slots, own_stats)
     returned = swap(terms, "chain")
     own = call(
         own_backward_kernel,
         "own_backward",
-        [vmem] * 7,
+        [smem] * 2 + [vmem] * 6,
         vmem,
         jax.ShapeDtypeStruct((chain, 3, chunk, width), low),
         limit=12,
-        slots=5,
-    )(query_input, key_input, value_input, grad_output, part, own_stats, stats)
+        slots=5 + 3 * TOPK,
+    )(listed, position, query_input, key_input, value_input, grad_output, slots, stats)
     summed = call(
         reduce_kernel,
         "reduce",

time: 132 us -> 132 us (level)
  waiting for transfers between devices: 35 us -> 30.9 us
  Pallas kernels: 18 us -> 20.9 us
  local copies, waits for them, and re-layouts: 1.27 us -> 3.17 us
    all_to_all x3, waiting for transfers between devices: 35 us -> 30.9 us  [swap(): return lax.all_to_all(array, axis, split_axis=0, concat_axis=0, tiled=True)]
    pallas_call x1, Pallas kernels: 1.84 us -> 5.12 us  [on_device(): call(own_backward_kernel, 'own_backward', [smem] * 2 + [vmem] * 6, vmem,...]
    unnamed x15 -> x19, local copies, waits for them, and re-layouts: 1.16 us -> 3.06 us
  transfers between devices with their start and end apart: 3 -> 3, of which waited for: 3 -> 3; matrix products, arithmetic and copies ran while one was open for 0% -> 0% of each run, Pallas kernels for 3% -> 6%
where the time goes in v7:
time: 132 us
  blocking collectives  61.2 us (46%)
  waiting for transfers between devices  30.9 us (23%)
  Pallas kernels  20.9 us (16%)
  starting transfers between devices  14.9 us (11%)
  local copies, waits for them, and re-layouts  3.17 us (2%)
    all_to_all x2, blocking collectives, swap(): return lax.all_to_all(array, axis, split_axis=0, concat_axis=0, tiled=True)  61.2 us
    all_to_all x3, waiting for transfers between devices, swap(): return lax.all_to_all(array, axis, split_axis=0, concat_axis=0, tiled=True)  30.9 us
    all_to_all x3, starting transfers between devices, swap(): return lax.all_to_all(array, axis, split_axis=0, concat_axis=0, tiled=True)  14.9 us
    pallas_call x1, Pallas kernels, on_device(): call(far_kernel, 'far', [smem, smem, vmem, anywhere, anywhere, vmem, vmem...  6.47 us
    pallas_call x1, Pallas kernels, on_device(): call(own_backward_kernel, 'own_backward', [smem] * 2 + [vmem] * 6, vmem,...  5.12 us
    unnamed x19, local copies, waits for them, and re-layouts  3.06 us
  transfers between devices with their start and end apart: 3, of which 3 were waited for; matrix products, arithmetic and copies ran while one was open for 0% of the time, Pallas kernels for 6%

profile of v7, /device:TPU:1, one launch (start us, length us, event | category | flops | bytes accessed | tf_op | source)
XLA Modules:
  0.0 131.9 jit_solution(14900443974857319708)
XLA Ops:
  0.6 0.0 copy-start
  0.6 0.0 copy-start.1
  0.7 0.0 copy-start.8
  0.7 0.0 copy-start.4
  0.7 0.0 copy-start.2
  0.7 1.9 %stack.1 = bf16[16,2,32,256]{3,2,1,0:T(8,128)(2,1)} custom-call(bf16[16,32,256]{2,1,0:T(8,128)(2,1)} %bitcast.3, bf16[16,32,256]{2,1,0:T(8,128)(2,1)} %bitcast.4), custom_call_target="tpu_custom_call" | custom-call | bytes 4194304 | tf_op jit(solution)/shard_map/stack/pallas_call | solution.py:349
  2.6 7.6 %all-to-all-start = ((bf16[16,2,32,256]{3,2,1,0:T(8,128)(2,1)}), bf16[16,2,32,256]{3,2,1,0:T(8,128)(2,1)S(1)}, u32[]{:S(2)}, u32[]{:S(2)}) async-start(bf16[16,2,32,256]{3,2,1,0:T(8,128)(2,1)} %stack.1), calls=%async_computation | async-start | bytes 1048576 | tf_op jit(solution)/shard_map/all_to_all | solution.py:332
  10.2 0.0 copy-done.8
  10.2 0.1 copy.9
  10.3 0.1 reshape.18.selection_ref
  10.4 0.0 copy-done
  10.4 0.0 copy-done.1
  10.4 0.0 copy-done.4
  10.5 0.0 copy-done.2
  10.5 2.4 %own_forward.1 = (s32[96]{0:T(128)S(1)}, bf16[2,2,128,512]{3,2,1,0:T(8,128)(2,1)S(1)}, f32[2,8,512]{2,1,0:T(8,128)S(1)}) custom-call(s32[96]{0:T(128)S(1)} %reshape.18.selection_ref, bf16[512,256]{1,0:T(8,128)(2,1)S(1)} %copy-done.2, bf16[512,256]{1,0:T(8,128)(2,1)S(1)} %copy-done, bf16[512,256]{1,0:T(8,128)(2,1)S(1)} %copy-done.1, ...), custom_call_target="tpu_custom_call" | custom-call | flops 268435456 | bytes 4194304 | tf_op jit(solution)/shard_map/own_forward/pallas_call | solution.py:363
  12.9 0.0 copy-start.6
  12.9 7.8 %all-to-all-done.held_ref = bf16[16,2,32,256]{3,2,1,0:T(8,128)(2,1)S(1)} async-done(((bf16[16,2,32,256]{3,2,1,0:T(8,128)(2,1)}), bf16[16,2,32,256]{3,2,1,0:T(8,128)(2,1)S(1)}, u32[]{:S(2)}, u32[]{:S(2)}) %all-to-all-start) | async-done | bytes 524320 | tf_op jit(solution)/shard_map/all_to_all | solution.py:332
  20.7 1.9 %pick.1 = bf16[16,2,3,32,256]{4,3,2,1,0:T(8,128)(2,1)} custom-call(s32[96]{0:T(128)S(1)} %get-tuple-element.8.selection_ref, bf16[16,2,32,256]{3,2,1,0:T(8,128)(2,1)S(1)} %all-to-all-done.held_ref), custom_call_target="tpu_custom_call" | custom-call | bytes 4194304 | tf_op jit(solution)/shard_map/pick/pallas_call | solution.py:377
  22.6 0.0 copy-done.6
  22.6 3.7 %all-to-all-start.1 = ((bf16[16,2,3,32,256]{4,3,2,1,0:T(8,128)(2,1)}), bf16[16,2,3,32,256]{4,3,2,1,0:T(8,128)(2,1)S(1)}, u32[]{:S(2)}, u32[]{:S(2)}) async-start(bf16[16,2,3,32,256]{4,3,2,1,0:T(8,128)(2,1)} %pick.1), calls=%async_computation.1 | async-start | bytes 3145728 | tf_op jit(solution)/shard_map/all_to_all | solution.py:332
  26.3 20.5 %all-to-all-done.1.listed_ref = bf16[16,2,3,32,256]{4,3,2,1,0:T(8,128)(2,1)S(1)} async-done(((bf16[16,2,3,32,256]{4,3,2,1,0:T(8,128)(2,1)}), bf16[16,2,3,32,256]{4,3,2,1,0:T(8,128)(2,1)S(1)}, u32[]{:S(2)}, u32[]{:S(2)}) %all-to-all-start.1) | async-done | bytes 1572896 | tf_op jit(solution)/shard_map/all_to_all | solution.py:332
  46.9 0.0 copy-start.7
  46.9 1.0 copy-done.7
  47.9 6.5 %far.1 = (bf16[16,2,3,32,256]{4,3,2,1,0:T(8,128)(2,1)S(1)}, f32[2,8,512]{2,1,0:T(8,128)S(1)}) custom-call(s32[96]{0:T(128)S(1)} %get-tuple-element.8.selection_ref, s32[1]{0:T(128)} %bitcast.position_ref, bf16[2,2,128,512]{3,2,1,0:T(8,128)(2,1)S(1)} %copy-done.7, bf16[512,256]{1,0:T(8,128)(2,1)S(1)} %copy-done.2, bf16[512,256]{1,0:T(8,128)(2,1)S(1)} %copy-done.4, ...), custom_call_target="tpu_custom_call" | custom-call | flops 1610612736 | bytes 4194304 | tf_op jit(solution)/shard_map/far/pallas_call | solution.py:389
  54.4 27.1 %all_to_all.25.terms_ref = bf16[16,2,3,32,256]{4,3,2,1,0:T(8,128)(2,1)S(1)} all-to-all(bf16[16,2,3,32,256]{4,3,2,1,0:T(8,128)(2,1)S(1)} %get-tuple-element.12), channel_id=1, replica_groups=mesh['chain'=16,'heads'=16] {'chain'}, dimensions={0} | all-to-all | bytes 3145728 | tf_op jit(solution)/shard_map/all_to_all | solution.py:332
  81.5 1.7 %reduce.1 = bf16[16,2,32,256]{3,2,1,0:T(8,128)(2,1)} custom-call(s32[96]{0:T(128)S(1)} %get-tuple-element.8.selection_ref, bf16[16,2,3,32,256]{4,3,2,1,0:T(8,128)(2,1)S(1)} %all_to_all.25.terms_ref), custom_call_target="tpu_custom_call" | custom-call | bytes 4194304 | tf_op jit(solution)/shard_map/reduce/pallas_call | solution.py:419
  83.2 3.6 %all-to-all-start.3 = ((bf16[16,2,32,256]{3,2,1,0:T(8,128)(2,1)}), bf16[16,2,32,256]{3,2,1,0:T(8,128)(2,1)S(1)}, u32[]{:S(2)}, u32[]{:S(2)}) async-start(bf16[16,2,32,256]{3,2,1,0:T(8,128)(2,1)} %reduce.1), calls=%async_computation.3 | async-start | bytes 1048576 | tf_op jit(solution)/shard_map/all_to_all | solution.py:332
  86.7 0.0 copy-start.3
  86.8 0.9 copy-done.3
  87.7 0.0 copy-start.5
  87.7 0.9 copy-done.5
  88.6 5.1 %own_backward.1.own_ref = bf16[16,3,32,256]{3,2,1,0:T(8,128)(2,1)S(1)} custom-call(s32[96]{0:T(128)S(1)} %get-tuple-element.8.selection_ref, s32[1]{0:T(128)} %bitcast.position_ref, bf16[512,256]{1,0:T(8,128)(2,1)S(1)} %copy-done.3, bf16[512,256]{1,0:T(8,128)(2,1)S(1)} %copy-done, bf16[512,256]{1,0:T(8,128)(2,1)S(1)} %copy-done.1, ...), custom_call_target="tpu_custom_call" | custom-call | flops 1879048192 | bytes 4194304 | tf_op jit(solution)/shard_map/own_backward/pallas_call | solution.py:410
  93.8 2.5 %all-to-all-done.3.others_ref = bf16[16,2,32,256]{3,2,1,0:T(8,128)(2,1)S(1)} async-done(((bf16[16,2,32,256]{3,2,1,0:T(8,128)(2,1)}), bf16[16,2,32,256]{3,2,1,0:T(8,128)(2,1)S(1)}, u32[]{:S(2)}, u32[]{:S(2)}) %all-to-all-start.3) | async-done | bytes 524320 | tf_op jit(solution)/shard_map/all_to_all | solution.py:332
  96.3 0.2 finish.1
  96.5 34.1 %all_to_all.26.parts_ref = bf16[16,3,32,256]{3,2,1,0:T(8,128)(2,1)S(1)} all-to-all(bf16[16,3,32,256]{3,2,1,0:T(8,128)(2,1)S(1)} %finish.1), channel_id=1, replica_groups=mesh['chain'=16,'heads'=16] {'heads'}, dimensions={0} | all-to-all | bytes 1572864 | tf_op jit(solution)/shard_map/all_to_all | solution.py:332
  130.6 1.3 lay.1
Async XLA Ops:
  0.6 9.8 %copy-start = (bf16[512,256]{1,0:T(8,128)(2,1)S(1)}, bf16[512,256]{1,0:T(8,128)(2,1)}, u32[]{:S(2)}) copy-start(bf16[512,256]{1,0:T(8,128)(2,1)} %key_ref.3) | copy-start | bytes 786436
  0.6 9.8 %copy-start.1 = (bf16[512,256]{1,0:T(8,128)(2,1)S(1)}, bf16[512,256]{1,0:T(8,128)(2,1)}, u32[]{:S(2)}) copy-start(bf16[512,256]{1,0:T(8,128)(2,1)} %value_ref.3) | copy-start | bytes 786436
  0.7 9.6 %copy-start.8 = (s32[16,2,3]{0,1,2:T(2,128)S(1)}, s32[16,2,3]{0,1,2:T(2,128)}, u32[]{:S(2)}) copy-start(s32[16,2,3]{0,1,2:T(2,128)} %param.9) | copy-start | bytes 1156
  0.7 9.8 %copy-start.4 = (bf16[512,256]{1,0:T(8,128)(2,1)S(1)}, bf16[512,256]{1,0:T(8,128)(2,1)}, u32[]{:S(2)}) copy-start(bf16[512,256]{1,0:T(8,128)(2,1)} %grad_ref.5) | copy-start | bytes 786436
  0.7 9.8 %copy-start.2 = (bf16[512,256]{1,0:T(8,128)(2,1)S(1)}, bf16[512,256]{1,0:T(8,128)(2,1)}, u32[]{:S(2)}) copy-start(bf16[512,256]{1,0:T(8,128)(2,1)} %query_ref.5) | copy-start | bytes 786436
  2.6 18.1 %all-to-all-start = ((bf16[16,2,32,256]{3,2,1,0:T(8,128)(2,1)}), bf16[16,2,32,256]{3,2,1,0:T(8,128)(2,1)S(1)}, u32[]{:S(2)}, u32[]{:S(2)}) async-start(bf16[16,2,32,256]{3,2,1,0:T(8,128)(2,1)} %stack.1), calls=%async_computation | async-start | bytes 1048576 | tf_op jit(solution)/shard_map/all_to_all | solution.py:332
  12.9 9.7 %copy-start.6 = (bf16[2,2,128,512]{3,2,1,0:T(8,128)(2,1)}, bf16[2,2,128,512]{3,2,1,0:T(8,128)(2,1)S(1)}, u32[]{:S(2)}) copy-start(bf16[2,2,128,512]{3,2,1,0:T(8,128)(2,1)S(1)} %get-tuple-element.9.turned_ref) | copy-start | bytes 1572868
  22.6 24.3 %all-to-all-start.1 = ((bf16[16,2,3,32,256]{4,3,2,1,0:T(8,128)(2,1)}), bf16[16,2,3,32,256]{4,3,2,1,0:T(8,128)(2,1)S(1)}, u32[]{:S(2)}, u32[]{:S(2)}) async-start(bf16[16,2,3,32,256]{4,3,2,1,0:T(8,128)(2,1)} %pick.1), calls=%async_computation.1 | async-start | bytes 3145728 | tf_op jit(solution)/shard_map/all_to_all | solution.py:332
  46.9 1.0 copy-start.7
  83.2 13.1 %all-to-all-start.3 = ((bf16[16,2,32,256]{3,2,1,0:T(8,128)(2,1)}), bf16[16,2,32,256]{3,2,1,0:T(8,128)(2,1)S(1)}, u32[]{:S(2)}, u32[]{:S(2)}) async-start(bf16[16,2,32,256]{3,2,1,0:T(8,128)(2,1)} %reduce.1), calls=%async_computation.3 | async-start | bytes 1048576 | tf_op jit(solution)/shard_map/all_to_all | solution.py:332
  86.7 1.0 copy-start.3
  87.7 0.9 copy-start.5

commit v8 on v5

--- a/solution.py
+++ b/solution.py
@@ -14,6 +14,7 @@
 EXPONENT = SCALING * math.log2(math.e)
 TILE = 256
 STATS = 8
+SUBLANES = 8
 MIB = 1 << 20
 
 
@@ -85,6 +86,10 @@
                 )
     for head, total_ref in enumerate(total_refs):
         out_ref[:, :, :, head_columns(head)] = total_ref[...].astype(out_ref.dtype)
+
+
+def fold(array):
+    return jnp.sum(array.reshape(-1, SUBLANES, array.shape[1]), axis=0)
 
 
 def causal(scores, first):
@@ -165,32 +170,36 @@
     for copy in copies:
         copy.start()
 
-    def listed(which, slot, head):
+    def listed(which, head):
+        return listed_ref[:, which, :, :, head_columns(head)].reshape(TOPK * rows, HEAD_DIM)
+
+    def one_slot(which, slot, head):
         return listed_ref[:, which, slot, :, head_columns(head)].reshape(rows, HEAD_DIM)
 
     def softmax(head):
-        score_ref, grad_prob_ref, prob_ref, grad_score_ref = scratch[4 * head : 4 * head + 4]
+        raised_ref, prob_ref, grad_score_ref = scratch[3 * head : 3 * head + 3]
         live = [
             selection_ref[(block * heads + head) * TOPK + slot] < block for slot in range(TOPK)
         ]
         for first in range(0, rows, TILE):
             tile = pl.ds(first, TILE)
+            query, grad = turned_ref[0, head, :, tile], turned_ref[1, head, :, tile]
+            scores = dot(listed(0, head), query, 1, 0).reshape(chunks, TOPK, chunk, TILE)
             top = jnp.full((1, TILE), MASKED, jnp.float32)
             for slot in range(TOPK):
-                scores = dot(listed(0, slot, head), turned_ref[0, head, :, tile], 1, 0)
-                score_ref[slot, :, tile] = scores
-                highest = jnp.max(scores, axis=0, keepdims=True)
+                highest = jnp.max(scores[:, slot].reshape(rows, TILE), axis=0, keepdims=True)
                 top = jnp.maximum(top, jnp.where(live[slot], highest, MASKED))
-            total = jnp.zeros_like(top)
-            product = jnp.zeros_like(top)
+            total = jnp.zeros((SUBLANES, TILE), jnp.float32)
+            product = jnp.zeros_like(total)
             for slot in range(TOPK):
                 shift = jnp.where(live[slot], top, -MASKED)
-                raised = jnp.exp2((score_ref[slot, :, tile] - shift) * EXPONENT)
-                score_ref[slot, :, tile] = raised
-                grad_probs = dot(listed(1, slot, head), turned_ref[1, head, :, tile], 1, 0)
-                grad_prob_ref[slot, :, tile] = grad_probs
-                total += jnp.sum(raised, axis=0, keepdims=True)
-                product += jnp.sum(raised * grad_probs, axis=0, keepdims=True)
+                scores = dot(one_slot(0, slot, head), query, 1, 0)
+                raised = jnp.exp2((scores - shift) * EXPONENT)
+                raised_ref[slot, :, tile] = raised
+                total += fold(raised)
+                product += fold(raised * dot(one_slot(1, slot, head), grad, 1, 0))
+            total = jnp.sum(total, axis=0, keepdims=True)
+            product = jnp.sum(product, axis=0, keepdims=True)
             own_top = own_stats_ref[head, 0:1, tile]
             highest = jnp.maximum(own_top, top)
             own_factor = jnp.exp2((own_top - highest) * EXPONENT)
@@ -201,14 +210,15 @@
             stats_ref[head, 0:1, tile] = own_weight
             stats_ref[head, 1:2, tile] = delta
             for slot in range(TOPK):
-                probability = score_ref[slot, :, tile] * weight
+                probability = raised_ref[slot, :, tile] * weight
                 prob_ref[slot, :, tile] = probability.astype(jnp.bfloat16)
-                grad_score_ref[slot, :, tile] = (
-                    probability * (grad_prob_ref[slot, :, tile] - delta)
-                ).astype(jnp.bfloat16)
+                grad_probs = dot(one_slot(1, slot, head), grad, 1, 0)
+                grad_score_ref[slot, :, tile] = (probability * (grad_probs - delta)).astype(
+                    jnp.bfloat16
+                )
 
     def gradients(head):
-        _, _, prob_ref, grad_score_ref = scratch[4 * head : 4 * head + 4]
+        _, prob_ref, grad_score_ref = scratch[3 * head : 3 * head + 3]
         columns = head_columns(head)
         query, grad = rows_ref[0, :, columns], rows_ref[1, :, columns]
         shape = (chunks, chunk, HEAD_DIM)
@@ -219,7 +229,7 @@
             terms_ref[:, 0, slot, :, columns] = grad_key.astype(jnp.bfloat16).reshape(shape)
             grad_value = dot(prob_ref[slot], grad, 1, 0)
             terms_ref[:, 1, slot, :, columns] = grad_value.astype(jnp.bfloat16).reshape(shape)
-            product = dot(listed(0, slot, head).T, grad_scores, 1, 0)
+            product = dot(one_slot(0, slot, head).T, grad_scores, 1, 0)
             part = product if part is None else part + product
         part_ref[head] = part
 
@@ -348,7 +358,7 @@
             jax.ShapeDtypeStruct((heads, STATS, rows), full),
         ),
         [pltpu.VMEM((4, rows, width), low), pltpu.SemaphoreType.DMA((4,))],
-        limit=58,
+        limit=16,
         slots=2,
     )(listed, query_input, key_input, value_input, grad_output)
     picked = call(
@@ -376,7 +386,6 @@
         [pltpu.VMEM((2, rows, width), low), pltpu.SemaphoreType.DMA((2,))]
         + [
             pltpu.VMEM((TOPK, rows, rows), full),
-            pltpu.VMEM((TOPK, rows, rows), full),
             pltpu.VMEM((TOPK, rows, rows), low),
             pltpu.VMEM((TOPK, rows, rows), low),
         ]

time: 132 us -> 132 us (level)
  transfers between devices with their start and end apart: 3 -> 3, of which waited for: 3 -> 3; matrix products, arithmetic and copies ran while one was open for 1% -> 0% of each run, Pallas kernels for 4% -> 3%
where the time goes in v8:
time: 132 us
  blocking collectives  61.2 us (46%)
  waiting for transfers between devices  35 us (27%)
  Pallas kernels  18.6 us (14%)
  starting transfers between devices  14.9 us (11%)
    all_to_all x2, blocking collectives, swap(): return lax.all_to_all(array, axis, split_axis=0, concat_axis=0, tiled=True)  61.2 us
    all_to_all x3, waiting for transfers between devices, swap(): return lax.all_to_all(array, axis, split_axis=0, concat_axis=0, tiled=True)  35 us
    all_to_all x3, starting transfers between devices, swap(): return lax.all_to_all(array, axis, split_axis=0, concat_axis=0, tiled=True)  14.9 us
    pallas_call x1, Pallas kernels, on_device(): call(far_kernel, 'far', [smem, smem, vmem, anywhere, anywhere, vmem, vmem...  7.5 us
  transfers between devices with their start and end apart: 3, of which 3 were waited for; matrix products, arithmetic and copies ran while one was open for 0% of the time, Pallas kernels for 3%

profile of v8, /device:TPU:1, one launch (start us, length us, event | category | flops | bytes accessed | tf_op | source)
XLA Modules:
  0.0 131.8 jit_solution(14311427911730584587)
XLA Ops:
  0.6 0.0 copy-start
  0.6 0.0 copy-start.1
  0.7 0.0 copy-start.6
  0.7 0.0 copy-start.3
  0.7 0.0 copy-start.2
  0.7 1.9 %stack.1 = bf16[16,2,32,256]{3,2,1,0:T(8,128)(2,1)} custom-call(bf16[16,32,256]{2,1,0:T(8,128)(2,1)} %bitcast.3, bf16[16,32,256]{2,1,0:T(8,128)(2,1)} %bitcast.4), custom_call_target="tpu_custom_call" | custom-call | bytes 4194304 | tf_op jit(solution)/shard_map/stack/pallas_call | solution.py:336
  2.6 7.6 %all-to-all-start = ((bf16[16,2,32,256]{3,2,1,0:T(8,128)(2,1)}), bf16[16,2,32,256]{3,2,1,0:T(8,128)(2,1)S(1)}, u32[]{:S(2)}, u32[]{:S(2)}) async-start(bf16[16,2,32,256]{3,2,1,0:T(8,128)(2,1)} %stack.1), calls=%async_computation | async-start | bytes 1048576 | tf_op jit(solution)/shard_map/all_to_all | solution.py:319
  10.2 0.0 copy-done.6
  10.2 0.1 copy.9
  10.3 0.1 reshape.18.selection_ref
  10.4 0.0 copy-done
  10.4 0.0 copy-done.1
  10.4 0.0 copy-done.3
  10.4 0.0 copy-done.2
  10.4 2.4 %own_forward.1 = (s32[96]{0:T(128)S(1)}, bf16[2,2,128,512]{3,2,1,0:T(8,128)(2,1)S(1)}, f32[2,8,512]{2,1,0:T(8,128)S(1)}) custom-call(s32[96]{0:T(128)S(1)} %reshape.18.selection_ref, bf16[512,256]{1,0:T(8,128)(2,1)S(1)} %copy-done.2, bf16[512,256]{1,0:T(8,128)(2,1)S(1)} %copy-done, bf16[512,256]{1,0:T(8,128)(2,1)S(1)} %copy-done.1, ...), custom_call_target="tpu_custom_call" | custom-call | flops 268435456 | bytes 4194304 | tf_op jit(solution)/shard_map/own_forward/pallas_call | solution.py:350
  12.9 7.8 %all-to-all-done.held_ref = bf16[16,2,32,256]{3,2,1,0:T(8,128)(2,1)S(1)} async-done(((bf16[16,2,32,256]{3,2,1,0:T(8,128)(2,1)}), bf16[16,2,32,256]{3,2,1,0:T(8,128)(2,1)S(1)}, u32[]{:S(2)}, u32[]{:S(2)}) %all-to-all-start) | async-done | bytes 524320 | tf_op jit(solution)/shard_map/all_to_all | solution.py:319
  20.7 1.9 %pick.1 = bf16[16,2,3,32,256]{4,3,2,1,0:T(8,128)(2,1)} custom-call(s32[96]{0:T(128)S(1)} %get-tuple-element.9.selection_ref, bf16[16,2,32,256]{3,2,1,0:T(8,128)(2,1)S(1)} %all-to-all-done.held_ref), custom_call_target="tpu_custom_call" | custom-call | bytes 4194304 | tf_op jit(solution)/shard_map/pick/pallas_call | solution.py:364
  22.6 3.7 %all-to-all-start.1 = ((bf16[16,2,3,32,256]{4,3,2,1,0:T(8,128)(2,1)}), bf16[16,2,3,32,256]{4,3,2,1,0:T(8,128)(2,1)S(1)}, u32[]{:S(2)}, u32[]{:S(2)}) async-start(bf16[16,2,3,32,256]{4,3,2,1,0:T(8,128)(2,1)} %pick.1), calls=%async_computation.1 | async-start | bytes 3145728 | tf_op jit(solution)/shard_map/all_to_all | solution.py:319
  26.3 20.5 %all-to-all-done.1.listed_ref = bf16[16,2,3,32,256]{4,3,2,1,0:T(8,128)(2,1)S(1)} async-done(((bf16[16,2,3,32,256]{4,3,2,1,0:T(8,128)(2,1)}), bf16[16,2,3,32,256]{4,3,2,1,0:T(8,128)(2,1)S(1)}, u32[]{:S(2)}, u32[]{:S(2)}) %all-to-all-start.1) | async-done | bytes 1572896 | tf_op jit(solution)/shard_map/all_to_all | solution.py:319
  46.8 7.5 %far.1 = (bf16[16,2,3,32,256]{4,3,2,1,0:T(8,128)(2,1)S(1)}, f32[2,128,512]{2,1,0:T(8,128)S(1)}, f32[2,8,512]{2,1,0:T(8,128)S(1)}) custom-call(s32[96]{0:T(128)S(1)} %get-tuple-element.9.selection_ref, s32[1]{0:T(128)} %bitcast.position_ref, bf16[2,2,128,512]{3,2,1,0:T(8,128)(2,1)S(1)} %get-tuple-element.10.turned_ref, bf16[512,256]{1,0:T(8,128)(2,1)S(1)} %copy-done.2, ...), custom_call_target="tpu_custom_call" | custom-call | flops 2013265920 | bytes 4194304 | tf_op jit(solution)/shard_map/far/pallas_call | solution.py:376
  54.3 0.0 copy-start.4
  54.4 27.1 %all_to_all.25.terms_ref = bf16[16,2,3,32,256]{4,3,2,1,0:T(8,128)(2,1)S(1)} all-to-all(bf16[16,2,3,32,256]{4,3,2,1,0:T(8,128)(2,1)S(1)} %get-tuple-element.14), channel_id=1, replica_groups=mesh['chain'=16,'heads'=16] {'chain'}, dimensions={0} | all-to-all | bytes 3145728 | tf_op jit(solution)/shard_map/all_to_all | solution.py:319
  81.5 0.0 copy-done.4
  81.5 1.7 %reduce.1 = bf16[16,2,32,256]{3,2,1,0:T(8,128)(2,1)} custom-call(s32[96]{0:T(128)S(1)} %get-tuple-element.9.selection_ref, bf16[16,2,3,32,256]{4,3,2,1,0:T(8,128)(2,1)S(1)} %all_to_all.25.terms_ref), custom_call_target="tpu_custom_call" | custom-call | bytes 4194304 | tf_op jit(solution)/shard_map/reduce/pallas_call | solution.py:406
  83.2 3.6 %all-to-all-start.3 = ((bf16[16,2,32,256]{3,2,1,0:T(8,128)(2,1)}), bf16[16,2,32,256]{3,2,1,0:T(8,128)(2,1)S(1)}, u32[]{:S(2)}, u32[]{:S(2)}) async-start(bf16[16,2,32,256]{3,2,1,0:T(8,128)(2,1)} %reduce.1), calls=%async_computation.3 | async-start | bytes 1048576 | tf_op jit(solution)/shard_map/all_to_all | solution.py:319
  86.7 0.0 copy-start.5
  86.7 1.0 copy-done.5
  87.8 1.8 %own_backward.1.own_ref = bf16[16,3,32,256]{3,2,1,0:T(8,128)(2,1)S(1)} custom-call(bf16[512,256]{1,0:T(8,128)(2,1)S(1)} %copy-done.2, bf16[512,256]{1,0:T(8,128)(2,1)S(1)} %copy-done, bf16[512,256]{1,0:T(8,128)(2,1)S(1)} %copy-done.1, bf16[512,256]{1,0:T(8,128)(2,1)S(1)} %copy-done.3, f32[2,128,512]{2,1,0:T(8,128)S(1)} %copy-done.5, ...), custom_call_target="tpu_custom_call" | custom-call | flops 671088640 | bytes 4194304 | tf_op jit(solution)/shard_map/own_backward/pallas_call | solution.py:397
  89.6 6.7 %all-to-all-done.3.others_ref = bf16[16,2,32,256]{3,2,1,0:T(8,128)(2,1)S(1)} async-done(((bf16[16,2,32,256]{3,2,1,0:T(8,128)(2,1)}), bf16[16,2,32,256]{3,2,1,0:T(8,128)(2,1)S(1)}, u32[]{:S(2)}, u32[]{:S(2)}) %all-to-all-start.3) | async-done | bytes 524320 | tf_op jit(solution)/shard_map/all_to_all | solution.py:319
  96.3 0.1 finish.1
  96.5 34.1 %all_to_all.26.parts_ref = bf16[16,3,32,256]{3,2,1,0:T(8,128)(2,1)S(1)} all-to-all(bf16[16,3,32,256]{3,2,1,0:T(8,128)(2,1)S(1)} %finish.1), channel_id=1, replica_groups=mesh['chain'=16,'heads'=16] {'heads'}, dimensions={0} | all-to-all | bytes 1572864 | tf_op jit(solution)/shard_map/all_to_all | solution.py:319
  130.6 1.3 lay.1
Async XLA Ops:
  0.6 9.8 %copy-start = (bf16[512,256]{1,0:T(8,128)(2,1)S(1)}, bf16[512,256]{1,0:T(8,128)(2,1)}, u32[]{:S(2)}) copy-start(bf16[512,256]{1,0:T(8,128)(2,1)} %key_ref.3) | copy-start | bytes 786436
  0.6 9.8 %copy-start.1 = (bf16[512,256]{1,0:T(8,128)(2,1)S(1)}, bf16[512,256]{1,0:T(8,128)(2,1)}, u32[]{:S(2)}) copy-start(bf16[512,256]{1,0:T(8,128)(2,1)} %value_ref.3) | copy-start | bytes 786436
  0.7 9.5 %copy-start.6 = (s32[16,2,3]{0,1,2:T(2,128)S(1)}, s32[16,2,3]{0,1,2:T(2,128)}, u32[]{:S(2)}) copy-start(s32[16,2,3]{0,1,2:T(2,128)} %param.9) | copy-start | bytes 1156
  0.7 9.8 %copy-start.3 = (bf16[512,256]{1,0:T(8,128)(2,1)S(1)}, bf16[512,256]{1,0:T(8,128)(2,1)}, u32[]{:S(2)}) copy-start(bf16[512,256]{1,0:T(8,128)(2,1)} %grad_ref.5) | copy-start | bytes 786436
  0.7 9.8 %copy-start.2 = (bf16[512,256]{1,0:T(8,128)(2,1)S(1)}, bf16[512,256]{1,0:T(8,128)(2,1)}, u32[]{:S(2)}) copy-start(bf16[512,256]{1,0:T(8,128)(2,1)} %query_ref.5) | copy-start | bytes 786436
  2.6 18.1 %all-to-all-start = ((bf16[16,2,32,256]{3,2,1,0:T(8,128)(2,1)}), bf16[16,2,32,256]{3,2,1,0:T(8,128)(2,1)S(1)}, u32[]{:S(2)}, u32[]{:S(2)}) async-start(bf16[16,2,32,256]{3,2,1,0:T(8,128)(2,1)} %stack.1), calls=%async_computation | async-start | bytes 1048576 | tf_op jit(solution)/shard_map/all_to_all | solution.py:319
  22.6 24.3 %all-to-all-start.1 = ((bf16[16,2,3,32,256]{4,3,2,1,0:T(8,128)(2,1)}), bf16[16,2,3,32,256]{4,3,2,1,0:T(8,128)(2,1)S(1)}, u32[]{:S(2)}, u32[]{:S(2)}) async-start(bf16[16,2,3,32,256]{4,3,2,1,0:T(8,128)(2,1)} %pick.1), calls=%async_computation.1 | async-start | bytes 3145728 | tf_op jit(solution)/shard_map/all_to_all | solution.py:319
  54.3 27.1 %copy-start.4 = (f32[2,128,512]{2,1,0:T(8,128)}, f32[2,128,512]{2,1,0:T(8,128)S(1)}, u32[]{:S(2)}) copy-start(f32[2,128,512]{2,1,0:T(8,128)S(1)} %get-tuple-element.12.part_ref) | copy-start | bytes 1572868
  83.2 13.2 %all-to-all-start.3 = ((bf16[16,2,32,256]{3,2,1,0:T(8,128)(2,1)}), bf16[16,2,32,256]{3,2,1,0:T(8,128)(2,1)S(1)}, u32[]{:S(2)}, u32[]{:S(2)}) async-start(bf16[16,2,32,256]{3,2,1,0:T(8,128)(2,1)} %reduce.1), calls=%async_computation.3 | async-start | bytes 1048576 | tf_op jit(solution)/shard_map/all_to_all | solution.py:319
  86.7 1.0 copy-start.5

commit v9 on v8

--- a/solution.py
+++ b/solution.py
@@ -158,11 +158,15 @@
     stats_ref,
     rows_ref,
     sem,
-    *scratch,
+    score_ref,
+    grad_prob_ref,
+    prob_ref,
+    grad_score_ref,
 ):
     heads, _, rows = own_stats_ref.shape
     chunks, _, _, chunk, _ = listed_ref.shape
     block = position_ref[0]
+    tiles = rows // TILE
     copies = [
         pltpu.make_async_copy(source, rows_ref.at[index], sem.at[index])
         for index, source in enumerate((query_ref, grad_ref))
@@ -170,75 +174,69 @@
     for copy in copies:
         copy.start()
 
-    def listed(which, head):
-        return listed_ref[:, which, :, :, head_columns(head)].reshape(TOPK * rows, HEAD_DIM)
-
-    def one_slot(which, slot, head):
-        return listed_ref[:, which, slot, :, head_columns(head)].reshape(rows, HEAD_DIM)
-
-    def softmax(head):
-        raised_ref, prob_ref, grad_score_ref = scratch[3 * head : 3 * head + 3]
+    def listed(which, slot, columns):
+        return listed_ref[:, which, slot, :, columns].reshape(rows, HEAD_DIM)
+
+    def softmax(index, carry):
+        head, at = index // tiles, index % tiles
+        columns = head_columns(head)
+        tile = pl.ds(pl.multiple_of(at * TILE, TILE), TILE)
         live = [
             selection_ref[(block * heads + head) * TOPK + slot] < block for slot in range(TOPK)
         ]
-        for first in range(0, rows, TILE):
-            tile = pl.ds(first, TILE)
-            query, grad = turned_ref[0, head, :, tile], turned_ref[1, head, :, tile]
-            scores = dot(listed(0, head), query, 1, 0).reshape(chunks, TOPK, chunk, TILE)
-            top = jnp.full((1, TILE), MASKED, jnp.float32)
-            for slot in range(TOPK):
-                highest = jnp.max(scores[:, slot].reshape(rows, TILE), axis=0, keepdims=True)
-                top = jnp.maximum(top, jnp.where(live[slot], highest, MASKED))
-            total = jnp.zeros((SUBLANES, TILE), jnp.float32)
-            product = jnp.zeros_like(total)
-            for slot in range(TOPK):
-                shift = jnp.where(live[slot], top, -MASKED)
-                scores = dot(one_slot(0, slot, head), query, 1, 0)
-                raised = jnp.exp2((scores - shift) * EXPONENT)
-                raised_ref[slot, :, tile] = raised
-                total += fold(raised)
-                product += fold(raised * dot(one_slot(1, slot, head), grad, 1, 0))
-            total = jnp.sum(total, axis=0, keepdims=True)
-            product = jnp.sum(product, axis=0, keepdims=True)
-            own_top = own_stats_ref[head, 0:1, tile]
-            highest = jnp.maximum(own_top, top)
-            own_factor = jnp.exp2((own_top - highest) * EXPONENT)
-            factor = jnp.exp2((top - highest) * EXPONENT)
-            inverse = 1.0 / (own_factor * own_stats_ref[head, 1:2, tile] + factor * total)
-            own_weight, weight = own_factor * inverse, factor * inverse
-            delta = own_weight * own_stats_ref[head, 2:3, tile] + weight * product
-            stats_ref[head, 0:1, tile] = own_weight
-            stats_ref[head, 1:2, tile] = delta
-            for slot in range(TOPK):
-                probability = raised_ref[slot, :, tile] * weight
-                prob_ref[slot, :, tile] = probability.astype(jnp.bfloat16)
-                grad_probs = dot(one_slot(1, slot, head), grad, 1, 0)
-                grad_score_ref[slot, :, tile] = (probability * (grad_probs - delta)).astype(
-                    jnp.bfloat16
-                )
-
-    def gradients(head):
-        _, prob_ref, grad_score_ref = scratch[3 * head : 3 * head + 3]
+        query, grad = turned_ref[0, head, :, tile], turned_ref[1, head, :, tile]
+        top = jnp.full((1, TILE), MASKED, jnp.float32)
+        for slot in range(TOPK):
+            scores = dot(listed(0, slot, columns), query, 1, 0)
+            score_ref[slot] = scores
+            highest = jnp.max(scores, axis=0, keepdims=True)
+            top = jnp.maximum(top, jnp.where(live[slot], highest, MASKED))
+        total = jnp.zeros((SUBLANES, TILE), jnp.float32)
+        product = jnp.zeros_like(total)
+        for slot in range(TOPK):
+            shift = jnp.where(live[slot], top, -MASKED)
+            raised = jnp.exp2((score_ref[slot] - shift) * EXPONENT)
+            score_ref[slot] = raised
+            grad_probs = dot(listed(1, slot, columns), grad, 1, 0)
+            grad_prob_ref[slot] = grad_probs
+            total += fold(raised)
+            product += fold(raised * grad_probs)
+        total = jnp.sum(total, axis=0, keepdims=True)
+        product = jnp.sum(product, axis=0, keepdims=True)
+        own_top = own_stats_ref[head, 0:1, tile]
+        highest = jnp.maximum(own_top, top)
+        own_factor = jnp.exp2((own_top - highest) * EXPONENT)
+        factor = jnp.exp2((top - highest) * EXPONENT)
+        inverse = 1.0 / (own_factor * own_stats_ref[head, 1:2, tile] + factor * total)
+        own_weight, weight = own_factor * inverse, factor * inverse
+        delta = own_weight * own_stats_ref[head, 2:3, tile] + weight * product
+        stats_ref[head, 0:1, tile] = own_weight
+        stats_ref[head, 1:2, tile] = delta
+        for slot in range(TOPK):
+            probability = score_ref[slot] * weight
+            prob_ref[head, slot, :, tile] = probability.astype(jnp.bfloat16)
+            grad_score_ref[head, slot, :, tile] = (
+                probability * (grad_prob_ref[slot] - delta)
+            ).astype(jnp.bfloat16)
+        return carry
+
+    def gradients(index, carry):
+        head, slot = index // TOPK, index % TOPK
         columns = head_columns(head)
-        query, grad = rows_ref[0, :, columns], rows_ref[1, :, columns]
         shape = (chunks, chunk, HEAD_DIM)
-        part = None
-        for slot in range(TOPK):
-            grad_scores = grad_score_ref[slot]
-            grad_key = dot(grad_scores, query, 1, 0) * SCALING
-            terms_ref[:, 0, slot, :, columns] = grad_key.astype(jnp.bfloat16).reshape(shape)
-            grad_value = dot(prob_ref[slot], grad, 1, 0)
-            terms_ref[:, 1, slot, :, columns] = grad_value.astype(jnp.bfloat16).reshape(shape)
-            product = dot(one_slot(0, slot, head).T, grad_scores, 1, 0)
-            part = product if part is None else part + product
-        part_ref[head] = part
-
-    for head in range(heads):
-        softmax(head)
-        if head == 0:
-            for copy in copies:
-                copy.wait()
-        gradients(head)
+        grad_scores = grad_score_ref[head, slot]
+        grad_key = dot(grad_scores, rows_ref[0, :, columns], 1, 0) * SCALING
+        terms_ref[:, 0, slot, :, columns] = grad_key.astype(jnp.bfloat16).reshape(shape)
+        grad_value = dot(prob_ref[head, slot], rows_ref[1, :, columns], 1, 0)
+        terms_ref[:, 1, slot, :, columns] = grad_value.astype(jnp.bfloat16).reshape(shape)
+        part_ref[head] += dot(listed(0, slot, columns).T, grad_scores, 1, 0)
+        return carry
+
+    part_ref[...] = jnp.zeros_like(part_ref)
+    lax.fori_loop(0, heads * tiles, softmax, 0)
+    for copy in copies:
+        copy.wait()
+    lax.fori_loop(0, heads * TOPK, gradients, 0)
 
 
 def own_backward_kernel(
@@ -383,13 +381,14 @@
             jax.ShapeDtypeStruct((heads, HEAD_DIM, rows), full),
             jax.ShapeDtypeStruct((heads, STATS, rows), full),
         ),
-        [pltpu.VMEM((2, rows, width), low), pltpu.SemaphoreType.DMA((2,))]
-        + [
-            pltpu.VMEM((TOPK, rows, rows), full),
-            pltpu.VMEM((TOPK, rows, rows), low),
-            pltpu.VMEM((TOPK, rows, rows), low),
-        ]
-        * heads,
+        [
+            pltpu.VMEM((2, rows, width), low),
+            pltpu.SemaphoreType.DMA((2,)),
+            pltpu.VMEM((TOPK, rows, TILE), full),
+            pltpu.VMEM((TOPK, rows, TILE), full),
+            pltpu.VMEM((heads, TOPK, rows, rows), low),
+            pltpu.VMEM((heads, TOPK, rows, rows), low),
+        ],
         limit=32,
         slots=5 * TOPK,
     )(listed, position, turned, query_input, grad_output, slots, own_stats)

time: 132 us -> 133 us (level)
  no operation moved by 1% of the time
where the time goes in v9:
time: 133 us
  blocking collectives  61.2 us (46%)
  waiting for transfers between devices  35 us (26%)
  Pallas kernels  19.7 us (15%)
  starting transfers between devices  14.9 us (11%)
    all_to_all x2, blocking collectives, swap(): return lax.all_to_all(array, axis, split_axis=0, concat_axis=0, tiled=True)  61.2 us
    all_to_all x3, waiting for transfers between devices, swap(): return lax.all_to_all(array, axis, split_axis=0, concat_axis=0, tiled=True)  35 us
    all_to_all x3, starting transfers between devices, swap(): return lax.all_to_all(array, axis, split_axis=0, concat_axis=0, tiled=True)  14.9 us
    pallas_call x1, Pallas kernels, on_device(): call(far_kernel, 'far', [smem, smem, vmem, anywhere, anywhere, vmem, vmem...  8.54 us
  transfers between devices with their start and end apart: 3, of which 3 were waited for; matrix products, arithmetic and copies ran while one was open for 0% of the time, Pallas kernels for 3%

profile of v9, /device:TPU:1, one launch (start us, length us, event | category | flops | bytes accessed | tf_op | source)
XLA Modules:
  0.0 132.9 jit_solution(8698405222467816653)
XLA Ops:
  0.6 0.0 copy-start
  0.6 0.0 copy-start.1
  0.7 0.0 copy-start.6
  0.7 0.0 copy-start.3
  0.7 0.0 copy-start.2
  0.7 1.9 %stack.1 = bf16[16,2,32,256]{3,2,1,0:T(8,128)(2,1)} custom-call(bf16[16,32,256]{2,1,0:T(8,128)(2,1)} %bitcast.3, bf16[16,32,256]{2,1,0:T(8,128)(2,1)} %bitcast.4), custom_call_target="tpu_custom_call" | custom-call | bytes 4194304 | tf_op jit(solution)/shard_map/stack/pallas_call | solution.py:334
  2.6 7.6 %all-to-all-start = ((bf16[16,2,32,256]{3,2,1,0:T(8,128)(2,1)}), bf16[16,2,32,256]{3,2,1,0:T(8,128)(2,1)S(1)}, u32[]{:S(2)}, u32[]{:S(2)}) async-start(bf16[16,2,32,256]{3,2,1,0:T(8,128)(2,1)} %stack.1), calls=%async_computation | async-start | bytes 1048576 | tf_op jit(solution)/shard_map/all_to_all | solution.py:317
  10.2 0.0 copy-done.6
  10.2 0.1 copy.9
  10.3 0.1 reshape.18.selection_ref
  10.4 0.0 copy-done
  10.4 0.0 copy-done.1
  10.4 0.0 copy-done.3
  10.4 0.0 copy-done.2
  10.4 2.4 %own_forward.1 = (s32[96]{0:T(128)S(1)}, bf16[2,2,128,512]{3,2,1,0:T(8,128)(2,1)S(1)}, f32[2,8,512]{2,1,0:T(8,128)S(1)}) custom-call(s32[96]{0:T(128)S(1)} %reshape.18.selection_ref, bf16[512,256]{1,0:T(8,128)(2,1)S(1)} %copy-done.2, bf16[512,256]{1,0:T(8,128)(2,1)S(1)} %copy-done, bf16[512,256]{1,0:T(8,128)(2,1)S(1)} %copy-done.1, ...), custom_call_target="tpu_custom_call" | custom-call | flops 268435456 | bytes 4194304 | tf_op jit(solution)/shard_map/own_forward/pallas_call | solution.py:348
  12.9 7.8 %all-to-all-done.held_ref = bf16[16,2,32,256]{3,2,1,0:T(8,128)(2,1)S(1)} async-done(((bf16[16,2,32,256]{3,2,1,0:T(8,128)(2,1)}), bf16[16,2,32,256]{3,2,1,0:T(8,128)(2,1)S(1)}, u32[]{:S(2)}, u32[]{:S(2)}) %all-to-all-start) | async-done | bytes 524320 | tf_op jit(solution)/shard_map/all_to_all | solution.py:317
  20.7 1.9 %pick.1 = bf16[16,2,3,32,256]{4,3,2,1,0:T(8,128)(2,1)} custom-call(s32[96]{0:T(128)S(1)} %get-tuple-element.9.selection_ref, bf16[16,2,32,256]{3,2,1,0:T(8,128)(2,1)S(1)} %all-to-all-done.held_ref), custom_call_target="tpu_custom_call" | custom-call | bytes 4194304 | tf_op jit(solution)/shard_map/pick/pallas_call | solution.py:362
  22.6 3.7 %all-to-all-start.1 = ((bf16[16,2,3,32,256]{4,3,2,1,0:T(8,128)(2,1)}), bf16[16,2,3,32,256]{4,3,2,1,0:T(8,128)(2,1)S(1)}, u32[]{:S(2)}, u32[]{:S(2)}) async-start(bf16[16,2,3,32,256]{4,3,2,1,0:T(8,128)(2,1)} %pick.1), calls=%async_computation.1 | async-start | bytes 3145728 | tf_op jit(solution)/shard_map/all_to_all | solution.py:317
  26.3 20.5 %all-to-all-done.1.listed_ref = bf16[16,2,3,32,256]{4,3,2,1,0:T(8,128)(2,1)S(1)} async-done(((bf16[16,2,3,32,256]{4,3,2,1,0:T(8,128)(2,1)}), bf16[16,2,3,32,256]{4,3,2,1,0:T(8,128)(2,1)S(1)}, u32[]{:S(2)}, u32[]{:S(2)}) %all-to-all-start.1) | async-done | bytes 1572896 | tf_op jit(solution)/shard_map/all_to_all | solution.py:317
  46.8 8.5 %far.1 = (bf16[16,2,3,32,256]{4,3,2,1,0:T(8,128)(2,1)S(1)}, f32[2,128,512]{2,1,0:T(8,128)S(1)}, f32[2,8,512]{2,1,0:T(8,128)S(1)}) custom-call(s32[96]{0:T(128)S(1)} %get-tuple-element.9.selection_ref, s32[1]{0:T(128)} %bitcast.position_ref, bf16[2,2,128,512]{3,2,1,0:T(8,128)(2,1)S(1)} %get-tuple-element.10.turned_ref, bf16[512,256]{1,0:T(8,128)(2,1)S(1)} %copy-done.2, ...), custom_call_target="tpu_custom_call" | custom-call | flops 2013265920 | bytes 4194304 | tf_op jit(solution)/shard_map/far/pallas_call | solution.py:374
  55.4 0.0 copy-start.4
  55.4 27.1 %all_to_all.25.terms_ref = bf16[16,2,3,32,256]{4,3,2,1,0:T(8,128)(2,1)S(1)} all-to-all(bf16[16,2,3,32,256]{4,3,2,1,0:T(8,128)(2,1)S(1)} %get-tuple-element.14), channel_id=1, replica_groups=mesh['chain'=16,'heads'=16] {'chain'}, dimensions={0} | all-to-all | bytes 3145728 | tf_op jit(solution)/shard_map/all_to_all | solution.py:317
  82.5 0.0 copy-done.4
  82.5 1.7 %reduce.1 = bf16[16,2,32,256]{3,2,1,0:T(8,128)(2,1)} custom-call(s32[96]{0:T(128)S(1)} %get-tuple-element.9.selection_ref, bf16[16,2,3,32,256]{4,3,2,1,0:T(8,128)(2,1)S(1)} %all_to_all.25.terms_ref), custom_call_target="tpu_custom_call" | custom-call | bytes 4194304 | tf_op jit(solution)/shard_map/reduce/pallas_call | solution.py:405
  84.2 3.6 %all-to-all-start.3 = ((bf16[16,2,32,256]{3,2,1,0:T(8,128)(2,1)}), bf16[16,2,32,256]{3,2,1,0:T(8,128)(2,1)S(1)}, u32[]{:S(2)}, u32[]{:S(2)}) async-start(bf16[16,2,32,256]{3,2,1,0:T(8,128)(2,1)} %reduce.1), calls=%async_computation.3 | async-start | bytes 1048576 | tf_op jit(solution)/shard_map/all_to_all | solution.py:317
  87.7 0.0 copy-start.5
  87.8 1.0 copy-done.5
  88.8 1.8 %own_backward.1.own_ref = bf16[16,3,32,256]{3,2,1,0:T(8,128)(2,1)S(1)} custom-call(bf16[512,256]{1,0:T(8,128)(2,1)S(1)} %copy-done.2, bf16[512,256]{1,0:T(8,128)(2,1)S(1)} %copy-done, bf16[512,256]{1,0:T(8,128)(2,1)S(1)} %copy-done.1, bf16[512,256]{1,0:T(8,128)(2,1)S(1)} %copy-done.3, f32[2,128,512]{2,1,0:T(8,128)S(1)} %copy-done.5, ...), custom_call_target="tpu_custom_call" | custom-call | flops 671088640 | bytes 4194304 | tf_op jit(solution)/shard_map/own_backward/pallas_call | solution.py:396
  90.6 6.7 %all-to-all-done.3.others_ref = bf16[16,2,32,256]{3,2,1,0:T(8,128)(2,1)S(1)} async-done(((bf16[16,2,32,256]{3,2,1,0:T(8,128)(2,1)}), bf16[16,2,32,256]{3,2,1,0:T(8,128)(2,1)S(1)}, u32[]{:S(2)}, u32[]{:S(2)}) %all-to-all-start.3) | async-done | bytes 524320 | tf_op jit(solution)/shard_map/all_to_all | solution.py:317
  97.3 0.1 finish.1
  97.5 34.1 %all_to_all.26.parts_ref = bf16[16,3,32,256]{3,2,1,0:T(8,128)(2,1)S(1)} all-to-all(bf16[16,3,32,256]{3,2,1,0:T(8,128)(2,1)S(1)} %finish.1), channel_id=1, replica_groups=mesh['chain'=16,'heads'=16] {'heads'}, dimensions={0} | all-to-all | bytes 1572864 | tf_op jit(solution)/shard_map/all_to_all | solution.py:317
  131.6 1.3 lay.1
Async XLA Ops:
  0.6 9.8 %copy-start = (bf16[512,256]{1,0:T(8,128)(2,1)S(1)}, bf16[512,256]{1,0:T(8,128)(2,1)}, u32[]{:S(2)}) copy-start(bf16[512,256]{1,0:T(8,128)(2,1)} %key_ref.3) | copy-start | bytes 786436
  0.6 9.8 %copy-start.1 = (bf16[512,256]{1,0:T(8,128)(2,1)S(1)}, bf16[512,256]{1,0:T(8,128)(2,1)}, u32[]{:S(2)}) copy-start(bf16[512,256]{1,0:T(8,128)(2,1)} %value_ref.3) | copy-start | bytes 786436
  0.7 9.5 %copy-start.6 = (s32[16,2,3]{0,1,2:T(2,128)S(1)}, s32[16,2,3]{0,1,2:T(2,128)}, u32[]{:S(2)}) copy-start(s32[16,2,3]{0,1,2:T(2,128)} %param.9) | copy-start | bytes 1156
  0.7 9.8 %copy-start.3 = (bf16[512,256]{1,0:T(8,128)(2,1)S(1)}, bf16[512,256]{1,0:T(8,128)(2,1)}, u32[]{:S(2)}) copy-start(bf16[512,256]{1,0:T(8,128)(2,1)} %grad_ref.5) | copy-start | bytes 786436
  0.7 9.8 %copy-start.2 = (bf16[512,256]{1,0:T(8,128)(2,1)S(1)}, bf16[512,256]{1,0:T(8,128)(2,1)}, u32[]{:S(2)}) copy-start(bf16[512,256]{1,0:T(8,128)(2,1)} %query_ref.5) | copy-start | bytes 786436
  2.6 18.1 %all-to-all-start = ((bf16[16,2,32,256]{3,2,1,0:T(8,128)(2,1)}), bf16[16,2,32,256]{3,2,1,0:T(8,128)(2,1)S(1)}, u32[]{:S(2)}, u32[]{:S(2)}) async-start(bf16[16,2,32,256]{3,2,1,0:T(8,128)(2,1)} %stack.1), calls=%async_computation | async-start | bytes 1048576 | tf_op jit(solution)/shard_map/all_to_all | solution.py:317
  22.6 24.3 %all-to-all-start.1 = ((bf16[16,2,3,32,256]{4,3,2,1,0:T(8,128)(2,1)}), bf16[16,2,3,32,256]{4,3,2,1,0:T(8,128)(2,1)S(1)}, u32[]{:S(2)}, u32[]{:S(2)}) async-start(bf16[16,2,3,32,256]{4,3,2,1,0:T(8,128)(2,1)} %pick.1), calls=%async_computation.1 | async-start | bytes 3145728 | tf_op jit(solution)/shard_map/all_to_all | solution.py:317
  55.4 27.1 %copy-start.4 = (f32[2,128,512]{2,1,0:T(8,128)}, f32[2,128,512]{2,1,0:T(8,128)S(1)}, u32[]{:S(2)}) copy-start(f32[2,128,512]{2,1,0:T(8,128)S(1)} %get-tuple-element.12.part_ref) | copy-start | bytes 1572868
  84.2 13.1 %all-to-all-start.3 = ((bf16[16,2,32,256]{3,2,1,0:T(8,128)(2,1)}), bf16[16,2,32,256]{3,2,1,0:T(8,128)(2,1)S(1)}, u32[]{:S(2)}, u32[]{:S(2)}) async-start(bf16[16,2,32,256]{3,2,1,0:T(8,128)(2,1)} %reduce.1), calls=%async_computation.3 | async-start | bytes 1048576 | tf_op jit(solution)/shard_map/all_to_all | solution.py:317
  87.7 1.0 copy-start.5

commit v10 on v6

--- a/solution.py
+++ b/solution.py
@@ -71,7 +71,7 @@
         copy.wait()
 
 
-def reduce_kernel(selection_ref, terms_ref, out_ref, *total_refs):
+def reduce_kernel(selection_ref, terms_ref, after_ref, out_ref, *total_refs):
     blocks, _, _, width = out_ref.shape
     heads = width // HEAD_DIM
     for head, total_ref in enumerate(total_refs):
@@ -158,6 +158,8 @@
     stats_ref,
     rows_ref,
     sem,
+    held_terms_ref,
+    terms_sem,
     *scratch,
 ):
     heads, _, rows = own_stats_ref.shape
@@ -226,21 +228,34 @@
         shape = (chunks, TOPK, chunk, HEAD_DIM)
         prob = prob_ref[...].reshape(TOPK * rows, rows)
         grad_scores = grad_score_ref[...].reshape(TOPK * rows, rows)
-        grad_key = dot(grad_scores, query, 1, 0) * SCALING
-        terms_ref[:, 0, :, :, columns] = grad_key.astype(jnp.bfloat16).reshape(shape)
-        grad_value = dot(prob, grad, 1, 0)
-        terms_ref[:, 1, :, :, columns] = grad_value.astype(jnp.bfloat16).reshape(shape)
+        for which in range(2):
+            if which == 0:
+                term = dot(grad_scores, query, 1, 0) * SCALING
+            else:
+                term = dot(prob, grad, 1, 0)
+            held_terms_ref[:, which, :, :, columns] = term.astype(jnp.bfloat16).reshape(shape)
+            copy = pltpu.make_async_copy(
+                held_terms_ref.at[:, which, :, :, columns],
+                terms_ref.at[:, which, :, :, columns],
+                terms_sem.at[head, which],
+            )
+            copy.start()
+            sent.append(copy)
         part_ref[head] = dot(listed(0, head).T, grad_scores, 1, 0)
 
+    sent = []
     for head in range(heads):
         softmax(head)
         if head == 0:
             for copy in copies:
                 copy.wait()
         gradients(head)
+    for copy in sent:
+        copy.wait()
 
 
 def own_backward_kernel(
+    place_ref,
     query_ref,
     key_ref,
     value_ref,
@@ -249,7 +264,9 @@
     own_stats_ref,
     stats_ref,
     own_ref,
+    *refs,
 ):
+    piece_refs, grad_query_ref = refs[:-1], refs[-1]
     heads, _, rows = stats_ref.shape
     chunks, _, chunk, _ = own_ref.shape
 
@@ -262,8 +279,9 @@
         probability = raised * stats_ref[head, 0:1, :]
         grad_probs = dot(value, grad, 1, 1)
         grad_scores = (probability * (grad_probs - stats_ref[head, 1:2, :])).astype(jnp.bfloat16)
+        grad_query = (part_ref[head] + dot(key.T, grad_scores, 1, 0)) * SCALING
+        grad_query_ref[:, columns] = grad_query.T.astype(jnp.bfloat16)
         results = (
-            ((part_ref[head] + dot(key.T, grad_scores, 1, 0)) * SCALING).T,
             dot(grad_scores, query, 1, 0) * SCALING,
             dot(probability.astype(jnp.bfloat16), grad, 1, 0),
         )
@@ -274,29 +292,53 @@
         return carry
 
     lax.fori_loop(0, heads, one_head, 0)
-
-
-def finish_kernel(own_ref, others_ref, out_ref):
-    out_ref[:, 0] = own_ref[:, 0]
-    out_ref[:, 1:] = (
-        others_ref[...].astype(jnp.float32) + own_ref[:, 1:].astype(jnp.float32)
+    planes = len(piece_refs)
+    plane = place_ref[1]
+    length = rows // planes
+    for step, piece_ref in enumerate(piece_refs):
+        first = pl.multiple_of(((plane + step) % planes) * length, length)
+        piece_ref[...] = grad_query_ref[pl.ds(first, length), :]
+
+
+def join_kernel(place_ref, *refs):
+    piece_refs, out_ref = refs[:-1], refs[-1]
+    share = out_ref.shape[1]
+    first = pl.multiple_of((1 - place_ref[2]) * share, share)
+    for step, piece_ref in enumerate(piece_refs):
+        out_ref[step] = piece_ref[pl.ds(first, share), :]
+
+
+def finish_kernel(own_ref, others_ref, after_ref, out_ref):
+    out_ref[...] = (
+        others_ref[...].astype(jnp.float32) + own_ref[...].astype(jnp.float32)
     ).astype(jnp.bfloat16)
 
 
-def lay_kernel(parts_ref, *refs):
-    outs, sem = refs[:-1], refs[-1]
-    senders, _, _, width = parts_ref.shape
-    copies = [
-        pltpu.make_async_copy(
-            parts_ref.at[sender, index],
-            out.at[:, pl.ds(sender * width, width)],
-            sem.at[index, sender],
-        )
-        for index, out in enumerate(outs)
-        for sender in range(senders)
-    ]
-    for copy in copies:
-        copy.start()
+def lay_kernel(place_ref, parts_ref, other_ref, *refs):
+    piece_refs, (query_ref, key_ref, value_ref, sem) = refs[:-4], refs[-4:]
+    senders, _, share, width = parts_ref.shape
+    planes = len(piece_refs)
+    cores = senders // planes
+    plane, core = place_ref[1], place_ref[2]
+    copies = []
+
+    def put(source, out, sender):
+        first = sender * width
+        if not isinstance(sender, int):
+            first = pl.multiple_of(first, width)
+        target = out.at[:, pl.ds(first, width)]
+        copies.append(pltpu.make_async_copy(source, target, sem.at[len(copies)]))
+        copies[-1].start()
+
+    for step, piece_ref in enumerate(piece_refs):
+        origin = (plane - step + planes) % planes
+        rows = pl.ds(pl.multiple_of(core * share, share), share)
+        put(piece_ref.at[rows], query_ref, origin * cores + core)
+        if cores > 1:
+            put(other_ref.at[step], query_ref, origin * cores + 1 - core)
+    for sender in range(senders):
+        put(parts_ref.at[sender, 0], key_ref, sender)
+        put(parts_ref.at[sender, 1], value_ref, sender)
     for copy in copies:
         copy.wait()
 
@@ -308,7 +350,10 @@
     chunk = rows // chain
     share = rows // spread
     listed = selection.reshape(-1)
-    position = lax.axis_index("chain").astype(jnp.int32).reshape(1)
+    cores = 2 if spread % 2 == 0 else 1
+    planes = spread // cores
+    at = lax.axis_index("heads")
+    position = jnp.stack([lax.axis_index("chain"), at // cores, at % cores]).astype(jnp.int32)
     smem = pl.BlockSpec(memory_space=pltpu.SMEM)
     vmem = pl.BlockSpec(memory_space=pltpu.VMEM)
     anywhere = pl.BlockSpec(memory_space=pl.ANY)
@@ -376,13 +421,18 @@
         far_kernel,
         "far",
         [smem, smem, vmem, anywhere, anywhere, vmem, vmem],
-        (vmem, vmem, vmem),
+        (anywhere, vmem, vmem),
         (
             jax.ShapeDtypeStruct((chain, 2, TOPK, chunk, width), low),
             jax.ShapeDtypeStruct((heads, HEAD_DIM, rows), full),
             jax.ShapeDtypeStruct((heads, STATS, rows), full),
         ),
-        [pltpu.VMEM((2, rows, width), low), pltpu.SemaphoreType.DMA((2,))]
+        [
+            pltpu.VMEM((2, rows, width), low),
+            pltpu.SemaphoreType.DMA((2,)),
+            pltpu.VMEM((chain, 2, TOPK, chunk, width), low),
+            pltpu.SemaphoreType.DMA((heads, 2)),
+        ]
         + [
             pltpu.VMEM((chain, TOPK, chunk, rows), full),
             pltpu.VMEM((chain, TOPK, chunk, rows), full),
@@ -394,23 +444,44 @@
         slots=5 * TOPK,
     )(listed, position, turned, query_input, grad_output, slots, own_stats)
     returned = swap(terms, "chain")
-    own = call(
+    own, *pieces = call(
         own_backward_kernel,
         "own_backward",
-        [vmem] * 7,
-        vmem,
-        jax.ShapeDtypeStruct((chain, 3, chunk, width), low),
+        [smem] + [vmem] * 7,
+        (vmem,) * (1 + planes),
+        (jax.ShapeDtypeStruct((chain, 2, chunk, width), low),)
+        + (jax.ShapeDtypeStruct((rows // planes, width), low),) * planes,
+        [pltpu.VMEM((rows, width), low)],
         limit=12,
         slots=5,
-    )(query_input, key_input, value_input, grad_output, part, own_stats, stats)
+    )(position, query_input, key_input, value_input, grad_output, part, own_stats, stats)
+
+    def to_plane(piece, step):
+        if step == 0:
+            return piece
+        pairs = [(one, (one + step * cores) % spread) for one in range(spread)]
+        return lax.ppermute(piece, "heads", pairs)
+
+    for step in sorted(range(planes), key=lambda step: -min(step, planes - step)):
+        pieces[step] = to_plane(pieces[step], step)
+    joined = other = pieces[0]
+    if cores > 1:
+        joined = call(
+            join_kernel,
+            "join",
+            [smem] + [vmem] * planes,
+            vmem,
+            jax.ShapeDtypeStruct((planes, share, width), low),
+        )(position, *pieces)
+        other = lax.ppermute(joined, "heads", [(one, one ^ 1) for one in range(spread)])
     summed = call(
         reduce_kernel,
         "reduce",
-        [smem, vmem],
+        [smem, vmem, anywhere],
         vmem,
         jax.ShapeDtypeStruct((chain, 2, chunk, width), low),
         [pltpu.VMEM((chain, 2, chunk, HEAD_DIM), full)] * heads,
-    )(listed, returned)
+    )(listed, returned, joined)
     others = swap(summed, "chain")
 
     def by_share(array):
@@ -421,19 +492,19 @@
     whole = call(
         finish_kernel,
         "finish",
-        [vmem] * 2,
+        [vmem] * 2 + [anywhere],
         vmem,
-        jax.ShapeDtypeStruct((spread, 3, share, width), low),
-    )(by_share(own), by_share(others))
+        jax.ShapeDtypeStruct((spread, 2, share, width), low),
+    )(by_share(own), by_share(others), other)
     whole = swap(whole, "heads")
     return call(
         lay_kernel,
         "lay",
-        [vmem],
+        [smem] + [vmem] * (2 + planes),
         (anywhere,) * 3,
         (jax.ShapeDtypeStruct((share, spread * width), low),) * 3,
-        [pltpu.SemaphoreType.DMA((3, spread))],
-    )(whole)
+        [pltpu.SemaphoreType.DMA((3 * spread,))],
+    )(position, whole, other, *pieces)
 
 
 def solution(mesh):

time: 132 us -> 132 us (level)
  blocking collectives: 61.2 us -> 25.9 us
  starting transfers between devices: 14.9 us -> 44.3 us
  Pallas kernels: 18 us -> 20.8 us
  local copies, waits for them, and re-layouts: 1.27 us -> 3.09 us
    all_to_all x2 -> x1, blocking collectives: 61.2 us -> 25.9 us  [swap(): return lax.all_to_all(array, axis, split_axis=0, concat_axis=0, tiled=True)]
    ppermute x0 -> x8, starting transfers between devices: none -> 20.8 us  [the longest x7 16.5 us: to_plane(): return lax.ppermute(piece, 'heads', pairs)]
    all_to_all x3 -> x4, starting transfers between devices: 14.9 us -> 23.4 us  [swap(): return lax.all_to_all(array, axis, split_axis=0, concat_axis=0, tiled=True)]
    ppermute x0 -> x8, waiting for transfers between devices: none -> 4.26 us  [the longest x7 3.27 us: to_plane(): return lax.ppermute(piece, 'heads', pairs)]
    all_to_all x3 -> x4, waiting for transfers between devices: 35 us -> 32 us  [swap(): return lax.all_to_all(array, axis, split_axis=0, concat_axis=0, tiled=True)]
    unnamed x15 -> x19, local copies, waits for them, and re-layouts: 1.16 us -> 2.98 us
    pallas_call x4 -> x5, Pallas kernels: 4.95 us -> 6.63 us  [the longest x1 2.4 us: on_device(): call(own_backward_kernel, 'own_backward', [smem] + [vmem] * 7, (vmem,) *...]
  transfers between devices with their start and end apart: 3 -> 12, of which waited for: 3 -> 6; matrix products, arithmetic and copies ran while one was open for 0% -> 0% of each run, Pallas kernels for 3% -> 4%
where the time goes in v10:
time: 132 us
  starting transfers between devices  44.3 us (34%)
  waiting for transfers between devices  36.3 us (27%)
  blocking collectives  25.9 us (20%)
  Pallas kernels  20.8 us (16%)
  local copies, waits for them, and re-layouts  3.09 us (2%)
    all_to_all x4, waiting for transfers between devices, swap(): return lax.all_to_all(array, axis, split_axis=0, concat_axis=0, tiled=True)  32 us
    all_to_all x1, blocking collectives, swap(): return lax.all_to_all(array, axis, split_axis=0, concat_axis=0, tiled=True)  25.9 us
    all_to_all x4, starting transfers between devices, swap(): return lax.all_to_all(array, axis, split_axis=0, concat_axis=0, tiled=True)  23.4 us
    ppermute x7, starting transfers between devices, to_plane(): return lax.ppermute(piece, 'heads', pairs)  16.5 us
    pallas_call x1, Pallas kernels, on_device(): call(far_kernel, 'far', [smem, smem, vmem, anywhere, anywhere, vmem, vmem...  7.96 us
    ppermute x1, starting transfers between devices, on_device(): lax.ppermute(joined, 'heads', [(one, one ^ 1) for one in range(spread)])  4.33 us
    ppermute x7, waiting for transfers between devices, to_plane(): return lax.ppermute(piece, 'heads', pairs)  3.27 us
    unnamed x19, local copies, waits for them, and re-layouts  2.98 us
  transfers between devices with their start and end apart: 12, of which 6 were waited for; matrix products, arithmetic and copies ran while one was open for 0% of the time, Pallas kernels for 4%

profile of v10, /device:TPU:1, one launch (start us, length us, event | category | flops | bytes accessed | tf_op | source)
XLA Modules:
  0.0 131.5 jit_solution(458885395620836454)
XLA Ops:
  0.6 0.0 copy-start
  0.6 0.0 copy-start.1
  0.7 0.0 copy-start.8
  0.7 0.0 copy-start.3
  0.7 0.0 copy-start.2
  0.7 1.9 %stack.17 = bf16[16,2,32,256]{3,2,1,0:T(8,128)(2,1)} custom-call(bf16[16,32,256]{2,1,0:T(8,128)(2,1)} %bitcast.5, bf16[16,32,256]{2,1,0:T(8,128)(2,1)} %bitcast.6), custom_call_target="tpu_custom_call" | custom-call | bytes 4194304 | tf_op jit(solution)/shard_map/stack/pallas_call | solution.py:380
  2.6 7.6 %all-to-all-start = ((bf16[16,2,32,256]{3,2,1,0:T(8,128)(2,1)}), bf16[16,2,32,256]{3,2,1,0:T(8,128)(2,1)S(1)}, u32[]{:S(2)}, u32[]{:S(2)}) async-start(bf16[16,2,32,256]{3,2,1,0:T(8,128)(2,1)} %stack.17), calls=%async_computation | async-start | bytes 1048576 | tf_op jit(solution)/shard_map/all_to_all | solution.py:363
  10.2 0.0 copy-done.8
  10.2 0.1 copy.9
  10.3 0.1 reshape.15.selection_ref
  10.4 0.0 copy-done
  10.4 0.0 copy-done.1
  10.5 0.0 copy-done.3
  10.5 0.0 copy-done.2
  10.5 2.4 %own_forward.1 = (s32[96]{0:T(128)S(1)}, bf16[2,2,128,512]{3,2,1,0:T(8,128)(2,1)S(1)}, f32[2,8,512]{2,1,0:T(8,128)S(1)}) custom-call(s32[96]{0:T(128)S(1)} %reshape.15.selection_ref, bf16[512,256]{1,0:T(8,128)(2,1)S(1)} %copy-done.2, bf16[512,256]{1,0:T(8,128)(2,1)S(1)} %copy-done, bf16[512,256]{1,0:T(8,128)(2,1)S(1)} %copy-done.1, ...), custom_call_target="tpu_custom_call" | custom-call | flops 268435456 | bytes 4194304 | tf_op jit(solution)/shard_map/own_forward/pallas_call | solution.py:394
  12.9 0.0 copy-start.4
  12.9 7.8 %all-to-all-done.held_ref = bf16[16,2,32,256]{3,2,1,0:T(8,128)(2,1)S(1)} async-done(((bf16[16,2,32,256]{3,2,1,0:T(8,128)(2,1)}), bf16[16,2,32,256]{3,2,1,0:T(8,128)(2,1)S(1)}, u32[]{:S(2)}, u32[]{:S(2)}) %all-to-all-start) | async-done | bytes 524320 | tf_op jit(solution)/shard_map/all_to_all | solution.py:363
  20.7 1.9 %pick.1 = bf16[16,2,3,32,256]{4,3,2,1,0:T(8,128)(2,1)} custom-call(s32[96]{0:T(128)S(1)} %get-tuple-element.18.selection_ref, bf16[16,2,32,256]{3,2,1,0:T(8,128)(2,1)S(1)} %all-to-all-done.held_ref), custom_call_target="tpu_custom_call" | custom-call | bytes 4194304 | tf_op jit(solution)/shard_map/pick/pallas_call | solution.py:408
  22.6 0.0 copy-done.4
  22.6 3.7 %all-to-all-start.1 = ((bf16[16,2,3,32,256]{4,3,2,1,0:T(8,128)(2,1)}), bf16[16,2,3,32,256]{4,3,2,1,0:T(8,128)(2,1)S(1)}, u32[]{:S(2)}, u32[]{:S(2)}) async-start(bf16[16,2,3,32,256]{4,3,2,1,0:T(8,128)(2,1)} %pick.1), calls=%async_computation.1 | async-start | bytes 3145728 | tf_op jit(solution)/shard_map/all_to_all | solution.py:363
  26.4 0.1 pad_add_fusion.position_ref.place_ref
  26.4 20.4 %all-to-all-done.1.listed_ref = bf16[16,2,3,32,256]{4,3,2,1,0:T(8,128)(2,1)S(1)} async-done(((bf16[16,2,3,32,256]{4,3,2,1,0:T(8,128)(2,1)}), bf16[16,2,3,32,256]{4,3,2,1,0:T(8,128)(2,1)S(1)}, u32[]{:S(2)}, u32[]{:S(2)}) %all-to-all-start.1) | async-done | bytes 1572896 | tf_op jit(solution)/shard_map/all_to_all | solution.py:363
  46.9 0.0 copy-start.5
  46.9 1.0 copy-done.5
  47.9 8.0 %far.1 = (bf16[16,2,3,32,256]{4,3,2,1,0:T(8,128)(2,1)}, f32[2,128,512]{2,1,0:T(8,128)S(1)}, f32[2,8,512]{2,1,0:T(8,128)S(1)}) custom-call(s32[96]{0:T(128)S(1)} %get-tuple-element.18.selection_ref, s32[3]{0:T(128)S(1)} %pad_add_fusion.position_ref.place_ref, bf16[2,2,128,512]{3,2,1,0:T(8,128)(2,1)S(1)} %copy-done.5, bf16[512,256]{1,0:T(8,128)(2,1)S(1)} %copy-done.2, ...), custom_call_target="tpu_custom_call" | custom-call | flops 2013265920 | bytes 4194304 | tf_op jit(solution)/shard_map/far/pallas_call | solution.py:420
  55.9 0.0 copy-start.6
  55.9 0.8 copy-done.6
  56.7 5.6 %all-to-all-start.2 = ((bf16[16,2,3,32,256]{4,3,2,1,0:T(8,128)(2,1)}), bf16[16,2,3,32,256]{4,3,2,1,0:T(8,128)(2,1)S(1)}, u32[]{:S(2)}, u32[]{:S(2)}) async-start(bf16[16,2,3,32,256]{4,3,2,1,0:T(8,128)(2,1)} %get-tuple-element.24), calls=%async_computation.2 | async-start | bytes 3145728 | tf_op jit(solution)/shard_map/all_to_all | solution.py:363
  62.3 0.0 copy-start.7
  62.3 1.0 copy-done.7
  63.3 2.4 %own_backward.1 = (bf16[16,2,32,256]{3,2,1,0:T(8,128)(2,1)S(1)}, bf16[64,256]{1,0:T(8,128)(2,1)S(1)}, bf16[64,256]{1,0:T(8,128)(2,1)S(1)}, bf16[64,256]{1,0:T(8,...) custom-call(s32[3]{0:T(128)S(1)} %pad_add_fusion.position_ref.place_, ...), custom_call_target="tpu_custom_call" | custom-call | flops 671088640 | bytes 4194304 | tf_op jit(solution)/shard_map/own_backward/pallas_call | solution.py:447
  65.7 1.7 %collective-permute-start = (bf16[64,256]{1,0:T(8,128)(2,1)S(1)}, bf16[64,256]{1,0:T(8,128)(2,1)S(1)}, u32[]{:S(2)}, u32[]{:S(2)}) collective-permute-start(bf16[64,256]{1,0:T(8,128)(2,1)S(1)} %get-tuple-element.26), channel_id=1, source_target_pairs={{0,2},{1,3},{2,4},{3,5},{4,6},{5,7},{6,8},{7,9},{8,10},{9,11},{10,... | collective-permute-start | bytes 98312 | tf_op jit(solution)/shard_map/ppermute | solution.py:463
  67.5 3.0 %collective-permute-start.1 = (bf16[64,256]{1,0:T(8,128)(2,1)S(1)}, bf16[64,256]{1,0:T(8,128)(2,1)S(1)}, u32[]{:S(2)}, u32[]{:S(2)}) collective-permute-start(bf16[64,256]{1,0:T(8,128)(2,1)S(1)} %get-tuple-element.27), channel_id=1, source_target_pairs={{0,4},{1,5},{2,6},{3,7},{4,8},{5,9},{6,10},{7,11},{8,12},{9,13},{1... | collective-permute-start | bytes 98312 | tf_op jit(solution)/shard_map/ppermute | solution.py:463
  70.5 3.7 %collective-permute-start.2 = (bf16[64,256]{1,0:T(8,128)(2,1)S(1)}, bf16[64,256]{1,0:T(8,128)(2,1)S(1)}, u32[]{:S(2)}, u32[]{:S(2)}) collective-permute-start(bf16[64,256]{1,0:T(8,128)(2,1)S(1)} %get-tuple-element.28), channel_id=1, source_target_pairs={{0,6},{1,7},{2,8},{3,9},{4,10},{5,11},{6,12},{7,13},{8,14},{9,15},... | collective-permute-start | bytes 98312 | tf_op jit(solution)/shard_map/ppermute | solution.py:463
  74.2 0.4 collective-permute-start.3
  74.7 4.5 %collective-permute-start.4 = (bf16[64,256]{1,0:T(8,128)(2,1)S(1)}, bf16[64,256]{1,0:T(8,128)(2,1)S(1)}, u32[]{:S(2)}, u32[]{:S(2)}) collective-permute-start(bf16[64,256]{1,0:T(8,128)(2,1)S(1)} %get-tuple-element.30), channel_id=1, source_target_pairs={{0,10},{1,11},{2,12},{3,13},{4,14},{5,15},{6,0},{7,1},{8,2},{9,3},... | collective-permute-start | bytes 98312 | tf_op jit(solution)/shard_map/ppermute | solution.py:463
  79.1 0.0 collective-permute-done.refs_1_
  79.1 2.4 %collective-permute-start.5 = (bf16[64,256]{1,0:T(8,128)(2,1)S(1)}, bf16[64,256]{1,0:T(8,128)(2,1)S(1)}, u32[]{:S(2)}, u32[]{:S(2)}) collective-permute-start(bf16[64,256]{1,0:T(8,128)(2,1)S(1)} %get-tuple-element.31), channel_id=1, source_target_pairs={{0,12},{1,13},{2,14},{3,15},{4,0},{5,1},{6,2},{7,3},{8,4},{9,5},{1... | collective-permute-start | bytes 98312 | tf_op jit(solution)/shard_map/ppermute | solution.py:463
  81.5 0.0 collective-permute-done.1.refs_2_
  81.5 0.7 collective-permute-start.6
  82.3 0.0 collective-permute-done.2.refs_3_
  82.3 0.0 collective-permute-done.3.refs_4_
  82.3 0.0 collective-permute-done.4.refs_5_
  82.3 1.0 collective-permute-done.5.refs_6_
  83.3 2.3 %collective-permute-done.6.refs_7_ = bf16[64,256]{1,0:T(8,128)(2,1)S(1)} collective-permute-done((bf16[64,256]{1,0:T(8,128)(2,1)S(1)}, bf16[64,256]{1,0:T(8,128)(2,1)S(1)}, u32[]{:S(2)}, u32[]{:S(2)}) %collective-permute-start.6) | collective-permute-done | bytes 32800 | tf_op jit(solution)/shard_map/ppermute | solution.py:463
  85.5 0.6 join.1.after_ref
  86.1 0.0 all-to-all-done.2.terms_ref
  86.1 1.7 %reduce.1 = bf16[16,2,32,256]{3,2,1,0:T(8,128)(2,1)} custom-call(s32[96]{0:T(128)S(1)} %get-tuple-element.18.selection_ref, bf16[16,2,3,32,256]{4,3,2,1,0:T(8,128)(2,1)S(1)} %all-to-all-done.2.terms_ref, bf16[8,32,256]{2,1,0:T(8,128)(2,1)S(1)} %join.1.after_ref), custom_call_target="tpu_custom_call" | custom-call | bytes 4194304 | tf_op jit(solution)/shard_map/reduce/pallas_call | solution.py:477
  87.8 6.5 %all-to-all-start.3 = ((bf16[16,2,32,256]{3,2,1,0:T(8,128)(2,1)}), bf16[16,2,32,256]{3,2,1,0:T(8,128)(2,1)S(1)}, u32[]{:S(2)}, u32[]{:S(2)}) async-start(bf16[16,2,32,256]{3,2,1,0:T(8,128)(2,1)} %reduce.1), calls=%async_computation.3 | async-start | bytes 1048576 | tf_op jit(solution)/shard_map/all_to_all | solution.py:363
  94.4 4.3 %collective-permute-start.7 = (bf16[8,32,256]{2,1,0:T(8,128)(2,1)S(1)}, bf16[8,32,256]{2,1,0:T(8,128)(2,1)S(1)}, u32[]{:S(2)}, u32[]{:S(2)}) collective-permute-start(bf16[8,32,256]{2,1,0:T(8,128)(2,1)S(1)} %join.1.after_ref), channel_id=1, source_target_pairs={{0,1},{1,0},{2,3},{3,2},{4,5},{5,4},{6,7},{7,6},{8,9},{9,8},{10,11... | collective-permute-start | bytes 393224 | tf_op jit(solution)/shard_map/ppermute | solution.py:476
  98.7 1.0 collective-permute-done.7.after_ref.other_ref
  99.7 3.8 %all-to-all-done.3.others_ref = bf16[16,2,32,256]{3,2,1,0:T(8,128)(2,1)S(1)} async-done(((bf16[16,2,32,256]{3,2,1,0:T(8,128)(2,1)}), bf16[16,2,32,256]{3,2,1,0:T(8,128)(2,1)S(1)}, u32[]{:S(2)}, u32[]{:S(2)}) %all-to-all-start.3) | async-done | bytes 524320 | tf_op jit(solution)/shard_map/all_to_all | solution.py:363
  103.5 0.1 finish.1
  103.6 25.9 %all_to_all.25.parts_ref = bf16[16,2,32,256]{3,2,1,0:T(8,128)(2,1)S(1)} all-to-all(bf16[16,2,32,256]{3,2,1,0:T(8,128)(2,1)S(1)} %finish.1), channel_id=1, replica_groups=mesh['chain'=16,'heads'=16] {'heads'}, dimensions={0} | all-to-all | bytes 1048576 | tf_op jit(solution)/shard_map/all_to_all | solution.py:363
  129.5 1.8 %lay.1 = (bf16[32,4096]{1,0:T(8,128)(2,1)}, bf16[32,4096]{1,0:T(8,128)(2,1)}, bf16[32,4096]{1,0:T(8,128)(2,1)}) custom-call(s32[3]{0:T(128)S(1)} %pad_add_fusion.position_ref.place_ref, bf16[16,2,32,256]{3,2,1,0:T(8,128)(2,1)S(1)} %all_to_all.25.parts_ref, bf16[8,32,256]{2,1,0:T(8,128)(2,1)S(1)} %collective-permute-done.7.after_ref.other_ref, ...), custom_call_target="tpu_custom_call" | custom-call | bytes 4194304 | tf_op jit(solution)/shard_map/lay/pallas_call | solution.py:500
Async XLA Ops:
  0.6 9.8 %copy-start = (bf16[512,256]{1,0:T(8,128)(2,1)S(1)}, bf16[512,256]{1,0:T(8,128)(2,1)}, u32[]{:S(2)}) copy-start(bf16[512,256]{1,0:T(8,128)(2,1)} %key_ref.3) | copy-start | bytes 786436
  0.6 9.8 %copy-start.1 = (bf16[512,256]{1,0:T(8,128)(2,1)S(1)}, bf16[512,256]{1,0:T(8,128)(2,1)}, u32[]{:S(2)}) copy-start(bf16[512,256]{1,0:T(8,128)(2,1)} %value_ref.3) | copy-start | bytes 786436
  0.7 9.6 %copy-start.8 = (s32[16,2,3]{0,1,2:T(2,128)S(1)}, s32[16,2,3]{0,1,2:T(2,128)}, u32[]{:S(2)}) copy-start(s32[16,2,3]{0,1,2:T(2,128)} %param.9) | copy-start | bytes 1156
  0.7 9.8 %copy-start.3 = (bf16[512,256]{1,0:T(8,128)(2,1)S(1)}, bf16[512,256]{1,0:T(8,128)(2,1)}, u32[]{:S(2)}) copy-start(bf16[512,256]{1,0:T(8,128)(2,1)} %grad_ref.5) | copy-start | bytes 786436
  0.7 9.8 %copy-start.2 = (bf16[512,256]{1,0:T(8,128)(2,1)S(1)}, bf16[512,256]{1,0:T(8,128)(2,1)}, u32[]{:S(2)}) copy-start(bf16[512,256]{1,0:T(8,128)(2,1)} %query_ref.5) | copy-start | bytes 786436
  2.6 18.1 %all-to-all-start = ((bf16[16,2,32,256]{3,2,1,0:T(8,128)(2,1)}), bf16[16,2,32,256]{3,2,1,0:T(8,128)(2,1)S(1)}, u32[]{:S(2)}, u32[]{:S(2)}) async-start(bf16[16,2,32,256]{3,2,1,0:T(8,128)(2,1)} %stack.17), calls=%async_computation | async-start | bytes 1048576 | tf_op jit(solution)/shard_map/all_to_all | solution.py:363
  12.9 9.7 %copy-start.4 = (bf16[2,2,128,512]{3,2,1,0:T(8,128)(2,1)}, bf16[2,2,128,512]{3,2,1,0:T(8,128)(2,1)S(1)}, u32[]{:S(2)}) copy-start(bf16[2,2,128,512]{3,2,1,0:T(8,128)(2,1)S(1)} %get-tuple-element.19.turned_ref) | copy-start | bytes 1572868
  22.6 24.3 %all-to-all-start.1 = ((bf16[16,2,3,32,256]{4,3,2,1,0:T(8,128)(2,1)}), bf16[16,2,3,32,256]{4,3,2,1,0:T(8,128)(2,1)S(1)}, u32[]{:S(2)}, u32[]{:S(2)}) async-start(bf16[16,2,3,32,256]{4,3,2,1,0:T(8,128)(2,1)} %pick.1), calls=%async_computation.1 | async-start | bytes 3145728 | tf_op jit(solution)/shard_map/all_to_all | solution.py:363
  46.9 1.0 copy-start.5
  55.9 0.8 copy-start.6
  56.7 29.4 %all-to-all-start.2 = ((bf16[16,2,3,32,256]{4,3,2,1,0:T(8,128)(2,1)}), bf16[16,2,3,32,256]{4,3,2,1,0:T(8,128)(2,1)S(1)}, u32[]{:S(2)}, u32[]{:S(2)}) async-start(bf16[16,2,3,32,256]{4,3,2,1,0:T(8,128)(2,1)} %get-tuple-element.24), calls=%async_computation.2 | async-start | bytes 3145728 | tf_op jit(solution)/shard_map/all_to_all | solution.py:363
  62.3 1.0 copy-start.7
  65.7 13.4 %collective-permute-start = (bf16[64,256]{1,0:T(8,128)(2,1)S(1)}, bf16[64,256]{1,0:T(8,128)(2,1)S(1)}, u32[]{:S(2)}, u32[]{:S(2)}) collective-permute-start(bf16[64,256]{1,0:T(8,128)(2,1)S(1)} %get-tuple-element.26), channel_id=1, source_target_pairs={{0,2},{1,3},{2,4},{3,5},{4,6},{5,7},{6,8},{7,9},{8,10},{9,11},{10,... | collective-permute-start | bytes 98312 | tf_op jit(solution)/shard_map/ppermute | solution.py:463
  67.5 14.1 %collective-permute-start.1 = (bf16[64,256]{1,0:T(8,128)(2,1)S(1)}, bf16[64,256]{1,0:T(8,128)(2,1)S(1)}, u32[]{:S(2)}, u32[]{:S(2)}) collective-permute-start(bf16[64,256]{1,0:T(8,128)(2,1)S(1)} %get-tuple-element.27), channel_id=1, source_target_pairs={{0,4},{1,5},{2,6},{3,7},{4,8},{5,9},{6,10},{7,11},{8,12},{9,13},{1... | collective-permute-start | bytes 98312 | tf_op jit(solution)/shard_map/ppermute | solution.py:463
  70.5 11.8 %collective-permute-start.2 = (bf16[64,256]{1,0:T(8,128)(2,1)S(1)}, bf16[64,256]{1,0:T(8,128)(2,1)S(1)}, u32[]{:S(2)}, u32[]{:S(2)}) collective-permute-start(bf16[64,256]{1,0:T(8,128)(2,1)S(1)} %get-tuple-element.28), channel_id=1, source_target_pairs={{0,6},{1,7},{2,8},{3,9},{4,10},{5,11},{6,12},{7,13},{8,14},{9,15},... | collective-permute-start | bytes 98312 | tf_op jit(solution)/shard_map/ppermute | solution.py:463
  74.2 8.1 %collective-permute-start.3 = (bf16[64,256]{1,0:T(8,128)(2,1)S(1)}, bf16[64,256]{1,0:T(8,128)(2,1)S(1)}, u32[]{:S(2)}, u32[]{:S(2)}) collective-permute-start(bf16[64,256]{1,0:T(8,128)(2,1)S(1)} %get-tuple-element.29), channel_id=1, source_target_pairs={{0,8},{1,9},{2,10},{3,11},{4,12},{5,13},{6,14},{7,15},{8,0},{9,1},... | collective-permute-start | bytes 98312 | tf_op jit(solution)/shard_map/ppermute | solution.py:463
  74.7 7.6 %collective-permute-start.4 = (bf16[64,256]{1,0:T(8,128)(2,1)S(1)}, bf16[64,256]{1,0:T(8,128)(2,1)S(1)}, u32[]{:S(2)}, u32[]{:S(2)}) collective-permute-start(bf16[64,256]{1,0:T(8,128)(2,1)S(1)} %get-tuple-element.30), channel_id=1, source_target_pairs={{0,10},{1,11},{2,12},{3,13},{4,14},{5,15},{6,0},{7,1},{8,2},{9,3},... | collective-permute-start | bytes 98312 | tf_op jit(solution)/shard_map/ppermute | solution.py:463
  79.1 4.1 %collective-permute-start.5 = (bf16[64,256]{1,0:T(8,128)(2,1)S(1)}, bf16[64,256]{1,0:T(8,128)(2,1)S(1)}, u32[]{:S(2)}, u32[]{:S(2)}) collective-permute-start(bf16[64,256]{1,0:T(8,128)(2,1)S(1)} %get-tuple-element.31), channel_id=1, source_target_pairs={{0,12},{1,13},{2,14},{3,15},{4,0},{5,1},{6,2},{7,3},{8,4},{9,5},{1... | collective-permute-start | bytes 98312 | tf_op jit(solution)/shard_map/ppermute | solution.py:463
  81.5 4.0 %collective-permute-start.6 = (bf16[64,256]{1,0:T(8,128)(2,1)S(1)}, bf16[64,256]{1,0:T(8,128)(2,1)S(1)}, u32[]{:S(2)}, u32[]{:S(2)}) collective-permute-start(bf16[64,256]{1,0:T(8,128)(2,1)S(1)} %get-tuple-element.32), channel_id=1, source_target_pairs={{0,14},{1,15},{2,0},{3,1},{4,2},{5,3},{6,4},{7,5},{8,6},{9,7},{10,... | collective-permute-start | bytes 98312 | tf_op jit(solution)/shard_map/ppermute | solution.py:463
  87.8 15.6 %all-to-all-start.3 = ((bf16[16,2,32,256]{3,2,1,0:T(8,128)(2,1)}), bf16[16,2,32,256]{3,2,1,0:T(8,128)(2,1)S(1)}, u32[]{:S(2)}, u32[]{:S(2)}) async-start(bf16[16,2,32,256]{3,2,1,0:T(8,128)(2,1)} %reduce.1), calls=%async_computation.3 | async-start | bytes 1048576 | tf_op jit(solution)/shard_map/all_to_all | solution.py:363
  94.4 5.3 %collective-permute-start.7 = (bf16[8,32,256]{2,1,0:T(8,128)(2,1)S(1)}, bf16[8,32,256]{2,1,0:T(8,128)(2,1)S(1)}, u32[]{:S(2)}, u32[]{:S(2)}) collective-permute-start(bf16[8,32,256]{2,1,0:T(8,128)(2,1)S(1)} %join.1.after_ref), channel_id=1, source_target_pairs={{0,1},{1,0},{2,3},{3,2},{4,5},{5,4},{6,7},{7,6},{8,9},{9,8},{10,11... | collective-permute-start | bytes 393224 | tf_op jit(solution)/shard_map/ppermute | solution.py:476

commit v11 on v10

--- a/solution.py
+++ b/solution.py
@@ -1,3 +1,4 @@
+import functools
 import math
 
 import jax
@@ -15,6 +16,7 @@
 TILE = 256
 STATS = 8
 SUBLANES = 8
+EARLY = 5
 MIB = 1 << 20
 
 
@@ -71,19 +73,18 @@
         copy.wait()
 
 
-def reduce_kernel(selection_ref, terms_ref, after_ref, out_ref, *total_refs):
+def reduce_kernel(after, selection_ref, terms_ref, *refs):
+    out_ref, total_refs = refs[after], refs[after + 1 :]
     blocks, _, _, width = out_ref.shape
     heads = width // HEAD_DIM
     for head, total_ref in enumerate(total_refs):
-        total_ref[: blocks - 1] = terms_ref[1:, :, 0, :, head_columns(head)].astype(jnp.float32)
+        total_ref[: blocks - 1] = terms_ref[1:, head, :, 0].astype(jnp.float32)
         total_ref[blocks - 1] = jnp.zeros_like(total_ref[blocks - 1])
     for block in range(blocks):
         for slot in range(1, TOPK):
             for head, total_ref in enumerate(total_refs):
                 target = selection_ref[(block * heads + head) * TOPK + slot]
-                total_ref[target] += terms_ref[block, :, slot, :, head_columns(head)].astype(
-                    jnp.float32
-                )
+                total_ref[target] += terms_ref[block, head, :, slot].astype(jnp.float32)
     for head, total_ref in enumerate(total_refs):
         out_ref[:, :, :, head_columns(head)] = total_ref[...].astype(out_ref.dtype)
 
@@ -105,7 +106,6 @@
     value_ref,
     grad_ref,
     listed_ref,
-    turned_ref,
     stats_ref,
     held_ref,
     sem,
@@ -129,14 +129,12 @@
     def one_head(head, carry):
         columns = head_columns(head)
         key, value = held_ref[2, :, columns], held_ref[3, :, columns]
-        for index in range(2):
-            turned_ref[index, head] = held_ref[index, :, columns].T
         for first in range(0, rows, TILE):
             tile = pl.ds(first, TILE)
-            scores = causal(dot(key, turned_ref[0, head, :, tile], 1, 0), first)
+            scores = causal(dot(key, held_ref[0, tile, columns], 1, 1), first)
             top = jnp.max(scores, axis=0, keepdims=True)
             raised = jnp.exp2((scores - top) * EXPONENT)
-            product = raised * dot(value, turned_ref[1, head, :, tile], 1, 0)
+            product = raised * dot(value, held_ref[1, tile, columns], 1, 1)
             stats_ref[head, 0:1, tile] = top
             stats_ref[head, 1:2, tile] = jnp.sum(raised, axis=0, keepdims=True)
             stats_ref[head, 2:3, tile] = jnp.sum(product, axis=0, keepdims=True)
@@ -148,7 +146,6 @@
 def far_kernel(
     selection_ref,
     position_ref,
-    turned_ref,
     query_ref,
     grad_ref,
     listed_ref,
@@ -156,21 +153,19 @@
     terms_ref,
     part_ref,
     stats_ref,
-    rows_ref,
+    held_terms_ref,
+    held_part_ref,
     sem,
-    held_terms_ref,
-    terms_sem,
     *scratch,
 ):
     heads, _, rows = own_stats_ref.shape
     chunks, _, _, chunk, _ = listed_ref.shape
     block = position_ref[0]
-    copies = [
-        pltpu.make_async_copy(source, rows_ref.at[index], sem.at[index])
-        for index, source in enumerate((query_ref, grad_ref))
-    ]
-    for copy in copies:
-        copy.start()
+    sent = []
+
+    def send(source, target, index):
+        sent.append(pltpu.make_async_copy(source, target, sem.at[index]))
+        sent[-1].start()
 
     def listed(which, head):
         return listed_ref[:, which, :, :, head_columns(head)].reshape(TOPK * rows, HEAD_DIM)
@@ -183,9 +178,9 @@
         shape = (chunks, TOPK, chunk, TILE)
         for first in range(0, rows, TILE):
             tile = pl.ds(first, TILE)
-            scores = dot(listed(0, head), turned_ref[0, head, :, tile], 1, 0)
+            scores = dot(listed(0, head), query_ref[tile, head_columns(head)], 1, 1)
             score_ref[:, :, :, tile] = scores.reshape(shape)
-            grad_probs = dot(listed(1, head), turned_ref[1, head, :, tile], 1, 0)
+            grad_probs = dot(listed(1, head), grad_ref[tile, head_columns(head)], 1, 1)
             grad_prob_ref[:, :, :, tile] = grad_probs.reshape(shape)
             top = jnp.full((1, TILE), MASKED, jnp.float32)
             for slot in range(TOPK):
@@ -224,31 +219,20 @@
     def gradients(head):
         _, _, prob_ref, grad_score_ref = scratch[4 * head : 4 * head + 4]
         columns = head_columns(head)
-        query, grad = rows_ref[0, :, columns], rows_ref[1, :, columns]
+        query, grad = query_ref[:, columns], grad_ref[:, columns]
         shape = (chunks, TOPK, chunk, HEAD_DIM)
         prob = prob_ref[...].reshape(TOPK * rows, rows)
         grad_scores = grad_score_ref[...].reshape(TOPK * rows, rows)
-        for which in range(2):
-            if which == 0:
-                term = dot(grad_scores, query, 1, 0) * SCALING
-            else:
-                term = dot(prob, grad, 1, 0)
-            held_terms_ref[:, which, :, :, columns] = term.astype(jnp.bfloat16).reshape(shape)
-            copy = pltpu.make_async_copy(
-                held_terms_ref.at[:, which, :, :, columns],
-                terms_ref.at[:, which, :, :, columns],
-                terms_sem.at[head, which],
-            )
-            copy.start()
-            sent.append(copy)
-        part_ref[head] = dot(listed(0, head).T, grad_scores, 1, 0)
-
-    sent = []
+        held_part_ref[head] = dot(listed(0, head).T, grad_scores, 1, 0)
+        send(held_part_ref.at[head], part_ref.at[head], 2 * head)
+        grad_key = dot(grad_scores, query, 1, 0) * SCALING
+        held_terms_ref[:, head, 0] = grad_key.astype(jnp.bfloat16).reshape(shape)
+        grad_value = dot(prob, grad, 1, 0)
+        held_terms_ref[:, head, 1] = grad_value.astype(jnp.bfloat16).reshape(shape)
+        send(held_terms_ref.at[:, head], terms_ref.at[:, head], 2 * head + 1)
+
     for head in range(heads):
         softmax(head)
-        if head == 0:
-            for copy in copies:
-                copy.wait()
         gradients(head)
     for copy in sent:
         copy.wait()
@@ -266,8 +250,10 @@
     own_ref,
     *refs,
 ):
-    piece_refs, grad_query_ref = refs[:-1], refs[-1]
+    piece_refs, (grad_query_ref, held_part_ref, sem) = refs[:-3], refs[-3:]
     heads, _, rows = stats_ref.shape
+    fetch = pltpu.make_async_copy(part_ref, held_part_ref, sem)
+    fetch.start()
     chunks, _, chunk, _ = own_ref.shape
 
     def one_head(head, carry):
@@ -279,7 +265,8 @@
         probability = raised * stats_ref[head, 0:1, :]
         grad_probs = dot(value, grad, 1, 1)
         grad_scores = (probability * (grad_probs - stats_ref[head, 1:2, :])).astype(jnp.bfloat16)
-        grad_query = (part_ref[head] + dot(key.T, grad_scores, 1, 0)) * SCALING
+        pl.when(head == 0)(fetch.wait)
+        grad_query = (held_part_ref[head] + dot(key.T, grad_scores, 1, 0)) * SCALING
         grad_query_ref[:, columns] = grad_query.T.astype(jnp.bfloat16)
         results = (
             dot(grad_scores, query, 1, 0) * SCALING,
@@ -391,14 +378,13 @@
         limit=59,
     )(key_input.reshape(chain, chunk, width), value_input.reshape(chain, chunk, width))
     held = swap(pair, "chain")
-    listed, turned, own_stats = call(
+    listed, own_stats = call(
         own_forward_kernel,
         "own_forward",
         [smem] + [anywhere] * 4,
-        (smem, vmem, vmem),
+        (smem, vmem),
         (
             jax.ShapeDtypeStruct(listed.shape, jnp.int32),
-            jax.ShapeDtypeStruct((2, heads, HEAD_DIM, rows), low),
             jax.ShapeDtypeStruct((heads, STATS, rows), full),
         ),
         [pltpu.VMEM((4, rows, width), low), pltpu.SemaphoreType.DMA((4,))],
@@ -420,18 +406,17 @@
     terms, part, stats = call(
         far_kernel,
         "far",
-        [smem, smem, vmem, anywhere, anywhere, vmem, vmem],
-        (anywhere, vmem, vmem),
+        [smem, smem] + [vmem] * 4,
+        (anywhere, anywhere, vmem),
         (
-            jax.ShapeDtypeStruct((chain, 2, TOPK, chunk, width), low),
+            jax.ShapeDtypeStruct((chain, heads, 2, TOPK, chunk, HEAD_DIM), low),
             jax.ShapeDtypeStruct((heads, HEAD_DIM, rows), full),
             jax.ShapeDtypeStruct((heads, STATS, rows), full),
         ),
         [
-            pltpu.VMEM((2, rows, width), low),
-            pltpu.SemaphoreType.DMA((2,)),
-            pltpu.VMEM((chain, 2, TOPK, chunk, width), low),
-            pltpu.SemaphoreType.DMA((heads, 2)),
+            pltpu.VMEM((chain, heads, 2, TOPK, chunk, HEAD_DIM), low),
+            pltpu.VMEM((heads, HEAD_DIM, rows), full),
+            pltpu.SemaphoreType.DMA((2 * heads,)),
         ]
         + [
             pltpu.VMEM((chain, TOPK, chunk, rows), full),
@@ -442,16 +427,20 @@
         * heads,
         limit=32,
         slots=5 * TOPK,
-    )(listed, position, turned, query_input, grad_output, slots, own_stats)
+    )(listed, position, query_input, grad_output, slots, own_stats)
     returned = swap(terms, "chain")
     own, *pieces = call(
         own_backward_kernel,
         "own_backward",
-        [smem] + [vmem] * 7,
+        [smem] + [vmem] * 4 + [anywhere] + [vmem] * 2,
         (vmem,) * (1 + planes),
         (jax.ShapeDtypeStruct((chain, 2, chunk, width), low),)
         + (jax.ShapeDtypeStruct((rows // planes, width), low),) * planes,
-        [pltpu.VMEM((rows, width), low)],
+        [
+            pltpu.VMEM((rows, width), low),
+            pltpu.VMEM((heads, HEAD_DIM, rows), full),
+            pltpu.SemaphoreType.DMA(()),
+        ],
         limit=12,
         slots=5,
     )(position, query_input, key_input, value_input, grad_output, part, own_stats, stats)
@@ -462,8 +451,18 @@
         pairs = [(one, (one + step * cores) % spread) for one in range(spread)]
         return lax.ppermute(piece, "heads", pairs)
 
-    for step in sorted(range(planes), key=lambda step: -min(step, planes - step)):
+    order = sorted(range(planes), key=lambda step: -min(step, planes - step))
+    for step in order:
         pieces[step] = to_plane(pieces[step], step)
+    early = [pieces[step] for step in order[:EARLY]]
+    summed = call(
+        functools.partial(reduce_kernel, len(early)),
+        "reduce",
+        [smem, vmem] + [anywhere] * len(early),
+        vmem,
+        jax.ShapeDtypeStruct((chain, 2, chunk, width), low),
+        [pltpu.VMEM((chain, 2, chunk, HEAD_DIM), full)] * heads,
+    )(listed, returned, *early)
     joined = other = pieces[0]
     if cores > 1:
         joined = call(
@@ -474,14 +473,6 @@
             jax.ShapeDtypeStruct((planes, share, width), low),
         )(position, *pieces)
         other = lax.ppermute(joined, "heads", [(one, one ^ 1) for one in range(spread)])
-    summed = call(
-        reduce_kernel,
-        "reduce",
-        [smem, vmem, anywhere],
-        vmem,
-        jax.ShapeDtypeStruct((chain, 2, chunk, width), low),
-        [pltpu.VMEM((chain, 2, chunk, HEAD_DIM), full)] * heads,
-    )(listed, returned, joined)
     others = swap(summed, "chain")
 
     def by_share(array):

time: 132 us -> 131 us (level)
  waiting for transfers between devices: 36.3 us -> 32.4 us
  starting transfers between devices: 44.3 us -> 47.1 us
    all_to_all x4, waiting for transfers between devices: 32 us -> 28.5 us  [swap(): return lax.all_to_all(array, axis, split_axis=0, concat_axis=0, tiled=True)]
    ppermute x7, starting transfers between devices: 16.5 us -> 19.7 us  [to_plane(): return lax.ppermute(piece, 'heads', pairs)]
    unnamed x19 -> x15, local copies, waits for them, and re-layouts: 2.98 us -> 1.94 us
  transfers between devices with their start and end apart: 12 -> 12, of which waited for: 6 -> 7; matrix products, arithmetic and copies ran while one was open for 0% -> 0% of each run, Pallas kernels for 4% -> 4%
where the time goes in v11:
time: 131 us; the launch traced here: 130 us
  starting transfers between devices  47.1 us (36%)
  waiting for transfers between devices  32.4 us (25%)
  blocking collectives  25.8 us (20%)
  Pallas kernels  21.6 us (16%)
  local copies, waits for them, and re-layouts  2.06 us (2%)
    all_to_all x4, waiting for transfers between devices, swap(): return lax.all_to_all(array, axis, split_axis=0, concat_axis=0, tiled=True)  28.5 us
    all_to_all x1, blocking collectives, swap(): return lax.all_to_all(array, axis, split_axis=0, concat_axis=0, tiled=True)  25.8 us
    all_to_all x4, starting transfers between devices, swap(): return lax.all_to_all(array, axis, split_axis=0, concat_axis=0, tiled=True)  23.6 us
    ppermute x7, starting transfers between devices, to_plane(): return lax.ppermute(piece, 'heads', pairs)  19.7 us
    pallas_call x1, Pallas kernels, on_device(): call(far_kernel, 'far', [smem, smem] + [vmem] * 4, (anywhere, anywhere, v...  8.62 us
    ppermute x1, starting transfers between devices, on_device(): lax.ppermute(joined, 'heads', [(one, one ^ 1) for one in range(spread)])  3.78 us
    ppermute x7, waiting for transfers between devices, to_plane(): return lax.ppermute(piece, 'heads', pairs)  2.94 us
  transfers between devices with their start and end apart: 12, of which 7 were waited for; matrix products, arithmetic and copies ran while one was open for 0% of the time, Pallas kernels for 4%

profile of v11, /device:TPU:1, one launch (start us, length us, event | category | flops | bytes accessed | tf_op | source)
XLA Modules:
  0.0 130.0 jit_solution(15280218712381270102)
XLA Ops:
  0.6 0.0 copy-start
  0.6 0.0 copy-start.1
  0.7 0.0 copy-start.6
  0.7 0.0 copy-start.3
  0.7 0.0 copy-start.2
  0.7 1.9 %stack.17 = bf16[16,2,32,256]{3,2,1,0:T(8,128)(2,1)} custom-call(bf16[16,32,256]{2,1,0:T(8,128)(2,1)} %bitcast.5, bf16[16,32,256]{2,1,0:T(8,128)(2,1)} %bitcast.6), custom_call_target="tpu_custom_call" | custom-call | bytes 4194304 | tf_op jit(solution)/shard_map/stack/pallas_call | solution.py:367
  2.6 7.6 %all-to-all-start = ((bf16[16,2,32,256]{3,2,1,0:T(8,128)(2,1)}), bf16[16,2,32,256]{3,2,1,0:T(8,128)(2,1)S(1)}, u32[]{:S(2)}, u32[]{:S(2)}) async-start(bf16[16,2,32,256]{3,2,1,0:T(8,128)(2,1)} %stack.17), calls=%async_computation | async-start | bytes 1048576 | tf_op jit(solution)/shard_map/all_to_all | solution.py:350
  10.2 0.0 copy-done.6
  10.2 0.1 copy.9
  10.3 0.1 reshape.15.selection_ref
  10.4 0.0 copy-done
  10.4 0.0 copy-done.1
  10.4 0.0 copy-done.3
  10.5 0.0 copy-done.2
  10.5 2.4 %own_forward.1 = (s32[96]{0:T(128)S(1)}, f32[2,8,512]{2,1,0:T(8,128)S(1)}) custom-call(s32[96]{0:T(128)S(1)} %reshape.15.selection_ref, bf16[512,256]{1,0:T(8,128)(2,1)S(1)} %copy-done.2, bf16[512,256]{1,0:T(8,128)(2,1)S(1)} %copy-done, bf16[512,256]{1,0:T(8,128)(2,1)S(1)} %copy-done.1, bf16[512,256]{1,0:T(8,128)(2,1)S(1)} %copy-done.3), custom_call_target="tpu_custom_call" | custom-call | flops 268435456 | bytes 4194304 | tf_op jit(solution)/shard_map/own_forward/pallas_call | solution.py:381
  12.9 7.9 %all-to-all-done.held_ref = bf16[16,2,32,256]{3,2,1,0:T(8,128)(2,1)S(1)} async-done(((bf16[16,2,32,256]{3,2,1,0:T(8,128)(2,1)}), bf16[16,2,32,256]{3,2,1,0:T(8,128)(2,1)S(1)}, u32[]{:S(2)}, u32[]{:S(2)}) %all-to-all-start) | async-done | bytes 524320 | tf_op jit(solution)/shard_map/all_to_all | solution.py:350
  20.7 1.9 %pick.1 = bf16[16,2,3,32,256]{4,3,2,1,0:T(8,128)(2,1)} custom-call(s32[96]{0:T(128)S(1)} %get-tuple-element.17.selection_ref, bf16[16,2,32,256]{3,2,1,0:T(8,128)(2,1)S(1)} %all-to-all-done.held_ref), custom_call_target="tpu_custom_call" | custom-call | bytes 4194304 | tf_op jit(solution)/shard_map/pick/pallas_call | solution.py:394
  22.6 3.7 %all-to-all-start.1 = ((bf16[16,2,3,32,256]{4,3,2,1,0:T(8,128)(2,1)}), bf16[16,2,3,32,256]{4,3,2,1,0:T(8,128)(2,1)S(1)}, u32[]{:S(2)}, u32[]{:S(2)}) async-start(bf16[16,2,3,32,256]{4,3,2,1,0:T(8,128)(2,1)} %pick.1), calls=%async_computation.1 | async-start | bytes 3145728 | tf_op jit(solution)/shard_map/all_to_all | solution.py:350
  26.3 0.1 pad_add_fusion.position_ref.place_ref
  26.4 20.4 %all-to-all-done.1.listed_ref = bf16[16,2,3,32,256]{4,3,2,1,0:T(8,128)(2,1)S(1)} async-done(((bf16[16,2,3,32,256]{4,3,2,1,0:T(8,128)(2,1)}), bf16[16,2,3,32,256]{4,3,2,1,0:T(8,128)(2,1)S(1)}, u32[]{:S(2)}, u32[]{:S(2)}) %all-to-all-start.1) | async-done | bytes 1572896 | tf_op jit(solution)/shard_map/all_to_all | solution.py:350
  46.8 8.6 %far.1 = (bf16[16,2,2,3,32,128]{5,4,3,2,1,0:T(8,128)(2,1)}, f32[2,128,512]{2,1,0:T(8,128)S(1)}, f32[2,8,512]{2,1,0:T(8,128)S(1)}) custom-call(s32[96]{0:T(128)S(1)} %get-tuple-element.17.selection_ref, s32[3]{0:T(128)S(1)} %pad_add_fusion.position_ref.place_ref, bf16[512,256]{1,0:T(8,128)(2,1)S(1)} %copy-done.2, bf16[512,256]{1,0:T(8,128)(2,1)S(1)} %copy-done.3, ...), custom_call_target="tpu_custom_call" | custom-call | flops 2013265920 | bytes 4194304 | tf_op jit(solution)/shard_map/far/pallas_call | solution.py:406
  55.5 0.0 copy-start.4
  55.5 0.8 copy-done.4
  56.3 5.6 %all-to-all-start.2 = ((bf16[16,2,2,3,32,128]{5,4,3,2,1,0:T(8,128)(2,1)}), bf16[16,2,2,3,32,128]{5,4,3,2,1,0:T(8,128)(2,1)S(1)}, u32[]{:S(2)}, u32[]{:S(2)}) async-start(bf16[16,2,2,3,32,128]{5,4,3,2,1,0:T(8,128)(2,1)} %get-tuple-element.22), calls=%async_computation.2 | async-start | bytes 3145728 | tf_op jit(solution)/shard_map/all_to_all | solution.py:350
  61.9 0.0 copy-start.5
  61.9 1.0 copy-done.5
  62.9 2.6 %own_backward.1 = (bf16[16,2,32,256]{3,2,1,0:T(8,128)(2,1)S(1)}, bf16[64,256]{1,0:T(8,128)(2,1)S(1)}, bf16[64,256]{1,0:T(8,128)(2,1)S(1)}, bf16[64,256]{1,0:T(8,...) custom-call(s32[3]{0:T(128)S(1)} %pad_add_fusion.position_ref.place_, ...), custom_call_target="tpu_custom_call" | custom-call | flops 671088640 | bytes 4194304 | tf_op jit(solution)/shard_map/own_backward/pallas_call | solution.py:432
  65.5 7.0 %collective-permute-start = (bf16[64,256]{1,0:T(8,128)(2,1)S(1)}, bf16[64,256]{1,0:T(8,128)(2,1)S(1)}, u32[]{:S(2)}, u32[]{:S(2)}) collective-permute-start(bf16[64,256]{1,0:T(8,128)(2,1)S(1)} %get-tuple-element.23), channel_id=1, source_target_pairs={{0,8},{1,9},{2,10},{3,11},{4,12},{5,13},{6,14},{7,15},{8,0},{9,1},... | collective-permute-start | bytes 98312 | tf_op jit(solution)/shard_map/ppermute | solution.py:452
  72.5 1.6 %collective-permute-start.1 = (bf16[64,256]{1,0:T(8,128)(2,1)S(1)}, bf16[64,256]{1,0:T(8,128)(2,1)S(1)}, u32[]{:S(2)}, u32[]{:S(2)}) collective-permute-start(bf16[64,256]{1,0:T(8,128)(2,1)S(1)} %get-tuple-element.24), channel_id=1, source_target_pairs={{0,6},{1,7},{2,8},{3,9},{4,10},{5,11},{6,12},{7,13},{8,14},{9,15},... | collective-permute-start | bytes 98312 | tf_op jit(solution)/shard_map/ppermute | solution.py:452
  74.1 2.8 %collective-permute-start.2 = (bf16[64,256]{1,0:T(8,128)(2,1)S(1)}, bf16[64,256]{1,0:T(8,128)(2,1)S(1)}, u32[]{:S(2)}, u32[]{:S(2)}) collective-permute-start(bf16[64,256]{1,0:T(8,128)(2,1)S(1)} %get-tuple-element.25), channel_id=1, source_target_pairs={{0,10},{1,11},{2,12},{3,13},{4,14},{5,15},{6,0},{7,1},{8,2},{9,3},... | collective-permute-start | bytes 98312 | tf_op jit(solution)/shard_map/ppermute | solution.py:452
  77.0 1.2 collective-permute-start.3
  78.2 2.4 %collective-permute-start.4 = (bf16[64,256]{1,0:T(8,128)(2,1)S(1)}, bf16[64,256]{1,0:T(8,128)(2,1)S(1)}, u32[]{:S(2)}, u32[]{:S(2)}) collective-permute-start(bf16[64,256]{1,0:T(8,128)(2,1)S(1)} %get-tuple-element.27), channel_id=1, source_target_pairs={{0,12},{1,13},{2,14},{3,15},{4,0},{5,1},{6,2},{7,3},{8,4},{9,5},{1... | collective-permute-start | bytes 98312 | tf_op jit(solution)/shard_map/ppermute | solution.py:452
  80.5 0.0 collective-permute-done.refs_0_.refs_4_
  80.6 0.0 collective-permute-done.1.refs_1_.refs_3_
  80.6 0.0 collective-permute-done.2.refs_2_.refs_5_
  80.6 1.4 %collective-permute-done.3.refs_3_.refs_2_ = bf16[64,256]{1,0:T(8,128)(2,1)S(1)} collective-permute-done((bf16[64,256]{1,0:T(8,128)(2,1)S(1)}, bf16[64,256]{1,0:T(8,128)(2,1)S(1)}, u32[]{:S(2)}, u32[]{:S(2)}) %collective-permute-start.3) | collective-permute-done | bytes 32800 | tf_op jit(solution)/shard_map/ppermute | solution.py:452
  82.0 0.3 collective-permute-done.4.refs_4_.refs_6_
  82.3 0.2 all-to-all-done.2.terms_ref
  82.4 1.7 %reduce.1 = bf16[16,2,32,256]{3,2,1,0:T(8,128)(2,1)} custom-call(s32[96]{0:T(128)S(1)} %get-tuple-element.17.selection_ref, bf16[16,2,2,3,32,128]{5,4,3,2,1,0:T(8,128)(2,1)S(1)} %all-to-all-done.2.terms_ref, bf16[64,256]{1,0:T(8,128)(2,1)S(1)} %collective-permute-done.refs_0_.refs_4_, bf16[64,256]{1,0:T(8,128)(2,1)S(1)} %collective-permute-done.1.refs_1_.refs_3_, ...), custom_call_target="tpu_custom_call" | custom-call | bytes 4194304 | tf_op jit(solution)/shard_map/reduce/pallas_call | solution.py:458
  84.1 6.7 %all-to-all-start.3 = ((bf16[16,2,32,256]{3,2,1,0:T(8,128)(2,1)}), bf16[16,2,32,256]{3,2,1,0:T(8,128)(2,1)S(1)}, u32[]{:S(2)}, u32[]{:S(2)}) async-start(bf16[16,2,32,256]{3,2,1,0:T(8,128)(2,1)} %reduce.1), calls=%async_computation.3 | async-start | bytes 1048576 | tf_op jit(solution)/shard_map/all_to_all | solution.py:350
  90.8 0.8 collective-permute-start.5
  91.6 3.9 %collective-permute-start.6 = (bf16[64,256]{1,0:T(8,128)(2,1)S(1)}, bf16[64,256]{1,0:T(8,128)(2,1)S(1)}, u32[]{:S(2)}, u32[]{:S(2)}) collective-permute-start(bf16[64,256]{1,0:T(8,128)(2,1)S(1)} %get-tuple-element.30), channel_id=1, source_target_pairs={{0,14},{1,15},{2,0},{3,1},{4,2},{5,3},{6,4},{7,5},{8,6},{9,7},{10,... | collective-permute-start | bytes 98312 | tf_op jit(solution)/shard_map/ppermute | solution.py:452
  95.5 1.2 collective-permute-done.5.refs_1_
  96.7 0.0 collective-permute-done.6.refs_7_
  96.7 0.6 join.1
  97.3 3.8 %collective-permute-start.7 = (bf16[8,32,256]{2,1,0:T(8,128)(2,1)S(1)}, bf16[8,32,256]{2,1,0:T(8,128)(2,1)S(1)}, u32[]{:S(2)}, u32[]{:S(2)}) collective-permute-start(bf16[8,32,256]{2,1,0:T(8,128)(2,1)S(1)} %join.1), channel_id=1, source_target_pairs={{0,1},{1,0},{2,3},{3,2},{4,5},{5,4},{6,7},{7,6},{8,9},{9,8},{10,11... | collective-permute-start | bytes 393224 | tf_op jit(solution)/shard_map/ppermute | solution.py:475
  101.1 1.0 collective-permute-done.7.after_ref.other_ref
  102.0 0.0 all-to-all-done.3.others_ref
  102.0 0.1 finish.1
  102.2 25.8 %all_to_all.25.parts_ref = bf16[16,2,32,256]{3,2,1,0:T(8,128)(2,1)S(1)} all-to-all(bf16[16,2,32,256]{3,2,1,0:T(8,128)(2,1)S(1)} %finish.1), channel_id=1, replica_groups=mesh['chain'=16,'heads'=16] {'heads'}, dimensions={0} | all-to-all | bytes 1048576 | tf_op jit(solution)/shard_map/all_to_all | solution.py:350
  128.0 1.8 %lay.1 = (bf16[32,4096]{1,0:T(8,128)(2,1)}, bf16[32,4096]{1,0:T(8,128)(2,1)}, bf16[32,4096]{1,0:T(8,128)(2,1)}) custom-call(s32[3]{0:T(128)S(1)} %pad_add_fusion.position_ref.place_ref, bf16[16,2,32,256]{3,2,1,0:T(8,128)(2,1)S(1)} %all_to_all.25.parts_ref, bf16[8,32,256]{2,1,0:T(8,128)(2,1)S(1)} %collective-permute-done.7.after_ref.other_ref, ...), custom_call_target="tpu_custom_call" | custom-call | bytes 4194304 | tf_op jit(solution)/shard_map/lay/pallas_call | solution.py:491
Async XLA Ops:
  0.6 9.8 %copy-start = (bf16[512,256]{1,0:T(8,128)(2,1)S(1)}, bf16[512,256]{1,0:T(8,128)(2,1)}, u32[]{:S(2)}) copy-start(bf16[512,256]{1,0:T(8,128)(2,1)} %key_ref.3) | copy-start | bytes 786436
  0.6 9.8 %copy-start.1 = (bf16[512,256]{1,0:T(8,128)(2,1)S(1)}, bf16[512,256]{1,0:T(8,128)(2,1)}, u32[]{:S(2)}) copy-start(bf16[512,256]{1,0:T(8,128)(2,1)} %value_ref.3) | copy-start | bytes 786436
  0.7 9.6 %copy-start.6 = (s32[16,2,3]{0,1,2:T(2,128)S(1)}, s32[16,2,3]{0,1,2:T(2,128)}, u32[]{:S(2)}) copy-start(s32[16,2,3]{0,1,2:T(2,128)} %param.9) | copy-start | bytes 1156
  0.7 9.8 %copy-start.3 = (bf16[512,256]{1,0:T(8,128)(2,1)S(1)}, bf16[512,256]{1,0:T(8,128)(2,1)}, u32[]{:S(2)}) copy-start(bf16[512,256]{1,0:T(8,128)(2,1)} %grad_ref.5) | copy-start | bytes 786436
  0.7 9.8 %copy-start.2 = (bf16[512,256]{1,0:T(8,128)(2,1)S(1)}, bf16[512,256]{1,0:T(8,128)(2,1)}, u32[]{:S(2)}) copy-start(bf16[512,256]{1,0:T(8,128)(2,1)} %query_ref.5) | copy-start | bytes 786436
  2.6 18.1 %all-to-all-start = ((bf16[16,2,32,256]{3,2,1,0:T(8,128)(2,1)}), bf16[16,2,32,256]{3,2,1,0:T(8,128)(2,1)S(1)}, u32[]{:S(2)}, u32[]{:S(2)}) async-start(bf16[16,2,32,256]{3,2,1,0:T(8,128)(2,1)} %stack.17), calls=%async_computation | async-start | bytes 1048576 | tf_op jit(solution)/shard_map/all_to_all | solution.py:350
  22.6 24.3 %all-to-all-start.1 = ((bf16[16,2,3,32,256]{4,3,2,1,0:T(8,128)(2,1)}), bf16[16,2,3,32,256]{4,3,2,1,0:T(8,128)(2,1)S(1)}, u32[]{:S(2)}, u32[]{:S(2)}) async-start(bf16[16,2,3,32,256]{4,3,2,1,0:T(8,128)(2,1)} %pick.1), calls=%async_computation.1 | async-start | bytes 3145728 | tf_op jit(solution)/shard_map/all_to_all | solution.py:350
  55.5 0.8 copy-start.4
  56.3 26.1 %all-to-all-start.2 = ((bf16[16,2,2,3,32,128]{5,4,3,2,1,0:T(8,128)(2,1)}), bf16[16,2,2,3,32,128]{5,4,3,2,1,0:T(8,128)(2,1)S(1)}, u32[]{:S(2)}, u32[]{:S(2)}) async-start(bf16[16,2,2,3,32,128]{5,4,3,2,1,0:T(8,128)(2,1)} %get-tuple-element.22), calls=%async_computation.2 | async-start | bytes 3145728 | tf_op jit(solution)/shard_map/all_to_all | solution.py:350
  61.9 1.0 copy-start.5
  65.5 15.0 %collective-permute-start = (bf16[64,256]{1,0:T(8,128)(2,1)S(1)}, bf16[64,256]{1,0:T(8,128)(2,1)S(1)}, u32[]{:S(2)}, u32[]{:S(2)}) collective-permute-start(bf16[64,256]{1,0:T(8,128)(2,1)S(1)} %get-tuple-element.23), channel_id=1, source_target_pairs={{0,8},{1,9},{2,10},{3,11},{4,12},{5,13},{6,14},{7,15},{8,0},{9,1},... | collective-permute-start | bytes 98312 | tf_op jit(solution)/shard_map/ppermute | solution.py:452
  72.5 8.1 %collective-permute-start.1 = (bf16[64,256]{1,0:T(8,128)(2,1)S(1)}, bf16[64,256]{1,0:T(8,128)(2,1)S(1)}, u32[]{:S(2)}, u32[]{:S(2)}) collective-permute-start(bf16[64,256]{1,0:T(8,128)(2,1)S(1)} %get-tuple-element.24), channel_id=1, source_target_pairs={{0,6},{1,7},{2,8},{3,9},{4,10},{5,11},{6,12},{7,13},{8,14},{9,15},... | collective-permute-start | bytes 98312 | tf_op jit(solution)/shard_map/ppermute | solution.py:452
  74.1 6.4 %collective-permute-start.2 = (bf16[64,256]{1,0:T(8,128)(2,1)S(1)}, bf16[64,256]{1,0:T(8,128)(2,1)S(1)}, u32[]{:S(2)}, u32[]{:S(2)}) collective-permute-start(bf16[64,256]{1,0:T(8,128)(2,1)S(1)} %get-tuple-element.25), channel_id=1, source_target_pairs={{0,10},{1,11},{2,12},{3,13},{4,14},{5,15},{6,0},{7,1},{8,2},{9,3},... | collective-permute-start | bytes 98312 | tf_op jit(solution)/shard_map/ppermute | solution.py:452
  77.0 5.0 %collective-permute-start.3 = (bf16[64,256]{1,0:T(8,128)(2,1)S(1)}, bf16[64,256]{1,0:T(8,128)(2,1)S(1)}, u32[]{:S(2)}, u32[]{:S(2)}) collective-permute-start(bf16[64,256]{1,0:T(8,128)(2,1)S(1)} %get-tuple-element.26), channel_id=1, source_target_pairs={{0,4},{1,5},{2,6},{3,7},{4,8},{5,9},{6,10},{7,11},{8,12},{9,13},{1... | collective-permute-start | bytes 98312 | tf_op jit(solution)/shard_map/ppermute | solution.py:452
  78.2 4.1 %collective-permute-start.4 = (bf16[64,256]{1,0:T(8,128)(2,1)S(1)}, bf16[64,256]{1,0:T(8,128)(2,1)S(1)}, u32[]{:S(2)}, u32[]{:S(2)}) collective-permute-start(bf16[64,256]{1,0:T(8,128)(2,1)S(1)} %get-tuple-element.27), channel_id=1, source_target_pairs={{0,12},{1,13},{2,14},{3,15},{4,0},{5,1},{6,2},{7,3},{8,4},{9,5},{1... | collective-permute-start | bytes 98312 | tf_op jit(solution)/shard_map/ppermute | solution.py:452
  84.1 17.9 %all-to-all-start.3 = ((bf16[16,2,32,256]{3,2,1,0:T(8,128)(2,1)}), bf16[16,2,32,256]{3,2,1,0:T(8,128)(2,1)S(1)}, u32[]{:S(2)}, u32[]{:S(2)}) async-start(bf16[16,2,32,256]{3,2,1,0:T(8,128)(2,1)} %reduce.1), calls=%async_computation.3 | async-start | bytes 1048576 | tf_op jit(solution)/shard_map/all_to_all | solution.py:350
  90.8 5.9 %collective-permute-start.5 = (bf16[64,256]{1,0:T(8,128)(2,1)S(1)}, bf16[64,256]{1,0:T(8,128)(2,1)S(1)}, u32[]{:S(2)}, u32[]{:S(2)}) collective-permute-start(bf16[64,256]{1,0:T(8,128)(2,1)S(1)} %get-tuple-element.29), channel_id=1, source_target_pairs={{0,2},{1,3},{2,4},{3,5},{4,6},{5,7},{6,8},{7,9},{8,10},{9,11},{10,... | collective-permute-start | bytes 98312 | tf_op jit(solution)/shard_map/ppermute | solution.py:452
  91.6 5.1 %collective-permute-start.6 = (bf16[64,256]{1,0:T(8,128)(2,1)S(1)}, bf16[64,256]{1,0:T(8,128)(2,1)S(1)}, u32[]{:S(2)}, u32[]{:S(2)}) collective-permute-start(bf16[64,256]{1,0:T(8,128)(2,1)S(1)} %get-tuple-element.30), channel_id=1, source_target_pairs={{0,14},{1,15},{2,0},{3,1},{4,2},{5,3},{6,4},{7,5},{8,6},{9,7},{10,... | collective-permute-start | bytes 98312 | tf_op jit(solution)/shard_map/ppermute | solution.py:452
  97.3 4.8 %collective-permute-start.7 = (bf16[8,32,256]{2,1,0:T(8,128)(2,1)S(1)}, bf16[8,32,256]{2,1,0:T(8,128)(2,1)S(1)}, u32[]{:S(2)}, u32[]{:S(2)}) collective-permute-start(bf16[8,32,256]{2,1,0:T(8,128)(2,1)S(1)} %join.1), channel_id=1, source_target_pairs={{0,1},{1,0},{2,3},{3,2},{4,5},{5,4},{6,7},{7,6},{8,9},{9,8},{10,11... | collective-permute-start | bytes 393224 | tf_op jit(solution)/shard_map/ppermute | solution.py:475

commit v12 on v11

--- a/solution.py
+++ b/solution.py
@@ -153,20 +153,11 @@
     terms_ref,
     part_ref,
     stats_ref,
-    held_terms_ref,
-    held_part_ref,
-    sem,
     *scratch,
 ):
     heads, _, rows = own_stats_ref.shape
     chunks, _, _, chunk, _ = listed_ref.shape
     block = position_ref[0]
-    sent = []
-
-    def send(source, target, index):
-        sent.append(pltpu.make_async_copy(source, target, sem.at[index]))
-        sent[-1].start()
-
     def listed(which, head):
         return listed_ref[:, which, :, :, head_columns(head)].reshape(TOPK * rows, HEAD_DIM)
 
@@ -223,19 +214,15 @@
         shape = (chunks, TOPK, chunk, HEAD_DIM)
         prob = prob_ref[...].reshape(TOPK * rows, rows)
         grad_scores = grad_score_ref[...].reshape(TOPK * rows, rows)
-        held_part_ref[head] = dot(listed(0, head).T, grad_scores, 1, 0)
-        send(held_part_ref.at[head], part_ref.at[head], 2 * head)
         grad_key = dot(grad_scores, query, 1, 0) * SCALING
-        held_terms_ref[:, head, 0] = grad_key.astype(jnp.bfloat16).reshape(shape)
+        terms_ref[:, head, 0] = grad_key.astype(jnp.bfloat16).reshape(shape)
         grad_value = dot(prob, grad, 1, 0)
-        held_terms_ref[:, head, 1] = grad_value.astype(jnp.bfloat16).reshape(shape)
-        send(held_terms_ref.at[:, head], terms_ref.at[:, head], 2 * head + 1)
+        terms_ref[:, head, 1] = grad_value.astype(jnp.bfloat16).reshape(shape)
+        part_ref[head] = dot(listed(0, head).T, grad_scores, 1, 0).astype(jnp.bfloat16)
 
     for head in range(heads):
         softmax(head)
         gradients(head)
-    for copy in sent:
-        copy.wait()
 
 
 def own_backward_kernel(
@@ -250,10 +237,8 @@
     own_ref,
     *refs,
 ):
-    piece_refs, (grad_query_ref, held_part_ref, sem) = refs[:-3], refs[-3:]
+    piece_refs, grad_query_ref = refs[:-1], refs[-1]
     heads, _, rows = stats_ref.shape
-    fetch = pltpu.make_async_copy(part_ref, held_part_ref, sem)
-    fetch.start()
     chunks, _, chunk, _ = own_ref.shape
 
     def one_head(head, carry):
@@ -265,8 +250,8 @@
         probability = raised * stats_ref[head, 0:1, :]
         grad_probs = dot(value, grad, 1, 1)
         grad_scores = (probability * (grad_probs - stats_ref[head, 1:2, :])).astype(jnp.bfloat16)
-        pl.when(head == 0)(fetch.wait)
-        grad_query = (held_part_ref[head] + dot(key.T, grad_scores, 1, 0)) * SCALING
+        grad_query = dot(key.T, grad_scores, 1, 0) + part_ref[head].astype(jnp.float32)
+        grad_query = grad_query * SCALING
         grad_query_ref[:, columns] = grad_query.T.astype(jnp.bfloat16)
         results = (
             dot(grad_scores, query, 1, 0) * SCALING,
@@ -407,18 +392,13 @@
         far_kernel,
         "far",
         [smem, smem] + [vmem] * 4,
-        (anywhere, anywhere, vmem),
+        (vmem, vmem, vmem),
         (
             jax.ShapeDtypeStruct((chain, heads, 2, TOPK, chunk, HEAD_DIM), low),
-            jax.ShapeDtypeStruct((heads, HEAD_DIM, rows), full),
+            jax.ShapeDtypeStruct((heads, HEAD_DIM, rows), low),
             jax.ShapeDtypeStruct((heads, STATS, rows), full),
         ),
         [
-            pltpu.VMEM((chain, heads, 2, TOPK, chunk, HEAD_DIM), low),
-            pltpu.VMEM((heads, HEAD_DIM, rows), full),
-            pltpu.SemaphoreType.DMA((2 * heads,)),
-        ]
-        + [
             pltpu.VMEM((chain, TOPK, chunk, rows), full),
             pltpu.VMEM((chain, TOPK, chunk, rows), full),
             pltpu.VMEM((chain, TOPK, chunk, rows), low),
@@ -432,15 +412,11 @@
     own, *pieces = call(
         own_backward_kernel,
         "own_backward",
-        [smem] + [vmem] * 4 + [anywhere] + [vmem] * 2,
+        [smem] + [vmem] * 7,
         (vmem,) * (1 + planes),
         (jax.ShapeDtypeStruct((chain, 2, chunk, width), low),)
         + (jax.ShapeDtypeStruct((rows // planes, width), low),) * planes,
-        [
-            pltpu.VMEM((rows, width), low),
-            pltpu.VMEM((heads, HEAD_DIM, rows), full),
-            pltpu.SemaphoreType.DMA(()),
-        ],
+        [pltpu.VMEM((rows, width), low)],
         limit=12,
         slots=5,
     )(position, query_input, key_input, value_input, grad_output, part, own_stats, stats)

time: 131 us -> 130 us (level)
  no operation moved by 1% of the time
where the time goes in v12:
time: 130 us; the launch traced here: 129 us
  starting transfers between devices  46.7 us (36%)
  waiting for transfers between devices  32.8 us (25%)
  blocking collectives  26.3 us (20%)
  Pallas kernels  20.6 us (16%)
  local copies, waits for them, and re-layouts  1.6 us (1%)
    all_to_all x4, waiting for transfers between devices, swap(): return lax.all_to_all(array, axis, split_axis=0, concat_axis=0, tiled=True)  28.9 us
    all_to_all x1, blocking collectives, swap(): return lax.all_to_all(array, axis, split_axis=0, concat_axis=0, tiled=True)  26.3 us
    all_to_all x4, starting transfers between devices, swap(): return lax.all_to_all(array, axis, split_axis=0, concat_axis=0, tiled=True)  23.2 us
    ppermute x7, starting transfers between devices, to_plane(): return lax.ppermute(piece, 'heads', pairs)  20.2 us
    pallas_call x1, Pallas kernels, on_device(): call(far_kernel, 'far', [smem, smem] + [vmem] * 4, (vmem, vmem, vmem), (j...  7.86 us
    ppermute x1, starting transfers between devices, on_device(): lax.ppermute(joined, 'heads', [(one, one ^ 1) for one in range(spread)])  3.32 us
    ppermute x7, waiting for transfers between devices, to_plane(): return lax.ppermute(piece, 'heads', pairs)  2.93 us
  transfers between devices with their start and end apart: 12, of which 7 were waited for; matrix products, arithmetic and copies ran while one was open for 0% of the time, Pallas kernels for 4%

profile of v12, /device:TPU:1, one launch (start us, length us, event | category | flops | bytes accessed | tf_op | source)
XLA Modules:
  0.0 129.1 jit_solution(16595398316216429229)
XLA Ops:
  0.6 0.0 copy-start
  0.6 0.0 copy-start.1
  0.7 0.0 copy-start.6
  0.7 0.0 copy-start.3
  0.7 0.0 copy-start.2
  0.7 1.9 %stack.17 = bf16[16,2,32,256]{3,2,1,0:T(8,128)(2,1)} custom-call(bf16[16,32,256]{2,1,0:T(8,128)(2,1)} %bitcast.5, bf16[16,32,256]{2,1,0:T(8,128)(2,1)} %bitcast.6), custom_call_target="tpu_custom_call" | custom-call | bytes 4194304 | tf_op jit(solution)/shard_map/stack/pallas_call | solution.py:352
  2.6 7.6 %all-to-all-start = ((bf16[16,2,32,256]{3,2,1,0:T(8,128)(2,1)}), bf16[16,2,32,256]{3,2,1,0:T(8,128)(2,1)S(1)}, u32[]{:S(2)}, u32[]{:S(2)}) async-start(bf16[16,2,32,256]{3,2,1,0:T(8,128)(2,1)} %stack.17), calls=%async_computation | async-start | bytes 1048576 | tf_op jit(solution)/shard_map/all_to_all | solution.py:335
  10.2 0.0 copy-done.6
  10.2 0.1 copy.9
  10.3 0.1 reshape.15.selection_ref
  10.4 0.0 copy-done
  10.4 0.0 copy-done.1
  10.4 0.0 copy-done.3
  10.5 0.0 copy-done.2
  10.5 2.4 %own_forward.1 = (s32[96]{0:T(128)S(1)}, f32[2,8,512]{2,1,0:T(8,128)S(1)}) custom-call(s32[96]{0:T(128)S(1)} %reshape.15.selection_ref, bf16[512,256]{1,0:T(8,128)(2,1)S(1)} %copy-done.2, bf16[512,256]{1,0:T(8,128)(2,1)S(1)} %copy-done, bf16[512,256]{1,0:T(8,128)(2,1)S(1)} %copy-done.1, bf16[512,256]{1,0:T(8,128)(2,1)S(1)} %copy-done.3), custom_call_target="tpu_custom_call" | custom-call | flops 268435456 | bytes 4194304 | tf_op jit(solution)/shard_map/own_forward/pallas_call | solution.py:366
  12.8 7.9 %all-to-all-done.held_ref = bf16[16,2,32,256]{3,2,1,0:T(8,128)(2,1)S(1)} async-done(((bf16[16,2,32,256]{3,2,1,0:T(8,128)(2,1)}), bf16[16,2,32,256]{3,2,1,0:T(8,128)(2,1)S(1)}, u32[]{:S(2)}, u32[]{:S(2)}) %all-to-all-start) | async-done | bytes 524320 | tf_op jit(solution)/shard_map/all_to_all | solution.py:335
  20.7 1.9 %pick.1 = bf16[16,2,3,32,256]{4,3,2,1,0:T(8,128)(2,1)} custom-call(s32[96]{0:T(128)S(1)} %get-tuple-element.17.selection_ref, bf16[16,2,32,256]{3,2,1,0:T(8,128)(2,1)S(1)} %all-to-all-done.held_ref), custom_call_target="tpu_custom_call" | custom-call | bytes 4194304 | tf_op jit(solution)/shard_map/pick/pallas_call | solution.py:379
  22.6 3.7 %all-to-all-start.1 = ((bf16[16,2,3,32,256]{4,3,2,1,0:T(8,128)(2,1)}), bf16[16,2,3,32,256]{4,3,2,1,0:T(8,128)(2,1)S(1)}, u32[]{:S(2)}, u32[]{:S(2)}) async-start(bf16[16,2,3,32,256]{4,3,2,1,0:T(8,128)(2,1)} %pick.1), calls=%async_computation.1 | async-start | bytes 3145728 | tf_op jit(solution)/shard_map/all_to_all | solution.py:335
  26.3 0.1 pad_add_fusion.position_ref.place_ref
  26.4 20.4 %all-to-all-done.1.listed_ref = bf16[16,2,3,32,256]{4,3,2,1,0:T(8,128)(2,1)S(1)} async-done(((bf16[16,2,3,32,256]{4,3,2,1,0:T(8,128)(2,1)}), bf16[16,2,3,32,256]{4,3,2,1,0:T(8,128)(2,1)S(1)}, u32[]{:S(2)}, u32[]{:S(2)}) %all-to-all-start.1) | async-done | bytes 1572896 | tf_op jit(solution)/shard_map/all_to_all | solution.py:335
  46.8 7.9 %far.1 = (bf16[16,2,2,3,32,128]{5,4,3,2,1,0:T(8,128)(2,1)}, bf16[2,128,512]{2,1,0:T(8,128)(2,1)S(1)}, f32[2,8,512]{2,1,0:T(8,128)S(1)}) custom-call(s32[96]{0:T(128)S(1)} %get-tuple-element.17.selection_ref, s32[3]{0:T(128)S(1)} %pad_add_fusion.position_ref.place_ref, bf16[512,256]{1,0:T(8,128)(2,1)S(1)} %copy-done.2, bf16[512,256]{1,0:T(8,128)(2,1)S(1)} %copy-done.3, ...), custom_call_target="tpu_custom_call" | custom-call | flops 2013265920 | bytes 4194304 | tf_op jit(solution)/shard_map/far/pallas_call | solution.py:391
  54.7 0.0 copy-start.4
  54.7 0.6 copy-done.4
  55.3 5.6 %all-to-all-start.2 = ((bf16[16,2,2,3,32,128]{5,4,3,2,1,0:T(8,128)(2,1)}), bf16[16,2,2,3,32,128]{5,4,3,2,1,0:T(8,128)(2,1)S(1)}, u32[]{:S(2)}, u32[]{:S(2)}) async-start(bf16[16,2,2,3,32,128]{5,4,3,2,1,0:T(8,128)(2,1)} %get-tuple-element.22), calls=%async_computation.2 | async-start | bytes 3145728 | tf_op jit(solution)/shard_map/all_to_all | solution.py:335
  60.9 0.0 copy-start.5
  61.0 0.7 copy-done.5
  61.7 2.4 %own_backward.1 = (bf16[16,2,32,256]{3,2,1,0:T(8,128)(2,1)S(1)}, bf16[64,256]{1,0:T(8,128)(2,1)S(1)}, bf16[64,256]{1,0:T(8,128)(2,1)S(1)}, bf16[64,256]{1,0:T(8,...) custom-call(s32[3]{0:T(128)S(1)} %pad_add_fusion.position_ref.place_, ...), custom_call_target="tpu_custom_call" | custom-call | flops 671088640 | bytes 4194304 | tf_op jit(solution)/shard_map/own_backward/pallas_call | solution.py:412
  64.1 7.0 %collective-permute-start = (bf16[64,256]{1,0:T(8,128)(2,1)S(1)}, bf16[64,256]{1,0:T(8,128)(2,1)S(1)}, u32[]{:S(2)}, u32[]{:S(2)}) collective-permute-start(bf16[64,256]{1,0:T(8,128)(2,1)S(1)} %get-tuple-element.23), channel_id=1, source_target_pairs={{0,8},{1,9},{2,10},{3,11},{4,12},{5,13},{6,14},{7,15},{8,0},{9,1},... | collective-permute-start | bytes 98312 | tf_op jit(solution)/shard_map/ppermute | solution.py:428
  71.1 1.6 %collective-permute-start.1 = (bf16[64,256]{1,0:T(8,128)(2,1)S(1)}, bf16[64,256]{1,0:T(8,128)(2,1)S(1)}, u32[]{:S(2)}, u32[]{:S(2)}) collective-permute-start(bf16[64,256]{1,0:T(8,128)(2,1)S(1)} %get-tuple-element.24), channel_id=1, source_target_pairs={{0,6},{1,7},{2,8},{3,9},{4,10},{5,11},{6,12},{7,13},{8,14},{9,15},... | collective-permute-start | bytes 98312 | tf_op jit(solution)/shard_map/ppermute | solution.py:428
  72.8 2.8 %collective-permute-start.2 = (bf16[64,256]{1,0:T(8,128)(2,1)S(1)}, bf16[64,256]{1,0:T(8,128)(2,1)S(1)}, u32[]{:S(2)}, u32[]{:S(2)}) collective-permute-start(bf16[64,256]{1,0:T(8,128)(2,1)S(1)} %get-tuple-element.25), channel_id=1, source_target_pairs={{0,10},{1,11},{2,12},{3,13},{4,14},{5,15},{6,0},{7,1},{8,2},{9,3},... | collective-permute-start | bytes 98312 | tf_op jit(solution)/shard_map/ppermute | solution.py:428
  75.6 1.2 collective-permute-start.3
  76.8 2.4 %collective-permute-start.4 = (bf16[64,256]{1,0:T(8,128)(2,1)S(1)}, bf16[64,256]{1,0:T(8,128)(2,1)S(1)}, u32[]{:S(2)}, u32[]{:S(2)}) collective-permute-start(bf16[64,256]{1,0:T(8,128)(2,1)S(1)} %get-tuple-element.27), channel_id=1, source_target_pairs={{0,12},{1,13},{2,14},{3,15},{4,0},{5,1},{6,2},{7,3},{8,4},{9,5},{1... | collective-permute-start | bytes 98312 | tf_op jit(solution)/shard_map/ppermute | solution.py:428
  79.2 0.0 collective-permute-done.refs_0_.refs_4_
  79.2 0.0 collective-permute-done.1.refs_1_.refs_3_
  79.2 0.0 collective-permute-done.2.refs_2_.refs_5_
  79.2 1.4 %collective-permute-done.3.refs_3_.refs_2_ = bf16[64,256]{1,0:T(8,128)(2,1)S(1)} collective-permute-done((bf16[64,256]{1,0:T(8,128)(2,1)S(1)}, bf16[64,256]{1,0:T(8,128)(2,1)S(1)}, u32[]{:S(2)}, u32[]{:S(2)}) %collective-permute-start.3) | collective-permute-done | bytes 32800 | tf_op jit(solution)/shard_map/ppermute | solution.py:428
  80.6 0.3 collective-permute-done.4.refs_4_.refs_6_
  80.9 0.6 all-to-all-done.2.terms_ref
  81.5 1.7 %reduce.1 = bf16[16,2,32,256]{3,2,1,0:T(8,128)(2,1)} custom-call(s32[96]{0:T(128)S(1)} %get-tuple-element.17.selection_ref, bf16[16,2,2,3,32,128]{5,4,3,2,1,0:T(8,128)(2,1)S(1)} %all-to-all-done.2.terms_ref, bf16[64,256]{1,0:T(8,128)(2,1)S(1)} %collective-permute-done.refs_0_.refs_4_, bf16[64,256]{1,0:T(8,128)(2,1)S(1)} %collective-permute-done.1.refs_1_.refs_3_, ...), custom_call_target="tpu_custom_call" | custom-call | bytes 4194304 | tf_op jit(solution)/shard_map/reduce/pallas_call | solution.py:434
  83.2 6.3 %all-to-all-start.3 = ((bf16[16,2,32,256]{3,2,1,0:T(8,128)(2,1)}), bf16[16,2,32,256]{3,2,1,0:T(8,128)(2,1)S(1)}, u32[]{:S(2)}, u32[]{:S(2)}) async-start(bf16[16,2,32,256]{3,2,1,0:T(8,128)(2,1)} %reduce.1), calls=%async_computation.3 | async-start | bytes 1048576 | tf_op jit(solution)/shard_map/all_to_all | solution.py:335
  89.5 1.1 collective-permute-start.5
  90.5 4.0 %collective-permute-start.6 = (bf16[64,256]{1,0:T(8,128)(2,1)S(1)}, bf16[64,256]{1,0:T(8,128)(2,1)S(1)}, u32[]{:S(2)}, u32[]{:S(2)}) collective-permute-start(bf16[64,256]{1,0:T(8,128)(2,1)S(1)} %get-tuple-element.30), channel_id=1, source_target_pairs={{0,14},{1,15},{2,0},{3,1},{4,2},{5,3},{6,4},{7,5},{8,6},{9,7},{10,... | collective-permute-start | bytes 98312 | tf_op jit(solution)/shard_map/ppermute | solution.py:428
  94.6 1.2 collective-permute-done.5.refs_1_
  95.8 0.0 collective-permute-done.6.refs_7_
  95.8 0.6 join.1
  96.3 3.3 %collective-permute-start.7 = (bf16[8,32,256]{2,1,0:T(8,128)(2,1)S(1)}, bf16[8,32,256]{2,1,0:T(8,128)(2,1)S(1)}, u32[]{:S(2)}, u32[]{:S(2)}) collective-permute-start(bf16[8,32,256]{2,1,0:T(8,128)(2,1)S(1)} %join.1), channel_id=1, source_target_pairs={{0,1},{1,0},{2,3},{3,2},{4,5},{5,4},{6,7},{7,6},{8,9},{9,8},{10,11... | collective-permute-start | bytes 393224 | tf_op jit(solution)/shard_map/ppermute | solution.py:451
  99.7 1.0 collective-permute-done.7.after_ref.other_ref
  100.7 0.0 all-to-all-done.3.others_ref
  100.7 0.1 finish.1
  100.8 26.3 %all_to_all.25.parts_ref = bf16[16,2,32,256]{3,2,1,0:T(8,128)(2,1)S(1)} all-to-all(bf16[16,2,32,256]{3,2,1,0:T(8,128)(2,1)S(1)} %finish.1), channel_id=1, replica_groups=mesh['chain'=16,'heads'=16] {'heads'}, dimensions={0} | all-to-all | bytes 1048576 | tf_op jit(solution)/shard_map/all_to_all | solution.py:335
  127.1 1.8 %lay.1 = (bf16[32,4096]{1,0:T(8,128)(2,1)}, bf16[32,4096]{1,0:T(8,128)(2,1)}, bf16[32,4096]{1,0:T(8,128)(2,1)}) custom-call(s32[3]{0:T(128)S(1)} %pad_add_fusion.position_ref.place_ref, bf16[16,2,32,256]{3,2,1,0:T(8,128)(2,1)S(1)} %all_to_all.25.parts_ref, bf16[8,32,256]{2,1,0:T(8,128)(2,1)S(1)} %collective-permute-done.7.after_ref.other_ref, ...), custom_call_target="tpu_custom_call" | custom-call | bytes 4194304 | tf_op jit(solution)/shard_map/lay/pallas_call | solution.py:467
Async XLA Ops:
  0.6 9.8 %copy-start = (bf16[512,256]{1,0:T(8,128)(2,1)S(1)}, bf16[512,256]{1,0:T(8,128)(2,1)}, u32[]{:S(2)}) copy-start(bf16[512,256]{1,0:T(8,128)(2,1)} %key_ref.3) | copy-start | bytes 786436
  0.6 9.8 %copy-start.1 = (bf16[512,256]{1,0:T(8,128)(2,1)S(1)}, bf16[512,256]{1,0:T(8,128)(2,1)}, u32[]{:S(2)}) copy-start(bf16[512,256]{1,0:T(8,128)(2,1)} %value_ref.3) | copy-start | bytes 786436
  0.7 9.6 %copy-start.6 = (s32[16,2,3]{0,1,2:T(2,128)S(1)}, s32[16,2,3]{0,1,2:T(2,128)}, u32[]{:S(2)}) copy-start(s32[16,2,3]{0,1,2:T(2,128)} %param.9) | copy-start | bytes 1156
  0.7 9.8 %copy-start.3 = (bf16[512,256]{1,0:T(8,128)(2,1)S(1)}, bf16[512,256]{1,0:T(8,128)(2,1)}, u32[]{:S(2)}) copy-start(bf16[512,256]{1,0:T(8,128)(2,1)} %grad_ref.5) | copy-start | bytes 786436
  0.7 9.8 %copy-start.2 = (bf16[512,256]{1,0:T(8,128)(2,1)S(1)}, bf16[512,256]{1,0:T(8,128)(2,1)}, u32[]{:S(2)}) copy-start(bf16[512,256]{1,0:T(8,128)(2,1)} %query_ref.5) | copy-start | bytes 786436
  2.6 18.1 %all-to-all-start = ((bf16[16,2,32,256]{3,2,1,0:T(8,128)(2,1)}), bf16[16,2,32,256]{3,2,1,0:T(8,128)(2,1)S(1)}, u32[]{:S(2)}, u32[]{:S(2)}) async-start(bf16[16,2,32,256]{3,2,1,0:T(8,128)(2,1)} %stack.17), calls=%async_computation | async-start | bytes 1048576 | tf_op jit(solution)/shard_map/all_to_all | solution.py:335
  22.6 24.3 %all-to-all-start.1 = ((bf16[16,2,3,32,256]{4,3,2,1,0:T(8,128)(2,1)}), bf16[16,2,3,32,256]{4,3,2,1,0:T(8,128)(2,1)S(1)}, u32[]{:S(2)}, u32[]{:S(2)}) async-start(bf16[16,2,3,32,256]{4,3,2,1,0:T(8,128)(2,1)} %pick.1), calls=%async_computation.1 | async-start | bytes 3145728 | tf_op jit(solution)/shard_map/all_to_all | solution.py:335
  54.7 0.6 copy-start.4
  55.3 26.2 %all-to-all-start.2 = ((bf16[16,2,2,3,32,128]{5,4,3,2,1,0:T(8,128)(2,1)}), bf16[16,2,2,3,32,128]{5,4,3,2,1,0:T(8,128)(2,1)S(1)}, u32[]{:S(2)}, u32[]{:S(2)}) async-start(bf16[16,2,2,3,32,128]{5,4,3,2,1,0:T(8,128)(2,1)} %get-tuple-element.22), calls=%async_computation.2 | async-start | bytes 3145728 | tf_op jit(solution)/shard_map/all_to_all | solution.py:335
  60.9 0.8 copy-start.5
  64.1 15.1 %collective-permute-start = (bf16[64,256]{1,0:T(8,128)(2,1)S(1)}, bf16[64,256]{1,0:T(8,128)(2,1)S(1)}, u32[]{:S(2)}, u32[]{:S(2)}) collective-permute-start(bf16[64,256]{1,0:T(8,128)(2,1)S(1)} %get-tuple-element.23), channel_id=1, source_target_pairs={{0,8},{1,9},{2,10},{3,11},{4,12},{5,13},{6,14},{7,15},{8,0},{9,1},... | collective-permute-start | bytes 98312 | tf_op jit(solution)/shard_map/ppermute | solution.py:428
  71.1 8.1 %collective-permute-start.1 = (bf16[64,256]{1,0:T(8,128)(2,1)S(1)}, bf16[64,256]{1,0:T(8,128)(2,1)S(1)}, u32[]{:S(2)}, u32[]{:S(2)}) collective-permute-start(bf16[64,256]{1,0:T(8,128)(2,1)S(1)} %get-tuple-element.24), channel_id=1, source_target_pairs={{0,6},{1,7},{2,8},{3,9},{4,10},{5,11},{6,12},{7,13},{8,14},{9,15},... | collective-permute-start | bytes 98312 | tf_op jit(solution)/shard_map/ppermute | solution.py:428
  72.8 6.4 %collective-permute-start.2 = (bf16[64,256]{1,0:T(8,128)(2,1)S(1)}, bf16[64,256]{1,0:T(8,128)(2,1)S(1)}, u32[]{:S(2)}, u32[]{:S(2)}) collective-permute-start(bf16[64,256]{1,0:T(8,128)(2,1)S(1)} %get-tuple-element.25), channel_id=1, source_target_pairs={{0,10},{1,11},{2,12},{3,13},{4,14},{5,15},{6,0},{7,1},{8,2},{9,3},... | collective-permute-start | bytes 98312 | tf_op jit(solution)/shard_map/ppermute | solution.py:428
  75.6 5.0 %collective-permute-start.3 = (bf16[64,256]{1,0:T(8,128)(2,1)S(1)}, bf16[64,256]{1,0:T(8,128)(2,1)S(1)}, u32[]{:S(2)}, u32[]{:S(2)}) collective-permute-start(bf16[64,256]{1,0:T(8,128)(2,1)S(1)} %get-tuple-element.26), channel_id=1, source_target_pairs={{0,4},{1,5},{2,6},{3,7},{4,8},{5,9},{6,10},{7,11},{8,12},{9,13},{1... | collective-permute-start | bytes 98312 | tf_op jit(solution)/shard_map/ppermute | solution.py:428
  76.8 4.1 %collective-permute-start.4 = (bf16[64,256]{1,0:T(8,128)(2,1)S(1)}, bf16[64,256]{1,0:T(8,128)(2,1)S(1)}, u32[]{:S(2)}, u32[]{:S(2)}) collective-permute-start(bf16[64,256]{1,0:T(8,128)(2,1)S(1)} %get-tuple-element.27), channel_id=1, source_target_pairs={{0,12},{1,13},{2,14},{3,15},{4,0},{5,1},{6,2},{7,3},{8,4},{9,5},{1... | collective-permute-start | bytes 98312 | tf_op jit(solution)/shard_map/ppermute | solution.py:428
  83.2 17.5 %all-to-all-start.3 = ((bf16[16,2,32,256]{3,2,1,0:T(8,128)(2,1)}), bf16[16,2,32,256]{3,2,1,0:T(8,128)(2,1)S(1)}, u32[]{:S(2)}, u32[]{:S(2)}) async-start(bf16[16,2,32,256]{3,2,1,0:T(8,128)(2,1)} %reduce.1), calls=%async_computation.3 | async-start | bytes 1048576 | tf_op jit(solution)/shard_map/all_to_all | solution.py:335
  89.5 6.3 %collective-permute-start.5 = (bf16[64,256]{1,0:T(8,128)(2,1)S(1)}, bf16[64,256]{1,0:T(8,128)(2,1)S(1)}, u32[]{:S(2)}, u32[]{:S(2)}) collective-permute-start(bf16[64,256]{1,0:T(8,128)(2,1)S(1)} %get-tuple-element.29), channel_id=1, source_target_pairs={{0,2},{1,3},{2,4},{3,5},{4,6},{5,7},{6,8},{7,9},{8,10},{9,11},{10,... | collective-permute-start | bytes 98312 | tf_op jit(solution)/shard_map/ppermute | solution.py:428
  90.5 5.2 %collective-permute-start.6 = (bf16[64,256]{1,0:T(8,128)(2,1)S(1)}, bf16[64,256]{1,0:T(8,128)(2,1)S(1)}, u32[]{:S(2)}, u32[]{:S(2)}) collective-permute-start(bf16[64,256]{1,0:T(8,128)(2,1)S(1)} %get-tuple-element.30), channel_id=1, source_target_pairs={{0,14},{1,15},{2,0},{3,1},{4,2},{5,3},{6,4},{7,5},{8,6},{9,7},{10,... | collective-permute-start | bytes 98312 | tf_op jit(solution)/shard_map/ppermute | solution.py:428
  96.3 4.3 %collective-permute-start.7 = (bf16[8,32,256]{2,1,0:T(8,128)(2,1)S(1)}, bf16[8,32,256]{2,1,0:T(8,128)(2,1)S(1)}, u32[]{:S(2)}, u32[]{:S(2)}) collective-permute-start(bf16[8,32,256]{2,1,0:T(8,128)(2,1)S(1)} %join.1), channel_id=1, source_target_pairs={{0,1},{1,0},{2,3},{3,2},{4,5},{5,4},{6,7},{7,6},{8,9},{9,8},{10,11... | collective-permute-start | bytes 393224 | tf_op jit(solution)/shard_map/ppermute | solution.py:451

commit v13 on v12

--- a/solution.py
+++ b/solution.py
@@ -16,7 +16,7 @@
 TILE = 256
 STATS = 8
 SUBLANES = 8
-EARLY = 5
+EARLY = 6
 MIB = 1 << 20
 
 

time: 130 us -> 129 us (level)
  local copies, waits for them, and re-layouts: 1.6 us -> 0.23 us
    ppermute x7, waiting for transfers between devices: 2.93 us -> 4.38 us  [to_plane(): return lax.ppermute(piece, 'heads', pairs)]
    unnamed x15 -> x11, local copies, waits for them, and re-layouts: 1.48 us -> 0.12 us
where the time goes in v13:
time: 129 us
  starting transfers between devices  47.4 us (37%)
  waiting for transfers between devices  33.7 us (26%)
  blocking collectives  25.5 us (20%)
  Pallas kernels  20.7 us (16%)
    all_to_all x4, waiting for transfers between devices, swap(): return lax.all_to_all(array, axis, split_axis=0, concat_axis=0, tiled=True)  28.3 us
    all_to_all x1, blocking collectives, swap(): return lax.all_to_all(array, axis, split_axis=0, concat_axis=0, tiled=True)  25.5 us
    all_to_all x4, starting transfers between devices, swap(): return lax.all_to_all(array, axis, split_axis=0, concat_axis=0, tiled=True)  23.4 us
    ppermute x7, starting transfers between devices, to_plane(): return lax.ppermute(piece, 'heads', pairs)  19.5 us
    pallas_call x1, Pallas kernels, on_device(): call(far_kernel, 'far', [smem, smem] + [vmem] * 4, (vmem, vmem, vmem), (j...  7.95 us
    ppermute x1, starting transfers between devices, on_device(): lax.ppermute(joined, 'heads', [(one, one ^ 1) for one in range(spread)])  4.43 us
    ppermute x7, waiting for transfers between devices, to_plane(): return lax.ppermute(piece, 'heads', pairs)  4.38 us
  transfers between devices with their start and end apart: 12, of which 7 were waited for; matrix products, arithmetic and copies ran while one was open for 0% of the time, Pallas kernels for 4%

profile of v13, /device:TPU:1, one launch (start us, length us, event | category | flops | bytes accessed | tf_op | source)
XLA Modules:
  0.0 128.5 jit_solution(2162028049487389999)
XLA Ops:
  0.6 0.0 copy-start
  0.6 0.0 copy-start.1
  0.7 0.0 copy-start.4
  0.7 0.0 copy-start.3
  0.7 0.0 copy-start.2
  0.7 1.9 %stack.17 = bf16[16,2,32,256]{3,2,1,0:T(8,128)(2,1)} custom-call(bf16[16,32,256]{2,1,0:T(8,128)(2,1)} %bitcast.5, bf16[16,32,256]{2,1,0:T(8,128)(2,1)} %bitcast.6), custom_call_target="tpu_custom_call" | custom-call | bytes 4194304 | tf_op jit(solution)/shard_map/stack/pallas_call | solution.py:352
  2.6 7.6 %all-to-all-start = ((bf16[16,2,32,256]{3,2,1,0:T(8,128)(2,1)}), bf16[16,2,32,256]{3,2,1,0:T(8,128)(2,1)S(1)}, u32[]{:S(2)}, u32[]{:S(2)}) async-start(bf16[16,2,32,256]{3,2,1,0:T(8,128)(2,1)} %stack.17), calls=%async_computation | async-start | bytes 1048576 | tf_op jit(solution)/shard_map/all_to_all | solution.py:335
  10.2 0.0 copy-done.4
  10.2 0.1 copy.9
  10.3 0.1 reshape.15.selection_ref
  10.4 0.0 copy-done
  10.4 0.0 copy-done.1
  10.4 0.0 copy-done.3
  10.5 0.0 copy-done.2
  10.5 2.4 %own_forward.1 = (s32[96]{0:T(128)S(1)}, f32[2,8,512]{2,1,0:T(8,128)S(1)}) custom-call(s32[96]{0:T(128)S(1)} %reshape.15.selection_ref, bf16[512,256]{1,0:T(8,128)(2,1)S(1)} %copy-done.2, bf16[512,256]{1,0:T(8,128)(2,1)S(1)} %copy-done, bf16[512,256]{1,0:T(8,128)(2,1)S(1)} %copy-done.1, bf16[512,256]{1,0:T(8,128)(2,1)S(1)} %copy-done.3), custom_call_target="tpu_custom_call" | custom-call | flops 268435456 | bytes 4194304 | tf_op jit(solution)/shard_map/own_forward/pallas_call | solution.py:366
  12.9 7.9 %all-to-all-done.held_ref = bf16[16,2,32,256]{3,2,1,0:T(8,128)(2,1)S(1)} async-done(((bf16[16,2,32,256]{3,2,1,0:T(8,128)(2,1)}), bf16[16,2,32,256]{3,2,1,0:T(8,128)(2,1)S(1)}, u32[]{:S(2)}, u32[]{:S(2)}) %all-to-all-start) | async-done | bytes 524320 | tf_op jit(solution)/shard_map/all_to_all | solution.py:335
  20.7 1.9 %pick.1 = bf16[16,2,3,32,256]{4,3,2,1,0:T(8,128)(2,1)} custom-call(s32[96]{0:T(128)S(1)} %get-tuple-element.17.selection_ref, bf16[16,2,32,256]{3,2,1,0:T(8,128)(2,1)S(1)} %all-to-all-done.held_ref), custom_call_target="tpu_custom_call" | custom-call | bytes 4194304 | tf_op jit(solution)/shard_map/pick/pallas_call | solution.py:379
  22.6 3.7 %all-to-all-start.1 = ((bf16[16,2,3,32,256]{4,3,2,1,0:T(8,128)(2,1)}), bf16[16,2,3,32,256]{4,3,2,1,0:T(8,128)(2,1)S(1)}, u32[]{:S(2)}, u32[]{:S(2)}) async-start(bf16[16,2,3,32,256]{4,3,2,1,0:T(8,128)(2,1)} %pick.1), calls=%async_computation.1 | async-start | bytes 3145728 | tf_op jit(solution)/shard_map/all_to_all | solution.py:335
  26.3 0.1 pad_add_fusion.position_ref.place_ref
  26.4 20.4 %all-to-all-done.1.listed_ref = bf16[16,2,3,32,256]{4,3,2,1,0:T(8,128)(2,1)S(1)} async-done(((bf16[16,2,3,32,256]{4,3,2,1,0:T(8,128)(2,1)}), bf16[16,2,3,32,256]{4,3,2,1,0:T(8,128)(2,1)S(1)}, u32[]{:S(2)}, u32[]{:S(2)}) %all-to-all-start.1) | async-done | bytes 1572896 | tf_op jit(solution)/shard_map/all_to_all | solution.py:335
  46.8 8.0 %far.1 = (bf16[16,2,2,3,32,128]{5,4,3,2,1,0:T(8,128)(2,1)}, bf16[2,128,512]{2,1,0:T(8,128)(2,1)S(1)}, f32[2,8,512]{2,1,0:T(8,128)S(1)}) custom-call(s32[96]{0:T(128)S(1)} %get-tuple-element.17.selection_ref, s32[3]{0:T(128)S(1)} %pad_add_fusion.position_ref.place_ref, bf16[512,256]{1,0:T(8,128)(2,1)S(1)} %copy-done.2, bf16[512,256]{1,0:T(8,128)(2,1)S(1)} %copy-done.3, ...), custom_call_target="tpu_custom_call" | custom-call | flops 2013265920 | bytes 4194304 | tf_op jit(solution)/shard_map/far/pallas_call | solution.py:391
  54.8 5.6 %all-to-all-start.2 = ((bf16[16,2,2,3,32,128]{5,4,3,2,1,0:T(8,128)(2,1)}), bf16[16,2,2,3,32,128]{5,4,3,2,1,0:T(8,128)(2,1)S(1)}, u32[]{:S(2)}, u32[]{:S(2)}) async-start(bf16[16,2,2,3,32,128]{5,4,3,2,1,0:T(8,128)(2,1)} %get-tuple-element.22), calls=%async_computation.2 | async-start | bytes 3145728 | tf_op jit(solution)/shard_map/all_to_all | solution.py:335
  60.4 2.4 %own_backward.1 = (bf16[16,2,32,256]{3,2,1,0:T(8,128)(2,1)S(1)}, bf16[64,256]{1,0:T(8,128)(2,1)S(1)}, bf16[64,256]{1,0:T(8,128)(2,1)S(1)}, bf16[64,256]{1,0:T(8,...) custom-call(s32[3]{0:T(128)S(1)} %pad_add_fusion.position_ref.place_, ...), custom_call_target="tpu_custom_call" | custom-call | flops 671088640 | bytes 4194304 | tf_op jit(solution)/shard_map/own_backward/pallas_call | solution.py:412
  62.8 7.0 %collective-permute-start = (bf16[64,256]{1,0:T(8,128)(2,1)S(1)}, bf16[64,256]{1,0:T(8,128)(2,1)S(1)}, u32[]{:S(2)}, u32[]{:S(2)}) collective-permute-start(bf16[64,256]{1,0:T(8,128)(2,1)S(1)} %get-tuple-element.23), channel_id=1, source_target_pairs={{0,8},{1,9},{2,10},{3,11},{4,12},{5,13},{6,14},{7,15},{8,0},{9,1},... | collective-permute-start | bytes 98312 | tf_op jit(solution)/shard_map/ppermute | solution.py:428
  69.8 1.6 %collective-permute-start.1 = (bf16[64,256]{1,0:T(8,128)(2,1)S(1)}, bf16[64,256]{1,0:T(8,128)(2,1)S(1)}, u32[]{:S(2)}, u32[]{:S(2)}) collective-permute-start(bf16[64,256]{1,0:T(8,128)(2,1)S(1)} %get-tuple-element.24), channel_id=1, source_target_pairs={{0,6},{1,7},{2,8},{3,9},{4,10},{5,11},{6,12},{7,13},{8,14},{9,15},... | collective-permute-start | bytes 98312 | tf_op jit(solution)/shard_map/ppermute | solution.py:428
  71.5 2.8 %collective-permute-start.2 = (bf16[64,256]{1,0:T(8,128)(2,1)S(1)}, bf16[64,256]{1,0:T(8,128)(2,1)S(1)}, u32[]{:S(2)}, u32[]{:S(2)}) collective-permute-start(bf16[64,256]{1,0:T(8,128)(2,1)S(1)} %get-tuple-element.25), channel_id=1, source_target_pairs={{0,10},{1,11},{2,12},{3,13},{4,14},{5,15},{6,0},{7,1},{8,2},{9,3},... | collective-permute-start | bytes 98312 | tf_op jit(solution)/shard_map/ppermute | solution.py:428
  74.3 1.2 collective-permute-start.3
  75.5 2.4 %collective-permute-start.4 = (bf16[64,256]{1,0:T(8,128)(2,1)S(1)}, bf16[64,256]{1,0:T(8,128)(2,1)S(1)}, u32[]{:S(2)}, u32[]{:S(2)}) collective-permute-start(bf16[64,256]{1,0:T(8,128)(2,1)S(1)} %get-tuple-element.27), channel_id=1, source_target_pairs={{0,12},{1,13},{2,14},{3,15},{4,0},{5,1},{6,2},{7,3},{8,4},{9,5},{1... | collective-permute-start | bytes 98312 | tf_op jit(solution)/shard_map/ppermute | solution.py:428
  77.9 0.0 collective-permute-done.refs_0_.refs_4_
  77.9 0.7 collective-permute-start.5
  78.6 0.0 collective-permute-done.1.refs_1_.refs_3_
  78.6 0.0 collective-permute-done.2.refs_2_.refs_5_
  78.6 0.8 collective-permute-done.3.refs_3_.refs_2_
  79.5 0.1 collective-permute-done.4.refs_4_.refs_6_
  79.6 2.4 %collective-permute-done.5.refs_5_.refs_1_ = bf16[64,256]{1,0:T(8,128)(2,1)S(1)} collective-permute-done((bf16[64,256]{1,0:T(8,128)(2,1)S(1)}, bf16[64,256]{1,0:T(8,128)(2,1)S(1)}, u32[]{:S(2)}, u32[]{:S(2)}) %collective-permute-start.5) | collective-permute-done | bytes 32800 | tf_op jit(solution)/shard_map/ppermute | solution.py:428
  82.0 0.0 all-to-all-done.2.terms_ref
  82.0 1.7 %reduce.1 = bf16[16,2,32,256]{3,2,1,0:T(8,128)(2,1)} custom-call(s32[96]{0:T(128)S(1)} %get-tuple-element.17.selection_ref, bf16[16,2,2,3,32,128]{5,4,3,2,1,0:T(8,128)(2,1)S(1)} %all-to-all-done.2.terms_ref, bf16[64,256]{1,0:T(8,128)(2,1)S(1)} %collective-permute-done.refs_0_.refs_4_, bf16[64,256]{1,0:T(8,128)(2,1)S(1)} %collective-permute-done.1.refs_1_.refs_3_, ...), custom_call_target="tpu_custom_call" | custom-call | bytes 4194304 | tf_op jit(solution)/shard_map/reduce/pallas_call | solution.py:434
  83.7 6.5 %all-to-all-start.3 = ((bf16[16,2,32,256]{3,2,1,0:T(8,128)(2,1)}), bf16[16,2,32,256]{3,2,1,0:T(8,128)(2,1)S(1)}, u32[]{:S(2)}, u32[]{:S(2)}) async-start(bf16[16,2,32,256]{3,2,1,0:T(8,128)(2,1)} %reduce.1), calls=%async_computation.3 | async-start | bytes 1048576 | tf_op jit(solution)/shard_map/all_to_all | solution.py:335
  90.2 3.7 %collective-permute-start.6 = (bf16[64,256]{1,0:T(8,128)(2,1)S(1)}, bf16[64,256]{1,0:T(8,128)(2,1)S(1)}, u32[]{:S(2)}, u32[]{:S(2)}) collective-permute-start(bf16[64,256]{1,0:T(8,128)(2,1)S(1)} %get-tuple-element.30), channel_id=1, source_target_pairs={{0,14},{1,15},{2,0},{3,1},{4,2},{5,3},{6,4},{7,5},{8,6},{9,7},{10,... | collective-permute-start | bytes 98312 | tf_op jit(solution)/shard_map/ppermute | solution.py:428
  93.9 1.0 collective-permute-done.6.refs_7_
  95.0 0.6 join.1
  95.5 4.4 %collective-permute-start.7 = (bf16[8,32,256]{2,1,0:T(8,128)(2,1)S(1)}, bf16[8,32,256]{2,1,0:T(8,128)(2,1)S(1)}, u32[]{:S(2)}, u32[]{:S(2)}) collective-permute-start(bf16[8,32,256]{2,1,0:T(8,128)(2,1)S(1)} %join.1), channel_id=1, source_target_pairs={{0,1},{1,0},{2,3},{3,2},{4,5},{5,4},{6,7},{7,6},{8,9},{9,8},{10,11... | collective-permute-start | bytes 393224 | tf_op jit(solution)/shard_map/ppermute | solution.py:451
  99.9 1.0 collective-permute-done.7.after_ref.other_ref
  100.9 0.0 all-to-all-done.3.others_ref
  100.9 0.1 finish.1
  101.1 25.5 %all_to_all.25.parts_ref = bf16[16,2,32,256]{3,2,1,0:T(8,128)(2,1)S(1)} all-to-all(bf16[16,2,32,256]{3,2,1,0:T(8,128)(2,1)S(1)} %finish.1), channel_id=1, replica_groups=mesh['chain'=16,'heads'=16] {'heads'}, dimensions={0} | all-to-all | bytes 1048576 | tf_op jit(solution)/shard_map/all_to_all | solution.py:335
  126.5 1.8 %lay.1 = (bf16[32,4096]{1,0:T(8,128)(2,1)}, bf16[32,4096]{1,0:T(8,128)(2,1)}, bf16[32,4096]{1,0:T(8,128)(2,1)}) custom-call(s32[3]{0:T(128)S(1)} %pad_add_fusion.position_ref.place_ref, bf16[16,2,32,256]{3,2,1,0:T(8,128)(2,1)S(1)} %all_to_all.25.parts_ref, bf16[8,32,256]{2,1,0:T(8,128)(2,1)S(1)} %collective-permute-done.7.after_ref.other_ref, ...), custom_call_target="tpu_custom_call" | custom-call | bytes 4194304 | tf_op jit(solution)/shard_map/lay/pallas_call | solution.py:467
Async XLA Ops:
  0.6 9.8 %copy-start = (bf16[512,256]{1,0:T(8,128)(2,1)S(1)}, bf16[512,256]{1,0:T(8,128)(2,1)}, u32[]{:S(2)}) copy-start(bf16[512,256]{1,0:T(8,128)(2,1)} %key_ref.3) | copy-start | bytes 786436
  0.6 9.8 %copy-start.1 = (bf16[512,256]{1,0:T(8,128)(2,1)S(1)}, bf16[512,256]{1,0:T(8,128)(2,1)}, u32[]{:S(2)}) copy-start(bf16[512,256]{1,0:T(8,128)(2,1)} %value_ref.3) | copy-start | bytes 786436
  0.7 9.6 %copy-start.4 = (s32[16,2,3]{0,1,2:T(2,128)S(1)}, s32[16,2,3]{0,1,2:T(2,128)}, u32[]{:S(2)}) copy-start(s32[16,2,3]{0,1,2:T(2,128)} %param.9) | copy-start | bytes 1156
  0.7 9.8 %copy-start.3 = (bf16[512,256]{1,0:T(8,128)(2,1)S(1)}, bf16[512,256]{1,0:T(8,128)(2,1)}, u32[]{:S(2)}) copy-start(bf16[512,256]{1,0:T(8,128)(2,1)} %grad_ref.5) | copy-start | bytes 786436
  0.7 9.8 %copy-start.2 = (bf16[512,256]{1,0:T(8,128)(2,1)S(1)}, bf16[512,256]{1,0:T(8,128)(2,1)}, u32[]{:S(2)}) copy-start(bf16[512,256]{1,0:T(8,128)(2,1)} %query_ref.5) | copy-start | bytes 786436
  2.6 18.1 %all-to-all-start = ((bf16[16,2,32,256]{3,2,1,0:T(8,128)(2,1)}), bf16[16,2,32,256]{3,2,1,0:T(8,128)(2,1)S(1)}, u32[]{:S(2)}, u32[]{:S(2)}) async-start(bf16[16,2,32,256]{3,2,1,0:T(8,128)(2,1)} %stack.17), calls=%async_computation | async-start | bytes 1048576 | tf_op jit(solution)/shard_map/all_to_all | solution.py:335
  22.6 24.3 %all-to-all-start.1 = ((bf16[16,2,3,32,256]{4,3,2,1,0:T(8,128)(2,1)}), bf16[16,2,3,32,256]{4,3,2,1,0:T(8,128)(2,1)S(1)}, u32[]{:S(2)}, u32[]{:S(2)}) async-start(bf16[16,2,3,32,256]{4,3,2,1,0:T(8,128)(2,1)} %pick.1), calls=%async_computation.1 | async-start | bytes 3145728 | tf_op jit(solution)/shard_map/all_to_all | solution.py:335
  54.8 27.2 %all-to-all-start.2 = ((bf16[16,2,2,3,32,128]{5,4,3,2,1,0:T(8,128)(2,1)}), bf16[16,2,2,3,32,128]{5,4,3,2,1,0:T(8,128)(2,1)S(1)}, u32[]{:S(2)}, u32[]{:S(2)}) async-start(bf16[16,2,2,3,32,128]{5,4,3,2,1,0:T(8,128)(2,1)} %get-tuple-element.22), calls=%async_computation.2 | async-start | bytes 3145728 | tf_op jit(solution)/shard_map/all_to_all | solution.py:335
  62.8 15.0 %collective-permute-start = (bf16[64,256]{1,0:T(8,128)(2,1)S(1)}, bf16[64,256]{1,0:T(8,128)(2,1)S(1)}, u32[]{:S(2)}, u32[]{:S(2)}) collective-permute-start(bf16[64,256]{1,0:T(8,128)(2,1)S(1)} %get-tuple-element.23), channel_id=1, source_target_pairs={{0,8},{1,9},{2,10},{3,11},{4,12},{5,13},{6,14},{7,15},{8,0},{9,1},... | collective-permute-start | bytes 98312 | tf_op jit(solution)/shard_map/ppermute | solution.py:428
  69.8 8.8 %collective-permute-start.1 = (bf16[64,256]{1,0:T(8,128)(2,1)S(1)}, bf16[64,256]{1,0:T(8,128)(2,1)S(1)}, u32[]{:S(2)}, u32[]{:S(2)}) collective-permute-start(bf16[64,256]{1,0:T(8,128)(2,1)S(1)} %get-tuple-element.24), channel_id=1, source_target_pairs={{0,6},{1,7},{2,8},{3,9},{4,10},{5,11},{6,12},{7,13},{8,14},{9,15},... | collective-permute-start | bytes 98312 | tf_op jit(solution)/shard_map/ppermute | solution.py:428
  71.5 7.2 %collective-permute-start.2 = (bf16[64,256]{1,0:T(8,128)(2,1)S(1)}, bf16[64,256]{1,0:T(8,128)(2,1)S(1)}, u32[]{:S(2)}, u32[]{:S(2)}) collective-permute-start(bf16[64,256]{1,0:T(8,128)(2,1)S(1)} %get-tuple-element.25), channel_id=1, source_target_pairs={{0,10},{1,11},{2,12},{3,13},{4,14},{5,15},{6,0},{7,1},{8,2},{9,3},... | collective-permute-start | bytes 98312 | tf_op jit(solution)/shard_map/ppermute | solution.py:428
  74.3 5.2 %collective-permute-start.3 = (bf16[64,256]{1,0:T(8,128)(2,1)S(1)}, bf16[64,256]{1,0:T(8,128)(2,1)S(1)}, u32[]{:S(2)}, u32[]{:S(2)}) collective-permute-start(bf16[64,256]{1,0:T(8,128)(2,1)S(1)} %get-tuple-element.26), channel_id=1, source_target_pairs={{0,4},{1,5},{2,6},{3,7},{4,8},{5,9},{6,10},{7,11},{8,12},{9,13},{1... | collective-permute-start | bytes 98312 | tf_op jit(solution)/shard_map/ppermute | solution.py:428
  75.5 4.1 %collective-permute-start.4 = (bf16[64,256]{1,0:T(8,128)(2,1)S(1)}, bf16[64,256]{1,0:T(8,128)(2,1)S(1)}, u32[]{:S(2)}, u32[]{:S(2)}) collective-permute-start(bf16[64,256]{1,0:T(8,128)(2,1)S(1)} %get-tuple-element.27), channel_id=1, source_target_pairs={{0,12},{1,13},{2,14},{3,15},{4,0},{5,1},{6,2},{7,3},{8,4},{9,5},{1... | collective-permute-start | bytes 98312 | tf_op jit(solution)/shard_map/ppermute | solution.py:428
  77.9 4.1 %collective-permute-start.5 = (bf16[64,256]{1,0:T(8,128)(2,1)S(1)}, bf16[64,256]{1,0:T(8,128)(2,1)S(1)}, u32[]{:S(2)}, u32[]{:S(2)}) collective-permute-start(bf16[64,256]{1,0:T(8,128)(2,1)S(1)} %get-tuple-element.28), channel_id=1, source_target_pairs={{0,2},{1,3},{2,4},{3,5},{4,6},{5,7},{6,8},{7,9},{8,10},{9,11},{10,... | collective-permute-start | bytes 98312 | tf_op jit(solution)/shard_map/ppermute | solution.py:428
  83.7 17.3 %all-to-all-start.3 = ((bf16[16,2,32,256]{3,2,1,0:T(8,128)(2,1)}), bf16[16,2,32,256]{3,2,1,0:T(8,128)(2,1)S(1)}, u32[]{:S(2)}, u32[]{:S(2)}) async-start(bf16[16,2,32,256]{3,2,1,0:T(8,128)(2,1)} %reduce.1), calls=%async_computation.3 | async-start | bytes 1048576 | tf_op jit(solution)/shard_map/all_to_all | solution.py:335
  90.2 4.7 %collective-permute-start.6 = (bf16[64,256]{1,0:T(8,128)(2,1)S(1)}, bf16[64,256]{1,0:T(8,128)(2,1)S(1)}, u32[]{:S(2)}, u32[]{:S(2)}) collective-permute-start(bf16[64,256]{1,0:T(8,128)(2,1)S(1)} %get-tuple-element.30), channel_id=1, source_target_pairs={{0,14},{1,15},{2,0},{3,1},{4,2},{5,3},{6,4},{7,5},{8,6},{9,7},{10,... | collective-permute-start | bytes 98312 | tf_op jit(solution)/shard_map/ppermute | solution.py:428
  95.5 5.4 %collective-permute-start.7 = (bf16[8,32,256]{2,1,0:T(8,128)(2,1)S(1)}, bf16[8,32,256]{2,1,0:T(8,128)(2,1)S(1)}, u32[]{:S(2)}, u32[]{:S(2)}) collective-permute-start(bf16[8,32,256]{2,1,0:T(8,128)(2,1)S(1)} %join.1), channel_id=1, source_target_pairs={{0,1},{1,0},{2,3},{3,2},{4,5},{5,4},{6,7},{7,6},{8,9},{9,8},{10,11... | collective-permute-start | bytes 393224 | tf_op jit(solution)/shard_map/ppermute | solution.py:451

commit v14 on v13

--- a/solution.py
+++ b/solution.py
@@ -16,7 +16,7 @@
 TILE = 256
 STATS = 8
 SUBLANES = 8
-EARLY = 6
+EARLY = 7
 MIB = 1 << 20
 
 

time: 129 us -> 130 us (level)
  blocking collectives: 25.5 us -> 27.9 us
    ppermute x7, waiting for transfers between devices: 4.38 us -> 1.42 us  [to_plane(): return lax.ppermute(piece, 'heads', pairs)]
    all_to_all x1, blocking collectives: 25.5 us -> 27.9 us  [swap(): return lax.all_to_all(array, axis, split_axis=0, concat_axis=0, tiled=True)]
    all_to_all x4, waiting for transfers between devices: 28.3 us -> 30.6 us  [swap(): return lax.all_to_all(array, axis, split_axis=0, concat_axis=0, tiled=True)]
    ppermute x7, starting transfers between devices: 19.5 us -> 17.7 us  [to_plane(): return lax.ppermute(piece, 'heads', pairs)]
  transfers between devices with their start and end apart: 12 -> 12, of which waited for: 7 -> 5; matrix products, arithmetic and copies ran while one was open for 0% -> 0% of each run, Pallas kernels for 4% -> 4%
where the time goes in v14:
time: 130 us; the launch traced here: 129 us
  starting transfers between devices  46.3 us (36%)
  waiting for transfers between devices  33 us (25%)
  blocking collectives  27.9 us (21%)
  Pallas kernels  20.7 us (16%)
    all_to_all x4, waiting for transfers between devices, swap(): return lax.all_to_all(array, axis, split_axis=0, concat_axis=0, tiled=True)  30.6 us
    all_to_all x1, blocking collectives, swap(): return lax.all_to_all(array, axis, split_axis=0, concat_axis=0, tiled=True)  27.9 us
    all_to_all x4, starting transfers between devices, swap(): return lax.all_to_all(array, axis, split_axis=0, concat_axis=0, tiled=True)  23.4 us
    ppermute x7, starting transfers between devices, to_plane(): return lax.ppermute(piece, 'heads', pairs)  17.7 us
    pallas_call x1, Pallas kernels, on_device(): call(far_kernel, 'far', [smem, smem] + [vmem] * 4, (vmem, vmem, vmem), (j...  7.95 us
    ppermute x1, starting transfers between devices, on_device(): lax.ppermute(joined, 'heads', [(one, one ^ 1) for one in range(spread)])  5.18 us
  transfers between devices with their start and end apart: 12, of which 5 were waited for; matrix products, arithmetic and copies ran while one was open for 0% of the time, Pallas kernels for 4%

profile of v14, /device:TPU:1, one launch (start us, length us, event | category | flops | bytes accessed | tf_op | source)
XLA Modules:
  0.0 129.2 jit_solution(14740776195069949181)
XLA Ops:
  0.6 0.0 copy-start
  0.6 0.0 copy-start.1
  0.7 0.0 copy-start.4
  0.7 0.0 copy-start.3
  0.7 0.0 copy-start.2
  0.7 1.9 %stack.17 = bf16[16,2,32,256]{3,2,1,0:T(8,128)(2,1)} custom-call(bf16[16,32,256]{2,1,0:T(8,128)(2,1)} %bitcast.5, bf16[16,32,256]{2,1,0:T(8,128)(2,1)} %bitcast.6), custom_call_target="tpu_custom_call" | custom-call | bytes 4194304 | tf_op jit(solution)/shard_map/stack/pallas_call | solution.py:352
  2.6 7.6 %all-to-all-start = ((bf16[16,2,32,256]{3,2,1,0:T(8,128)(2,1)}), bf16[16,2,32,256]{3,2,1,0:T(8,128)(2,1)S(1)}, u32[]{:S(2)}, u32[]{:S(2)}) async-start(bf16[16,2,32,256]{3,2,1,0:T(8,128)(2,1)} %stack.17), calls=%async_computation | async-start | bytes 1048576 | tf_op jit(solution)/shard_map/all_to_all | solution.py:335
  10.2 0.0 copy-done.4
  10.2 0.1 copy.9
  10.3 0.1 reshape.15.selection_ref
  10.4 0.0 copy-done
  10.4 0.0 copy-done.1
  10.4 0.0 copy-done.3
  10.5 0.0 copy-done.2
  10.5 2.4 %own_forward.1 = (s32[96]{0:T(128)S(1)}, f32[2,8,512]{2,1,0:T(8,128)S(1)}) custom-call(s32[96]{0:T(128)S(1)} %reshape.15.selection_ref, bf16[512,256]{1,0:T(8,128)(2,1)S(1)} %copy-done.2, bf16[512,256]{1,0:T(8,128)(2,1)S(1)} %copy-done, bf16[512,256]{1,0:T(8,128)(2,1)S(1)} %copy-done.1, bf16[512,256]{1,0:T(8,128)(2,1)S(1)} %copy-done.3), custom_call_target="tpu_custom_call" | custom-call | flops 268435456 | bytes 4194304 | tf_op jit(solution)/shard_map/own_forward/pallas_call | solution.py:366
  12.9 7.9 %all-to-all-done.held_ref = bf16[16,2,32,256]{3,2,1,0:T(8,128)(2,1)S(1)} async-done(((bf16[16,2,32,256]{3,2,1,0:T(8,128)(2,1)}), bf16[16,2,32,256]{3,2,1,0:T(8,128)(2,1)S(1)}, u32[]{:S(2)}, u32[]{:S(2)}) %all-to-all-start) | async-done | bytes 524320 | tf_op jit(solution)/shard_map/all_to_all | solution.py:335
  20.7 1.9 %pick.1 = bf16[16,2,3,32,256]{4,3,2,1,0:T(8,128)(2,1)} custom-call(s32[96]{0:T(128)S(1)} %get-tuple-element.17.selection_ref, bf16[16,2,32,256]{3,2,1,0:T(8,128)(2,1)S(1)} %all-to-all-done.held_ref), custom_call_target="tpu_custom_call" | custom-call | bytes 4194304 | tf_op jit(solution)/shard_map/pick/pallas_call | solution.py:379
  22.6 3.7 %all-to-all-start.1 = ((bf16[16,2,3,32,256]{4,3,2,1,0:T(8,128)(2,1)}), bf16[16,2,3,32,256]{4,3,2,1,0:T(8,128)(2,1)S(1)}, u32[]{:S(2)}, u32[]{:S(2)}) async-start(bf16[16,2,3,32,256]{4,3,2,1,0:T(8,128)(2,1)} %pick.1), calls=%async_computation.1 | async-start | bytes 3145728 | tf_op jit(solution)/shard_map/all_to_all | solution.py:335
  26.3 0.1 pad_add_fusion.position_ref.place_ref
  26.4 20.4 %all-to-all-done.1.listed_ref = bf16[16,2,3,32,256]{4,3,2,1,0:T(8,128)(2,1)S(1)} async-done(((bf16[16,2,3,32,256]{4,3,2,1,0:T(8,128)(2,1)}), bf16[16,2,3,32,256]{4,3,2,1,0:T(8,128)(2,1)S(1)}, u32[]{:S(2)}, u32[]{:S(2)}) %all-to-all-start.1) | async-done | bytes 1572896 | tf_op jit(solution)/shard_map/all_to_all | solution.py:335
  46.8 8.0 %far.1 = (bf16[16,2,2,3,32,128]{5,4,3,2,1,0:T(8,128)(2,1)}, bf16[2,128,512]{2,1,0:T(8,128)(2,1)S(1)}, f32[2,8,512]{2,1,0:T(8,128)S(1)}) custom-call(s32[96]{0:T(128)S(1)} %get-tuple-element.17.selection_ref, s32[3]{0:T(128)S(1)} %pad_add_fusion.position_ref.place_ref, bf16[512,256]{1,0:T(8,128)(2,1)S(1)} %copy-done.2, bf16[512,256]{1,0:T(8,128)(2,1)S(1)} %copy-done.3, ...), custom_call_target="tpu_custom_call" | custom-call | flops 2013265920 | bytes 4194304 | tf_op jit(solution)/shard_map/far/pallas_call | solution.py:391
  54.8 5.6 %all-to-all-start.2 = ((bf16[16,2,2,3,32,128]{5,4,3,2,1,0:T(8,128)(2,1)}), bf16[16,2,2,3,32,128]{5,4,3,2,1,0:T(8,128)(2,1)S(1)}, u32[]{:S(2)}, u32[]{:S(2)}) async-start(bf16[16,2,2,3,32,128]{5,4,3,2,1,0:T(8,128)(2,1)} %get-tuple-element.22), calls=%async_computation.2 | async-start | bytes 3145728 | tf_op jit(solution)/shard_map/all_to_all | solution.py:335
  60.4 2.4 %own_backward.1 = (bf16[16,2,32,256]{3,2,1,0:T(8,128)(2,1)S(1)}, bf16[64,256]{1,0:T(8,128)(2,1)S(1)}, bf16[64,256]{1,0:T(8,128)(2,1)S(1)}, bf16[64,256]{1,0:T(8,...) custom-call(s32[3]{0:T(128)S(1)} %pad_add_fusion.position_ref.place_, ...), custom_call_target="tpu_custom_call" | custom-call | flops 671088640 | bytes 4194304 | tf_op jit(solution)/shard_map/own_backward/pallas_call | solution.py:412
  62.8 7.0 %collective-permute-start = (bf16[64,256]{1,0:T(8,128)(2,1)S(1)}, bf16[64,256]{1,0:T(8,128)(2,1)S(1)}, u32[]{:S(2)}, u32[]{:S(2)}) collective-permute-start(bf16[64,256]{1,0:T(8,128)(2,1)S(1)} %get-tuple-element.23), channel_id=1, source_target_pairs={{0,8},{1,9},{2,10},{3,11},{4,12},{5,13},{6,14},{7,15},{8,0},{9,1},... | collective-permute-start | bytes 98312 | tf_op jit(solution)/shard_map/ppermute | solution.py:428
  69.8 1.6 %collective-permute-start.1 = (bf16[64,256]{1,0:T(8,128)(2,1)S(1)}, bf16[64,256]{1,0:T(8,128)(2,1)S(1)}, u32[]{:S(2)}, u32[]{:S(2)}) collective-permute-start(bf16[64,256]{1,0:T(8,128)(2,1)S(1)} %get-tuple-element.24), channel_id=1, source_target_pairs={{0,6},{1,7},{2,8},{3,9},{4,10},{5,11},{6,12},{7,13},{8,14},{9,15},... | collective-permute-start | bytes 98312 | tf_op jit(solution)/shard_map/ppermute | solution.py:428
  71.5 2.8 %collective-permute-start.2 = (bf16[64,256]{1,0:T(8,128)(2,1)S(1)}, bf16[64,256]{1,0:T(8,128)(2,1)S(1)}, u32[]{:S(2)}, u32[]{:S(2)}) collective-permute-start(bf16[64,256]{1,0:T(8,128)(2,1)S(1)} %get-tuple-element.25), channel_id=1, source_target_pairs={{0,10},{1,11},{2,12},{3,13},{4,14},{5,15},{6,0},{7,1},{8,2},{9,3},... | collective-permute-start | bytes 98312 | tf_op jit(solution)/shard_map/ppermute | solution.py:428
  74.3 1.2 collective-permute-start.3
  75.5 2.4 %collective-permute-start.4 = (bf16[64,256]{1,0:T(8,128)(2,1)S(1)}, bf16[64,256]{1,0:T(8,128)(2,1)S(1)}, u32[]{:S(2)}, u32[]{:S(2)}) collective-permute-start(bf16[64,256]{1,0:T(8,128)(2,1)S(1)} %get-tuple-element.27), channel_id=1, source_target_pairs={{0,12},{1,13},{2,14},{3,15},{4,0},{5,1},{6,2},{7,3},{8,4},{9,5},{1... | collective-permute-start | bytes 98312 | tf_op jit(solution)/shard_map/ppermute | solution.py:428
  77.9 0.0 collective-permute-done.refs_0_.refs_4_
  77.9 0.7 collective-permute-start.5
  78.6 0.0 collective-permute-done.1.refs_1_.refs_3_
  78.6 1.9 %collective-permute-start.6 = (bf16[64,256]{1,0:T(8,128)(2,1)S(1)}, bf16[64,256]{1,0:T(8,128)(2,1)S(1)}, u32[]{:S(2)}, u32[]{:S(2)}) collective-permute-start(bf16[64,256]{1,0:T(8,128)(2,1)S(1)} %get-tuple-element.29), channel_id=1, source_target_pairs={{0,14},{1,15},{2,0},{3,1},{4,2},{5,3},{6,4},{7,5},{8,6},{9,7},{10,... | collective-permute-start | bytes 98312 | tf_op jit(solution)/shard_map/ppermute | solution.py:428
  80.6 0.0 collective-permute-done.2.refs_2_.refs_5_
  80.6 0.0 collective-permute-done.3.refs_3_.refs_2_
  80.6 0.0 collective-permute-done.4.refs_4_.refs_6_
  80.6 1.4 %collective-permute-done.5.refs_5_.refs_1_ = bf16[64,256]{1,0:T(8,128)(2,1)S(1)} collective-permute-done((bf16[64,256]{1,0:T(8,128)(2,1)S(1)}, bf16[64,256]{1,0:T(8,128)(2,1)S(1)}, u32[]{:S(2)}, u32[]{:S(2)}) %collective-permute-start.5) | collective-permute-done | bytes 32800 | tf_op jit(solution)/shard_map/ppermute | solution.py:428
  82.0 0.0 collective-permute-done.6.refs_6_.refs_7_
  82.0 0.0 all-to-all-done.2.terms_ref
  82.0 1.7 %reduce.1 = bf16[16,2,32,256]{3,2,1,0:T(8,128)(2,1)} custom-call(s32[96]{0:T(128)S(1)} %get-tuple-element.17.selection_ref, bf16[16,2,2,3,32,128]{5,4,3,2,1,0:T(8,128)(2,1)S(1)} %all-to-all-done.2.terms_ref, bf16[64,256]{1,0:T(8,128)(2,1)S(1)} %collective-permute-done.refs_0_.refs_4_, bf16[64,256]{1,0:T(8,128)(2,1)S(1)} %collective-permute-done.1.refs_1_.refs_3_, ...), custom_call_target="tpu_custom_call" | custom-call | bytes 4194304 | tf_op jit(solution)/shard_map/reduce/pallas_call | solution.py:434
  83.7 6.5 %all-to-all-start.3 = ((bf16[16,2,32,256]{3,2,1,0:T(8,128)(2,1)}), bf16[16,2,32,256]{3,2,1,0:T(8,128)(2,1)S(1)}, u32[]{:S(2)}, u32[]{:S(2)}) async-start(bf16[16,2,32,256]{3,2,1,0:T(8,128)(2,1)} %reduce.1), calls=%async_computation.3 | async-start | bytes 1048576 | tf_op jit(solution)/shard_map/all_to_all | solution.py:335
  90.2 0.6 join.1
  90.8 5.2 %collective-permute-start.7 = (bf16[8,32,256]{2,1,0:T(8,128)(2,1)S(1)}, bf16[8,32,256]{2,1,0:T(8,128)(2,1)S(1)}, u32[]{:S(2)}, u32[]{:S(2)}) collective-permute-start(bf16[8,32,256]{2,1,0:T(8,128)(2,1)S(1)} %join.1), channel_id=1, source_target_pairs={{0,1},{1,0},{2,3},{3,2},{4,5},{5,4},{6,7},{7,6},{8,9},{9,8},{10,11... | collective-permute-start | bytes 393224 | tf_op jit(solution)/shard_map/ppermute | solution.py:451
  96.0 1.0 collective-permute-done.7.after_ref.other_ref
  96.9 2.3 %all-to-all-done.3.others_ref = bf16[16,2,32,256]{3,2,1,0:T(8,128)(2,1)S(1)} async-done(((bf16[16,2,32,256]{3,2,1,0:T(8,128)(2,1)}), bf16[16,2,32,256]{3,2,1,0:T(8,128)(2,1)S(1)}, u32[]{:S(2)}, u32[]{:S(2)}) %all-to-all-start.3) | async-done | bytes 524320 | tf_op jit(solution)/shard_map/all_to_all | solution.py:335
  99.2 0.1 finish.1
  99.3 27.9 %all_to_all.25.parts_ref = bf16[16,2,32,256]{3,2,1,0:T(8,128)(2,1)S(1)} all-to-all(bf16[16,2,32,256]{3,2,1,0:T(8,128)(2,1)S(1)} %finish.1), channel_id=1, replica_groups=mesh['chain'=16,'heads'=16] {'heads'}, dimensions={0} | all-to-all | bytes 1048576 | tf_op jit(solution)/shard_map/all_to_all | solution.py:335
  127.2 1.8 %lay.1 = (bf16[32,4096]{1,0:T(8,128)(2,1)}, bf16[32,4096]{1,0:T(8,128)(2,1)}, bf16[32,4096]{1,0:T(8,128)(2,1)}) custom-call(s32[3]{0:T(128)S(1)} %pad_add_fusion.position_ref.place_ref, bf16[16,2,32,256]{3,2,1,0:T(8,128)(2,1)S(1)} %all_to_all.25.parts_ref, bf16[8,32,256]{2,1,0:T(8,128)(2,1)S(1)} %collective-permute-done.7.after_ref.other_ref, ...), custom_call_target="tpu_custom_call" | custom-call | bytes 4194304 | tf_op jit(solution)/shard_map/lay/pallas_call | solution.py:467
Async XLA Ops:
  0.6 9.8 %copy-start = (bf16[512,256]{1,0:T(8,128)(2,1)S(1)}, bf16[512,256]{1,0:T(8,128)(2,1)}, u32[]{:S(2)}) copy-start(bf16[512,256]{1,0:T(8,128)(2,1)} %key_ref.3) | copy-start | bytes 786436
  0.6 9.8 %copy-start.1 = (bf16[512,256]{1,0:T(8,128)(2,1)S(1)}, bf16[512,256]{1,0:T(8,128)(2,1)}, u32[]{:S(2)}) copy-start(bf16[512,256]{1,0:T(8,128)(2,1)} %value_ref.3) | copy-start | bytes 786436
  0.7 9.6 %copy-start.4 = (s32[16,2,3]{0,1,2:T(2,128)S(1)}, s32[16,2,3]{0,1,2:T(2,128)}, u32[]{:S(2)}) copy-start(s32[16,2,3]{0,1,2:T(2,128)} %param.9) | copy-start | bytes 1156
  0.7 9.8 %copy-start.3 = (bf16[512,256]{1,0:T(8,128)(2,1)S(1)}, bf16[512,256]{1,0:T(8,128)(2,1)}, u32[]{:S(2)}) copy-start(bf16[512,256]{1,0:T(8,128)(2,1)} %grad_ref.5) | copy-start | bytes 786436
  0.7 9.8 %copy-start.2 = (bf16[512,256]{1,0:T(8,128)(2,1)S(1)}, bf16[512,256]{1,0:T(8,128)(2,1)}, u32[]{:S(2)}) copy-start(bf16[512,256]{1,0:T(8,128)(2,1)} %query_ref.5) | copy-start | bytes 786436
  2.6 18.1 %all-to-all-start = ((bf16[16,2,32,256]{3,2,1,0:T(8,128)(2,1)}), bf16[16,2,32,256]{3,2,1,0:T(8,128)(2,1)S(1)}, u32[]{:S(2)}, u32[]{:S(2)}) async-start(bf16[16,2,32,256]{3,2,1,0:T(8,128)(2,1)} %stack.17), calls=%async_computation | async-start | bytes 1048576 | tf_op jit(solution)/shard_map/all_to_all | solution.py:335
  22.6 24.3 %all-to-all-start.1 = ((bf16[16,2,3,32,256]{4,3,2,1,0:T(8,128)(2,1)}), bf16[16,2,3,32,256]{4,3,2,1,0:T(8,128)(2,1)S(1)}, u32[]{:S(2)}, u32[]{:S(2)}) async-start(bf16[16,2,3,32,256]{4,3,2,1,0:T(8,128)(2,1)} %pick.1), calls=%async_computation.1 | async-start | bytes 3145728 | tf_op jit(solution)/shard_map/all_to_all | solution.py:335
  54.8 27.2 %all-to-all-start.2 = ((bf16[16,2,2,3,32,128]{5,4,3,2,1,0:T(8,128)(2,1)}), bf16[16,2,2,3,32,128]{5,4,3,2,1,0:T(8,128)(2,1)S(1)}, u32[]{:S(2)}, u32[]{:S(2)}) async-start(bf16[16,2,2,3,32,128]{5,4,3,2,1,0:T(8,128)(2,1)} %get-tuple-element.22), calls=%async_computation.2 | async-start | bytes 3145728 | tf_op jit(solution)/shard_map/all_to_all | solution.py:335
  62.8 15.0 %collective-permute-start = (bf16[64,256]{1,0:T(8,128)(2,1)S(1)}, bf16[64,256]{1,0:T(8,128)(2,1)S(1)}, u32[]{:S(2)}, u32[]{:S(2)}) collective-permute-start(bf16[64,256]{1,0:T(8,128)(2,1)S(1)} %get-tuple-element.23), channel_id=1, source_target_pairs={{0,8},{1,9},{2,10},{3,11},{4,12},{5,13},{6,14},{7,15},{8,0},{9,1},... | collective-permute-start | bytes 98312 | tf_op jit(solution)/shard_map/ppermute | solution.py:428
  69.8 8.8 %collective-permute-start.1 = (bf16[64,256]{1,0:T(8,128)(2,1)S(1)}, bf16[64,256]{1,0:T(8,128)(2,1)S(1)}, u32[]{:S(2)}, u32[]{:S(2)}) collective-permute-start(bf16[64,256]{1,0:T(8,128)(2,1)S(1)} %get-tuple-element.24), channel_id=1, source_target_pairs={{0,6},{1,7},{2,8},{3,9},{4,10},{5,11},{6,12},{7,13},{8,14},{9,15},... | collective-permute-start | bytes 98312 | tf_op jit(solution)/shard_map/ppermute | solution.py:428
  71.5 9.1 %collective-permute-start.2 = (bf16[64,256]{1,0:T(8,128)(2,1)S(1)}, bf16[64,256]{1,0:T(8,128)(2,1)S(1)}, u32[]{:S(2)}, u32[]{:S(2)}) collective-permute-start(bf16[64,256]{1,0:T(8,128)(2,1)S(1)} %get-tuple-element.25), channel_id=1, source_target_pairs={{0,10},{1,11},{2,12},{3,13},{4,14},{5,15},{6,0},{7,1},{8,2},{9,3},... | collective-permute-start | bytes 98312 | tf_op jit(solution)/shard_map/ppermute | solution.py:428
  74.3 6.3 %collective-permute-start.3 = (bf16[64,256]{1,0:T(8,128)(2,1)S(1)}, bf16[64,256]{1,0:T(8,128)(2,1)S(1)}, u32[]{:S(2)}, u32[]{:S(2)}) collective-permute-start(bf16[64,256]{1,0:T(8,128)(2,1)S(1)} %get-tuple-element.26), channel_id=1, source_target_pairs={{0,4},{1,5},{2,6},{3,7},{4,8},{5,9},{6,10},{7,11},{8,12},{9,13},{1... | collective-permute-start | bytes 98312 | tf_op jit(solution)/shard_map/ppermute | solution.py:428
  75.5 5.1 %collective-permute-start.4 = (bf16[64,256]{1,0:T(8,128)(2,1)S(1)}, bf16[64,256]{1,0:T(8,128)(2,1)S(1)}, u32[]{:S(2)}, u32[]{:S(2)}) collective-permute-start(bf16[64,256]{1,0:T(8,128)(2,1)S(1)} %get-tuple-element.27), channel_id=1, source_target_pairs={{0,12},{1,13},{2,14},{3,15},{4,0},{5,1},{6,2},{7,3},{8,4},{9,5},{1... | collective-permute-start | bytes 98312 | tf_op jit(solution)/shard_map/ppermute | solution.py:428
  77.9 4.1 %collective-permute-start.5 = (bf16[64,256]{1,0:T(8,128)(2,1)S(1)}, bf16[64,256]{1,0:T(8,128)(2,1)S(1)}, u32[]{:S(2)}, u32[]{:S(2)}) collective-permute-start(bf16[64,256]{1,0:T(8,128)(2,1)S(1)} %get-tuple-element.28), channel_id=1, source_target_pairs={{0,2},{1,3},{2,4},{3,5},{4,6},{5,7},{6,8},{7,9},{8,10},{9,11},{10,... | collective-permute-start | bytes 98312 | tf_op jit(solution)/shard_map/ppermute | solution.py:428
  78.6 3.4 %collective-permute-start.6 = (bf16[64,256]{1,0:T(8,128)(2,1)S(1)}, bf16[64,256]{1,0:T(8,128)(2,1)S(1)}, u32[]{:S(2)}, u32[]{:S(2)}) collective-permute-start(bf16[64,256]{1,0:T(8,128)(2,1)S(1)} %get-tuple-element.29), channel_id=1, source_target_pairs={{0,14},{1,15},{2,0},{3,1},{4,2},{5,3},{6,4},{7,5},{8,6},{9,7},{10,... | collective-permute-start | bytes 98312 | tf_op jit(solution)/shard_map/ppermute | solution.py:428
  83.7 15.5 %all-to-all-start.3 = ((bf16[16,2,32,256]{3,2,1,0:T(8,128)(2,1)}), bf16[16,2,32,256]{3,2,1,0:T(8,128)(2,1)S(1)}, u32[]{:S(2)}, u32[]{:S(2)}) async-start(bf16[16,2,32,256]{3,2,1,0:T(8,128)(2,1)} %reduce.1), calls=%async_computation.3 | async-start | bytes 1048576 | tf_op jit(solution)/shard_map/all_to_all | solution.py:335
  90.8 6.2 %collective-permute-start.7 = (bf16[8,32,256]{2,1,0:T(8,128)(2,1)S(1)}, bf16[8,32,256]{2,1,0:T(8,128)(2,1)S(1)}, u32[]{:S(2)}, u32[]{:S(2)}) collective-permute-start(bf16[8,32,256]{2,1,0:T(8,128)(2,1)S(1)} %join.1), channel_id=1, source_target_pairs={{0,1},{1,0},{2,3},{3,2},{4,5},{5,4},{6,7},{7,6},{8,9},{9,8},{10,11... | collective-permute-start | bytes 393224 | tf_op jit(solution)/shard_map/ppermute | solution.py:451
